TPU v7x, 256 devices: a whole 4x4x8 slice. The times are simulated.
256 devices in a mesh: orb: 64 (over z, x, core), pair: 4 (over y).
Axes of the slice: x: 4, y: 4, z: 8, core: 2. Of those that a mesh axis runs over, the one named last changes fastest.
Arguments:
- integrals: bfloat16 [2048, 1024, 256], P(('orb', 'pair')), may hold values from -2 to 2
- fock_blocks: bfloat16 [1024, 256, 256], P(('orb', 'pair')), as said below
- occ_energy: float32 [1024], P('orb'), may hold values from -2 to -0.3
- dom_len: int32 [1024], P('orb'), may hold values from 85 to 256, as said below
- amplitudes: bfloat16 [4096, 256, 256], P(('orb', 'pair')), may hold values from -1.796875 to 1.796875
- pair_list: int32 [4096, 2], P('orb'), may hold values from 0 to 15, as said below
Outputs:
- residual: bfloat16 [4096, 256, 256], P(('orb', 'pair'))
- new_amplitudes: bfloat16 [4096, 256, 256], P(('orb', 'pair'))
Inputs may be any that keep to these rules, and one draw needn't show every extreme that they name: `pair_list`: rows g * 64 to g * 64 + 63 hold the pairs of group g; each row names two orbital numbers with the first not above the second, and no row repeats within a group. `dom_len`: the largest length is 256 in every draw. `fock_blocks`: diagonal entries lie between 1 and 3.
All inputs are finite; a program needn't handle non-finite values.
Results may differ from a plain program's by a relative error of at most 0.001.
Values may be sent and summed in bfloat16 or wider, within the bound.
No kernel may reach another device: no remote copies, remote signals or barrier semaphores. Data moves between devices by JAX's collectives and lax.ppermute only.
A program may use at most 192 MiB of HBM per device.

v0:
```python
import jax
import jax.numpy as jnp
from jax import lax
from jax.sharding import PartitionSpec as P


def contract(block, rows):
    left = jnp.take(block, rows[:, 0], axis=1)
    right = jnp.take(block, rows[:, 1], axis=1)
    return jnp.einsum("qpa,qpb->pab", left, right, preferred_element_type=jnp.float32)


def pick_values(table, rows):
    numbers = jnp.arange(table.shape[0], dtype=jnp.int32)
    chosen = rows[:, None] == numbers[None, :]
    return jnp.sum(jnp.where(chosen, table[None, :], jnp.zeros_like(table)[None, :]), axis=1)


def local(integrals, fock_blocks, occ_energy, dom_len, amplitudes, pair_list):
    exchanged = lax.all_to_all(integrals, "orb", split_axis=1, concat_axis=0, tiled=True)
    group_fock = lax.all_gather(fock_blocks, "pair", axis=0, tiled=True)
    owned = amplitudes.shape[0]
    width = amplitudes.shape[1]
    begin = lax.axis_index("pair") * owned
    mine = lax.dynamic_slice_in_dim(pair_list, begin, owned, 0)
    exchange = contract(lax.all_gather(exchanged, "pair", axis=0, tiled=True), mine)
    first = mine[:, 0]
    second = mine[:, 1]
    fock_first = jnp.take(group_fock, first, axis=0)
    fock_second = jnp.take(group_fock, second, axis=0)
    left_term = jnp.einsum(
        "pac,pcb->pab", fock_first, amplitudes, preferred_element_type=jnp.float32
    )
    right_term = jnp.einsum(
        "pac,pbc->pab", amplitudes, fock_second, preferred_element_type=jnp.float32
    )
    energies = pick_values(occ_energy, first) + pick_values(occ_energy, second)
    positions = jnp.arange(width, dtype=jnp.int32)
    inside_first = positions[None, :] < pick_values(dom_len, first)[:, None]
    inside_second = positions[None, :] < pick_values(dom_len, second)[:, None]
    mask = (inside_first[:, :, None] & inside_second[:, None, :]).astype(jnp.float32)
    old = amplitudes.astype(jnp.float32)
    resid = mask * (exchange + left_term + right_term - energies[:, None, None] * old)
    diag_first = jnp.diagonal(fock_first, axis1=1, axis2=2).astype(jnp.float32)
    diag_second = jnp.diagonal(fock_second, axis1=1, axis2=2).astype(jnp.float32)
    denominator = diag_first[:, :, None] + diag_second[:, None, :] - energies[:, None, None]
    updated = mask * (old - resid / denominator)
    return (resid.astype(jnp.bfloat16), updated.astype(jnp.bfloat16))


def solution(mesh):
    placed = (
        P(("orb", "pair"), None, None),
        P(("orb", "pair"), None, None),
        P("orb"),
        P("orb"),
        P(("orb", "pair"), None, None),
        P("orb", None),
    )
    return jax.shard_map(
        local,
        mesh=mesh,
        in_specs=placed,
        out_specs=(P(("orb", "pair"), None, None), P(("orb", "pair"), None, None)),
        check_vma=False,
    )
```

profile of v0, /device:TPU:2, one launch (start us, length us, event | category | flops | bytes accessed | tf_op | source)
XLA Modules:
  0.0 343.4 jit_solution(14764295135750016750)
XLA Ops:
  7.2 0.0 copy-start
  7.2 6.5 %copy.38 = bf16[8,1024,256]{2,0,1:T(8,128)(2,1)} copy(bf16[8,1024,256]{2,1,0:T(8,128)(2,1)} %param.10) | data formatting | bytes 8388608 | tf_op args[0]
  13.7 12.2 %all-to-all-start = ((bf16[8,1024,256]{2,0,1:T(8,128)(2,1)}), bf16[8,1024,256]{2,0,1:T(8,128)(2,1)}, u32[]{:S(2)}, u32[]{:S(2)}) async-start(bf16[8,1024,256]{2,0,1:T(8,128)(2,1)} %copy.38), calls=%async_computation | async-start | bytes 8388608 | tf_op jit(solution)/shard_map/all_to_all | solution.py:20
  25.9 0.0 all-gather.5.cloned.1.call-start
  26.0 0.7 all-gather.5.cloned.1.call-update
  26.7 0.2 all-gather.3.cloned.1.call-start
  26.9 95.2 %all-to-all-done = bf16[8,1024,256]{2,0,1:T(8,128)(2,1)} async-done(((bf16[8,1024,256]{2,0,1:T(8,128)(2,1)}), bf16[8,1024,256]{2,0,1:T(8,128)(2,1)}, u32[]{:S(2)}, u32[]{:S(2)}) %all-to-all-start) | async-done | bytes 4194336 | tf_op jit(solution)/shard_map/all_to_all | solution.py:20
  122.0 5.6 %copy.40 = bf16[64,8,16,256]{3,2,1,0:T(8,128)(2,1)} copy(bf16[64,8,16,256]{3,1,2,0:T(8,128)(2,1)} %bitcast.4) | data formatting | bytes 8388608 | tf_op jit(solution)/shard_map/all_to_all | solution.py:20
  127.6 7.6 %copy.41 = bf16[512,16,256]{0,2,1:T(8,128)(2,1)} copy(bf16[512,16,256]{2,1,0:T(8,128)(2,1)} %bitcast.43) | data formatting | bytes 8388608 | tf_op jit(solution)/shard_map/all_to_all | solution.py:20
  135.2 0.0 copy-start.5
  135.2 0.0 copy-start.6
  135.2 0.0 all-gather.3.cloned.1.call-update
  135.3 0.0 copy-done
  135.3 0.1 constant_dynamic-slice_fusion
  135.3 0.5 copy-done.5
  135.9 0.2 select_reduce_fusion
  136.1 0.0 copy-done.6
  136.1 0.2 select_reduce_fusion.3
  136.3 0.1 iota_compare_fusion
  136.4 0.0 all-gather.5.cloned.1.call-done
  136.4 0.0 copy-start.2
  136.4 3.7 %gather_fusion.5 = bf16[16,256,256]{2,1,0:T(8,128)(2,1)} fusion(bf16[16,256,256]{2,1,0:T(8,128)(2,1)} %all-gather.5.cloned.1.call-done, s32[1024]{0:T(1024)S(1)} %pad_clamp_fusion), kind=kCustom, calls=%fused_computation.3.clone | custom fusion | bytes 4194368 | tf_op jit(solution)/shard_map/jit(_take)/gather | solution.py:30
  140.1 0.0 copy-done.2
  140.2 2.0 gather_fusion.4
  142.1 4.6 %broadcast_select_fusion = (bf16[16,256,256]{2,1,0:T(8,128)(2,1)}, bf16[16,256,256]{2,1,0:T(8,128)(2,1)S(1)}) fusion(bf16[16,256,256]{2,1,0:T(8,128)(2,1)} %gather_fusion.5, pred[16]{0:T(512)(128)(4,1)S(1)} %get-tuple-element.16, bf16[16,256,256]{2,1,0:T(8,128)(2,1)} %gather_fusion.4, pred[16]{0:T(512)(128)(4,1)S(1)} %get-tuple-element.8), kind=kLoop, calls=%fused_computation.21 | loop fusion | flops 2097152 | bytes 8388640 | tf_op jit(solution)/shard_map/jit(_take)/select_n | solution.py:30
  146.8 11.5 %copy.44 = bf16[16,256,256]{0,2,1:T(8,128)(2,1)} copy(bf16[16,256,256]{2,1,0:T(8,128)(2,1)S(1)} %get-tuple-element.20) | data formatting | bytes 4194304 | tf_op jit(solution)/shard_map/jit(_take)/select_n | solution.py:29
  158.2 2.7 gather_fusion
  160.9 0.1 copy.45
  161.0 13.2 %copy.46 = bf16[16,256,256]{0,2,1:T(8,128)(2,1)} copy(bf16[16,256,256]{2,1,0:T(8,128)(2,1)} %get-tuple-element.19) | data formatting | bytes 4194304 | tf_op jit(solution)/shard_map/jit(_take)/select_n | solution.py:30
  174.2 2.7 gather_fusion.1
  176.9 0.1 copy.47
  177.0 0.0 copy-start.3
  177.0 5.3 %fusion.16 = f32[16,256,256]{1,2,0:T(8,128)} fusion(bf16[16,256,256]{2,1,0:T(8,128)(2,1)} %get-tuple-element.19, bf16[16,256,256]{2,1,0:T(8,128)(2,1)} %param.14), kind=kOutput, calls=%fused_computation.45 | convolution fusion | flops 536870912 | bytes 8388608 | tf_op jit(solution)/shard_map/pac,pbc->pab/dot_general | solution.py:34
  182.2 0.0 copy-done.3
  182.2 2.7 fusion.15
  184.9 103.5 %all-gather.3.cloned.1.call-done = bf16[2048,16,256]{0,2,1:T(8,128)(2,1)} async-done(((bf16[512,16,256]{0,2,1:T(8,128)(2,1)}), bf16[2048,16,256]{0,2,1:T(8,128)(2,1)}) %all-gather.3.cloned.1.call-update) | async-done | bytes 16777232 | tf_op jit(solution)/shard_map/all_gather | solution.py:26
  288.4 13.0 %gather_fusion.3 = bf16[16,2048,256]{1,2,0:T(8,128)(2,1)} fusion(bf16[2048,16,256]{0,2,1:T(8,128)(2,1)} %all-gather.3.cloned.1.call-done, s32[1024]{0:T(1024)S(1)} %pad_clamp_fusion), kind=kCustom, calls=%fused_computation.2.clone | custom fusion | bytes 33554496 | tf_op jit(solution)/shard_map/jit(_take)/gather | solution.py:9
  301.4 0.0 copy-start.4
  301.4 13.2 %gather_fusion.2 = bf16[16,2048,256]{1,2,0:T(8,128)(2,1)} fusion(bf16[2048,16,256]{0,2,1:T(8,128)(2,1)} %all-gather.3.cloned.1.call-done, s32[1024]{0:T(1024)S(1)} %pad_clamp_fusion.1), kind=kCustom, calls=%fused_computation.clone | custom fusion | bytes 33554496 | tf_op jit(solution)/shard_map/jit(_take)/gather | solution.py:8
  314.6 0.0 copy-done.4
  314.6 0.0 copy-start.1
  314.6 21.9 %fusion.9 = (bf16[16,256,256]{2,1,0:T(8,128)(2,1)}, bf16[16,256,256]{2,1,0:T(8,128)(2,1)}) fusion(bf16[16,256,256]{2,1,0:T(8,128)(2,1)S(1)} %copy-done.4, f32[16,256]{1,0:T(8,128)S(1)} %copy.47, f32[16,256]{1,0:T(8,128)S(1)} %copy.45, f32[16]{0:T(128)S(1)} %add.44, pred[16,256]{1,0:T(8,128)(4,1)S(1)} %get-tuple-element.21, ...), kind=kOutput, calls=%fused_computation.19 | convolution fusion | flops 4326424576 | bytes 48275552 | tf_op jit(solution)/shard_map/qpa,qpb->pab/dot_general | solution.py:10
  336.5 0.0 copy-done.1
  (8 shorter events, 0.1 us)
Async XLA Ops:
  7.2 128.1 %copy-start = (s32[64,2]{0,1:T(2,128)S(1)}, s32[64,2]{0,1:T(2,128)}, u32[]{:S(2)}) copy-start(s32[64,2]{0,1:T(2,128)} %param.15) | copy-start | bytes 1540
  13.7 108.3 %all-to-all-start = ((bf16[8,1024,256]{2,0,1:T(8,128)(2,1)}), bf16[8,1024,256]{2,0,1:T(8,128)(2,1)}, u32[]{:S(2)}, u32[]{:S(2)}) async-start(bf16[8,1024,256]{2,0,1:T(8,128)(2,1)} %copy.38), calls=%async_computation | async-start | bytes 8388608 | tf_op jit(solution)/shard_map/all_to_all | solution.py:20
  25.9 110.5 %all-gather.5.cloned.1.call-start = ((), (), s32[]{:S(2)}) async-start(), calls=%async_computation.2 | async-start | bytes 2621440 | tf_op jit(solution)/shard_map/all_gather | solution.py:21
  26.7 261.7 %all-gather.3.cloned.1.call-start = ((), (), s32[]{:S(2)}) async-start(), calls=%async_computation.1 | async-start | bytes 20971520 | tf_op jit(solution)/shard_map/all_gather | solution.py:26
  135.2 0.7 copy-start.5
  135.2 0.9 copy-start.6
  136.4 3.8 %copy-start.2 = (bf16[16,256,256]{2,1,0:T(8,128)(2,1)S(1)}, bf16[16,256,256]{2,1,0:T(8,128)(2,1)}, u32[]{:S(2)}) copy-start(bf16[16,256,256]{2,1,0:T(8,128)(2,1)} %all-gather.5.cloned.1.call-done) | copy-start | bytes 6291460
  177.0 5.3 %copy-start.3 = (bf16[16,256,256]{2,1,0:T(8,128)(2,1)S(1)}, bf16[16,256,256]{2,1,0:T(8,128)(2,1)}, u32[]{:S(2)}) copy-start(bf16[16,256,256]{2,1,0:T(8,128)(2,1)} %param.14) | copy-start | bytes 6291460
  301.4 13.2 %copy-start.4 = (bf16[16,256,256]{2,1,0:T(8,128)(2,1)S(1)}, bf16[16,256,256]{2,1,0:T(8,128)(2,1)}, u32[]{:S(2)}) copy-start(bf16[16,256,256]{2,1,0:T(8,128)(2,1)} %param.14) | copy-start | bytes 6291460
  314.6 21.9 %copy-start.1 = (s32[64,2]{0,1:T(2,128)S(1)}, s32[64,2]{0,1:T(2,128)}, u32[]{:S(2)}) copy-start(s32[64,2]{0,1:T(2,128)} %param.15) | copy-start | bytes 1540
Sparse Core Ops, SparseCore 0:
  28.6 34.6 all-gather.4
  135.4 152.9 all-gather.2
where the time goes:
time: 345 us; the launch traced here: 343 us
  waiting for transfers between devices  199 us (58%)
  local copies, waits for them, and re-layouts  82.5 us (24%)
  matrix products  29.9 us (9%)
  between operations  14.1 us (4%)
  starting transfers between devices  12.5 us (4%)
  other arithmetic  5.13 us (1%)
    all_gather x1, waiting for transfers between devices, local(): lax.all_gather(exchanged, 'pair', axis=0, tiled=True)  103 us
    all_to_all x1, waiting for transfers between devices, local(): lax.all_to_all(integrals, 'orb', split_axis=1, concat_axis=0, tiled=True)  95.2 us
    dot_general x1, matrix products, contract(): jnp.einsum('qpa,qpb->pab', left, right, preferred_element_type=jnp.float32)  21.9 us
    select_n x1, local copies, waits for them, and re-layouts, local(): fock_second = jnp.take(group_fock, second, axis=0)  13.2 us
    gather x1, local copies, waits for them, and re-layouts, contract(): left = jnp.take(block, rows[:, 0], axis=1)  13.2 us
    all_to_all x2, local copies, waits for them, and re-layouts, local(): lax.all_to_all(integrals, 'orb', split_axis=1, concat_axis=0, tiled=True)  13.2 us
    gather x1, local copies, waits for them, and re-layouts, contract(): right = jnp.take(block, rows[:, 1], axis=1)  13 us
    all_to_all x1, starting transfers between devices, local(): lax.all_to_all(integrals, 'orb', split_axis=1, concat_axis=0, tiled=True)  12.2 us
  transfers between devices with their start and end apart: 3, of which 2 were waited for; matrix products, arithmetic and copies ran while one was open for 18% of the time, Pallas kernels for 0%

commit v1 on v0

v1 whole, which is shorter than its diff:
```python
import functools

import jax
import jax.numpy as jnp
from jax import lax
from jax.experimental import pallas as pl
from jax.experimental.pallas import tpu as pltpu
from jax.sharding import PartitionSpec as P

BOTH = ("orb", "pair")
SPLITS = ((0, 12), (12, 16))
VMEM = 24 * 2**20


def gather_mate(orb, y):
    return y ^ 1 if orb % 2 == 0 else 3 - y


def sum_mate(orb, y):
    return 3 - y if orb % 2 == 0 else y ^ 1


def exchange_with(x, mate, orbs, ys):
    pairs = [(o * ys + y, o * ys + mate(o, y)) for o in range(orbs) for y in range(ys)]
    return lax.ppermute(x, BOTH, pairs)


def load_blocks(parts, held, sems):
    copies = []
    for half in range(2):
        for c, (lo, hi) in enumerate(SPLITS):
            k = half * len(SPLITS) + c
            copies.append(
                pltpu.make_async_copy(parts[k], held.at[half, :, lo:hi], sems.at[k])
            )
    return copies


def half_sum(held, i, j):
    total = None
    for half in range(2):
        left = held[half, :, i].reshape(-1, held.shape[-1])
        right = held[half, :, j].reshape(-1, held.shape[-1])
        term = lax.dot_general(
            left, right, (((0,), (0,)), ((), ())), preferred_element_type=jnp.float32
        )
        total = term if total is None else total + term
    return total


def partial_kernel(first, pairs_ref, begin_ref, *refs):
    parts, out_refs, held, sems = refs[:4], refs[4:-2], refs[-2], refs[-1]
    p = pl.program_id(0)

    @pl.when(p == 0)
    def _():
        copies = load_blocks(parts, held, sems)
        for c in copies:
            c.start()
        for c in copies:
            c.wait()

    row = begin_ref[0] + first + p
    out_refs[0][0] = half_sum(held, pairs_ref[2 * row], pairs_ref[2 * row + 1])


def partial_sums(parts, pairs, begin, first, count):
    _, _, aux, dom = parts[0].shape
    orbs = SPLITS[-1][1]
    src = parts[0].shape[0]
    return pl.pallas_call(
        functools.partial(partial_kernel, first),
        grid_spec=pltpu.PrefetchScalarGridSpec(
            num_scalar_prefetch=2,
            grid=(count,),
            in_specs=[pl.BlockSpec(memory_space=pl.ANY)] * 4,
            out_specs=[pl.BlockSpec((1, dom, dom), lambda p, *_: (p, 0, 0))],
            scratch_shapes=[
                pltpu.VMEM((2, src, orbs, aux, dom), jnp.bfloat16),
                pltpu.SemaphoreType.DMA((4,)),
            ],
        ),
        out_shape=[jax.ShapeDtypeStruct((count, dom, dom), jnp.float32)],
        compiler_params=pltpu.CompilerParams(vmem_limit_bytes=VMEM),
        cost_estimate=pl.CostEstimate(
            flops=2 * count * 2 * src * aux * dom * dom * 4,
            bytes_accessed=4 * src * orbs * aux * dom + count * dom * dom * 4,
            transcendentals=0,
        ),
    )(pairs, begin, *parts)[0]


def own_kernel(pairs_ref, begin_ref, *refs):
    parts, base_ref, out_ref, held, sems = refs[:4], refs[4], refs[5], refs[6], refs[7]
    p = pl.program_id(0)

    @pl.when(p == 0)
    def _():
        copies = load_blocks(parts, held, sems)
        for c in copies:
            c.start()
        for c in copies:
            c.wait()

    row = begin_ref[0] + p
    out_ref[0] = base_ref[0] + half_sum(held, pairs_ref[2 * row], pairs_ref[2 * row + 1])


def own_sums(parts, base, pairs, begin):
    src, _, aux, dom = parts[0].shape
    orbs = SPLITS[-1][1]
    count = base.shape[0]
    one = pl.BlockSpec((1, dom, dom), lambda p, *_: (p, 0, 0))
    return pl.pallas_call(
        own_kernel,
        grid_spec=pltpu.PrefetchScalarGridSpec(
            num_scalar_prefetch=2,
            grid=(count,),
            in_specs=[pl.BlockSpec(memory_space=pl.ANY)] * 4 + [one],
            out_specs=[one],
            scratch_shapes=[
                pltpu.VMEM((2, src, orbs, aux, dom), jnp.bfloat16),
                pltpu.SemaphoreType.DMA((4,)),
            ],
        ),
        out_shape=[jax.ShapeDtypeStruct((count, dom, dom), jnp.float32)],
        input_output_aliases={6: 0},
        compiler_params=pltpu.CompilerParams(vmem_limit_bytes=VMEM),
        cost_estimate=pl.CostEstimate(
            flops=2 * count * 2 * src * aux * dom * dom * 4,
            bytes_accessed=4 * src * orbs * aux * dom + count * dom * dom * 8,
            transcendentals=0,
        ),
    )(pairs, begin, *parts, base)[0]


def fock_kernel(pairs_ref, begin_ref, slot_ref, occ_ref, len_ref, *refs):
    focks, amp_ref, base_ref, inv_ref, fock, sems = refs[:4], refs[4], *refs[5:]
    p = pl.program_id(0)
    dom = fock.shape[-1]

    @pl.when(p == 0)
    def _():
        each = focks[0].shape[0]
        copies = [
            pltpu.make_async_copy(
                focks[s], fock.at[s * each : (s + 1) * each], sems.at[s]
            )
            for s in range(4)
        ]
        for c in copies:
            c.start()
        for c in copies:
            c.wait()

    row = begin_ref[0] + p
    i = pairs_ref[2 * row]
    j = pairs_ref[2 * row + 1]
    energies = occ_ref[i] + occ_ref[j]
    old = amp_ref[0]
    fock_i = fock[slot_ref[i]]
    fock_j = fock[slot_ref[j]]
    total = jnp.dot(fock_i, old, preferred_element_type=jnp.float32)
    total += lax.dot_general(
        old, fock_j, (((1,), (1,)), ((), ())), preferred_element_type=jnp.float32
    )
    base_ref[0] = total - energies * old.astype(jnp.float32)
    rows = lax.broadcasted_iota(jnp.int32, (dom, dom), 0)
    columns = lax.broadcasted_iota(jnp.int32, (dom, dom), 1)
    eye = rows == columns
    diag_i = jnp.sum(
        jnp.where(eye, fock_i.astype(jnp.float32), 0.0), axis=1, keepdims=True
    )
    diag_j = jnp.sum(
        jnp.where(eye, fock_j.astype(jnp.float32), 0.0), axis=0, keepdims=True
    )
    inside = (rows < len_ref[i]) & (columns < len_ref[j])
    inv_ref[0] = jnp.where(inside, 1.0 / (diag_i + diag_j - energies), 0.0)


def fock_terms(focks, amplitudes, pairs, begin, slot, occ, lengths):
    count, dom, _ = amplitudes.shape
    one = pl.BlockSpec((1, dom, dom), lambda p, *_: (p, 0, 0))
    shape = jax.ShapeDtypeStruct((count, dom, dom), jnp.float32)
    return pl.pallas_call(
        fock_kernel,
        grid_spec=pltpu.PrefetchScalarGridSpec(
            num_scalar_prefetch=5,
            grid=(count,),
            in_specs=[pl.BlockSpec(memory_space=pl.ANY)] * 4 + [one],
            out_specs=[one, one],
            scratch_shapes=[
                pltpu.VMEM((4 * focks[0].shape[0], dom, dom), jnp.bfloat16),
                pltpu.SemaphoreType.DMA((4,)),
            ],
        ),
        out_shape=[shape, shape],
        compiler_params=pltpu.CompilerParams(vmem_limit_bytes=VMEM),
        cost_estimate=pl.CostEstimate(
            flops=2 * count * 2 * dom * dom * dom,
            bytes_accessed=count * dom * dom * 12,
            transcendentals=0,
        ),
    )(pairs, begin, slot, occ, lengths, *focks, amplitudes)


def finish_kernel(own_ref, other_ref, amp_ref, inv_ref, *refs):
    resid_ref, new_ref = refs[-2:]
    inv = inv_ref[0]
    inside = inv != 0.0
    resid = jnp.where(inside, own_ref[0] + other_ref[0], 0.0)
    old = amp_ref[0].astype(jnp.float32)
    resid_ref[0] = resid.astype(resid_ref.dtype)
    new_ref[0] = jnp.where(inside, old - resid * inv, 0.0).astype(new_ref.dtype)


def finish(own, other, amplitudes, inv, first, held):
    total, dom, _ = amplitudes.shape
    count = other.shape[0]
    shifted = pl.BlockSpec((1, dom, dom), lambda p: (p + first, 0, 0))
    shape = jax.ShapeDtypeStruct((total, dom, dom), jnp.bfloat16)
    extra = [] if held is None else list(held)
    return pl.pallas_call(
        finish_kernel,
        grid=(count,),
        in_specs=[
            shifted,
            pl.BlockSpec((1, dom, dom), lambda p: (p, 0, 0)),
            shifted,
            shifted,
        ]
        + [pl.BlockSpec(memory_space=pl.ANY)] * len(extra),
        out_specs=[shifted, shifted],
        out_shape=[shape, shape],
        input_output_aliases={4: 0, 5: 1} if extra else {},
        compiler_params=pltpu.CompilerParams(vmem_limit_bytes=VMEM),
        cost_estimate=pl.CostEstimate(
            flops=count * dom * dom * 5,
            bytes_accessed=count * dom * dom * 18,
            transcendentals=0,
        ),
    )(own, other, amplitudes, inv, *extra)


CHUNKS = ((0, 4), (4, 12), (12, 16))


def local(orbs, ys, integrals, fock_blocks, occ_energy, dom_len, amplitudes, pair_list):
    aux, occ, dom = integrals.shape
    group = occ // orbs
    owned = amplitudes.shape[0]
    y = lax.axis_index("pair")
    even = lax.rem(lax.axis_index("orb"), 2) == 0
    mate = jnp.where(even, 3 - y, y ^ 1)
    pairs = pair_list.reshape(-1)
    mine = (y * owned).reshape(1).astype(jnp.int32)
    theirs = (mate * owned).reshape(1).astype(jnp.int32)
    each = fock_blocks.shape[0]
    number = jnp.arange(group, dtype=jnp.int32)
    slot = ((number // each - y) & 3) * each + number % each
    focks = [fock_blocks] + [
        lax.ppermute(fock_blocks, "pair", [((s + shift) % ys, s) for s in range(ys)])
        for shift in (1, 2, 3)
    ]

    blocks = integrals.reshape(aux, orbs, group, dom).transpose(1, 2, 0, 3)
    near, far = [], []
    for c, (lo, hi) in enumerate(SPLITS):
        block = blocks[:, lo:hi]
        if c == len(SPLITS) - 1:
            block, *focks = lax.optimization_barrier([block] + focks)
        got = lax.all_to_all(block, "orb", split_axis=0, concat_axis=0, tiled=True)
        near.append(got)
        far.append(exchange_with(got, gather_mate, orbs, ys))
    parts = near + far

    others = []
    for lo, hi in CHUNKS:
        sums = partial_sums(parts, pairs, theirs, lo, hi - lo)
        others.append(exchange_with(sums, sum_mate, orbs, ys))
    base, inv = fock_terms(focks, amplitudes, pairs, mine, slot, occ_energy, dom_len)
    own = own_sums(parts, base, pairs, mine)
    held = None
    for (lo, _), other in zip(CHUNKS, others):
        held = finish(own, other, amplitudes, inv, lo, held)
    return tuple(held)


def solution(mesh):
    placed = (
        P(("orb", "pair"), None, None),
        P(("orb", "pair"), None, None),
        P("orb"),
        P("orb"),
        P(("orb", "pair"), None, None),
        P("orb", None),
    )
    return jax.shard_map(
        functools.partial(local, mesh.shape["orb"], mesh.shape["pair"]),
        mesh=mesh,
        in_specs=placed,
        out_specs=(P(("orb", "pair"), None, None), P(("orb", "pair"), None, None)),
        check_vma=False,
    )
```

time: 345 us -> 210 us (0.61)
  waiting for transfers between devices: 199 us -> 86.9 us
  local copies, waits for them, and re-layouts: 82.5 us -> 12.9 us
  Pallas kernels: 0 us -> 50.4 us
  blocking collectives: 0 us -> 34.9 us
  matrix products: 29.9 us -> 0 us
  between operations: 14.1 us -> 0.79 us
  starting transfers between devices: 12.5 us -> 24 us
  other arithmetic: 5.13 us -> 0.01 us
    all_gather x2 -> x0, waiting for transfers between devices: 103 us -> none  [the longest x1 103 us: local(): lax.all_gather(exchanged, 'pair', axis=0, tiled=True)]
    pallas_call x0 -> x8, Pallas kernels: none -> 50.4 us  [the longest x3 20.3 us: partial_sums(): pl.pallas_call(functools.partial(partial_kernel, first), grid_spec=pltpu....]
    gather x6 -> x0, local copies, waits for them, and re-layouts: 37.3 us -> none  [the longest x1 13.2 us: contract(): left = jnp.take(block, rows[:, 0], axis=1)]
    all_to_all x0 -> x1, blocking collectives: none -> 34.9 us  [local(): got = lax.all_to_all(block, 'orb', split_axis=0, concat_axis=0, tiled=True)]
    dot_general x3 -> x0, matrix products: 29.9 us -> none  [the longest x1 21.9 us: contract(): jnp.einsum('qpa,qpb->pab', left, right, preferred_element_type=jnp.float32)]
    all_to_all x1, waiting for transfers between devices: 95.2 us -> 69 us  [local(): got = lax.all_to_all(block, 'orb', split_axis=0, concat_axis=0, tiled=True)]
    select_n x2 -> x0, local copies, waits for them, and re-layouts: 24.7 us -> none  [the longest x1 13.2 us: local(): fock_second = jnp.take(group_fock, second, axis=0)]
    ppermute x0 -> x8, waiting for transfers between devices: none -> 17.9 us  [the longest x5 17.9 us: exchange_with(): return lax.ppermute(x, BOTH, pairs)]
  transfers between devices with their start and end apart: 3 -> 9, of which waited for: 2 -> 4; matrix products, arithmetic and copies ran while one was open for 18% -> 1% of each run, Pallas kernels for 0% -> 18%
where the time goes in v1:
time: 210 us
  waiting for transfers between devices  86.9 us (41%)
  Pallas kernels  50.4 us (24%)
  blocking collectives  34.9 us (17%)
  starting transfers between devices  24 us (11%)
  local copies, waits for them, and re-layouts  12.9 us (6%)
    all_to_all x1, waiting for transfers between devices, local(): got = lax.all_to_all(block, 'orb', split_axis=0, concat_axis=0, tiled=True)  69 us
    all_to_all x1, blocking collectives, local(): got = lax.all_to_all(block, 'orb', split_axis=0, concat_axis=0, tiled=True)  34.9 us
    pallas_call x3, Pallas kernels, partial_sums(): pl.pallas_call(functools.partial(partial_kernel, first), grid_spec=pltpu....  20.3 us
    ppermute x5, waiting for transfers between devices, exchange_with(): return lax.ppermute(x, BOTH, pairs)  17.9 us
    pallas_call x3, Pallas kernels, finish(): pl.pallas_call(finish_kernel, grid=(count,), in_specs=[shifted, pl.BlockS...  12.6 us
    all_to_all x1, starting transfers between devices, local(): got = lax.all_to_all(block, 'orb', split_axis=0, concat_axis=0, tiled=True)  12 us
    pallas_call x1, Pallas kernels, own_sums(): pl.pallas_call(own_kernel, grid_spec=pltpu.PrefetchScalarGridSpec(num_sca...  10.8 us
    unnamed x20, local copies, waits for them, and re-layouts  9.54 us
  transfers between devices with their start and end apart: 9, of which 4 were waited for; matrix products, arithmetic and copies ran while one was open for 1% of the time, Pallas kernels for 18%

profile of v1, /device:TPU:2, one launch (start us, length us, event | category | flops | bytes accessed | tf_op | source)
XLA Modules:
  0.0 209.8 jit_solution(10611398630493445350)
XLA Ops:
  0.6 4.6 %copy.16 = bf16[8,1024,256]{2,0,1:T(8,128)(2,1)S(1)} copy(bf16[8,1024,256]{2,1,0:T(8,128)(2,1)} %param.6) | data formatting | bytes 8388608 | tf_op args[0]
  5.2 0.0 copy-start.7
  5.2 1.9 copy-done.7
  7.1 1.9 slice.8
  9.0 12.0 %all-to-all-start = ((bf16[64,12,8,256]{3,2,1,0:T(8,128)(2,1)}), bf16[64,12,8,256]{3,2,1,0:T(8,128)(2,1)S(1)}, u32[]{:S(2)}, u32[]{:S(2)}) async-start(bf16[64,12,8,256]{3,2,1,0:T(8,128)(2,1)} %slice.8), calls=%async_computation | async-start | bytes 6291456 | tf_op jit(solution)/shard_map/all_to_all | solution.py:272
  21.1 0.0 copy-start.8
  21.1 3.1 %collective-permute-start = (bf16[4,256,256]{2,1,0:T(8,128)(2,1)}, bf16[4,256,256]{2,1,0:T(8,128)(2,1)}, u32[]{:S(2)}, u32[]{:S(2)}) collective-permute-start(bf16[4,256,256]{2,1,0:T(8,128)(2,1)} %refs_0_), channel_id=1, source_target_pairs={{1,0},{2,1},{3,2},{0,3},{5,4},{6,5},{7,6},{4,7},{9,8},{10,9},{11,1... | collective-permute-start | bytes 1572872 | tf_op jit(solution)/shard_map/ppermute | solution.py:262
  24.2 0.6 collective-permute-start.1
  24.8 1.0 collective-permute-start.2
  25.8 69.0 %all-to-all-done.refs_0_ = bf16[64,12,8,256]{3,2,1,0:T(8,128)(2,1)S(1)} async-done(((bf16[64,12,8,256]{3,2,1,0:T(8,128)(2,1)}), bf16[64,12,8,256]{3,2,1,0:T(8,128)(2,1)S(1)}, u32[]{:S(2)}, u32[]{:S(2)}) %all-to-all-start) | async-done | bytes 3145760 | tf_op jit(solution)/shard_map/all_to_all | solution.py:272
  94.8 0.0 copy-start.1
  94.8 1.6 collective-permute-start.3
  96.4 1.3 slice.9
  97.7 0.0 collective-permute-done.refs_1_
  97.7 0.0 collective-permute-done.1.refs_2_
  97.7 0.0 collective-permute-done.2.refs_3_
  97.7 34.9 %all_to_all.10.refs_1_ = bf16[64,4,8,256]{3,2,1,0:T(8,128)(2,1)} all-to-all(bf16[64,4,8,256]{3,2,1,0:T(8,128)(2,1)S(1)} %slice.9), channel_id=1, replica_groups=mesh['orb'=64,'pair'=4] {'orb'}, dimensions={0} | all-to-all | bytes 2097152 | tf_op jit(solution)/shard_map/all_to_all | solution.py:272
  132.6 0.4 collective-permute-start.4
  133.0 0.0 copy-done.8
  133.0 0.1 copy.15
  133.1 0.1 reshape.16.pairs_ref
  133.2 14.5 %collective-permute-done.4.refs_3_ = bf16[64,4,8,256]{3,2,1,0:T(8,128)(2,1)} collective-permute-done((bf16[64,4,8,256]{3,2,1,0:T(8,128)(2,1)}, bf16[64,4,8,256]{3,2,1,0:T(8,128)(2,1)}, u32[]{:S(2)}, u32[]{:S(2)}) %collective-permute-start.4) | collective-permute-done | bytes 1048608 | tf_op jit(solution)/shard_map/ppermute | solution.py:25
  147.7 0.0 collective-permute-done.3.refs_2_
  147.7 8.6 %shard_map.80 = f32[8,256,256]{2,1,0:T(8,128)} custom-call(s32[128]{0:T(128)S(1)} %reshape.16.pairs_ref, s32[1]{0:T(128)} %bitcast.4.begin_ref, bf16[64,12,8,256]{3,2,1,0:T(8,128)(2,1)S(1)} %all-to-all-done.refs_0_, bf16[64,4,8,256]{3,2,1,0:T(8,128)(2,1)} %all_to_all.10.refs_1_, bf16[64,12,8,256]{3,2,1,0:T(8,128)(2,1)} %collective-permute-done.3.refs_2_, ...), custom_call_target="tpu_custom_call" | custom-call | flops 4294967296 | bytes 10485760 | tf_op jit(solution)/shard_map/pallas_call | solution.py:71
  156.3 1.9 collective-permute-start.6
  158.2 0.0 copy-done.1
  158.2 6.3 %shard_map.81 = f32[4,256,256]{2,1,0:T(8,128)} custom-call(s32[128]{0:T(128)S(1)} %reshape.16.pairs_ref, s32[1]{0:T(128)} %bitcast.4.begin_ref, bf16[64,12,8,256]{3,2,1,0:T(8,128)(2,1)S(1)} %all-to-all-done.refs_0_, bf16[64,4,8,256]{3,2,1,0:T(8,128)(2,1)} %all_to_all.10.refs_1_, bf16[64,12,8,256]{3,2,1,0:T(8,128)(2,1)} %collective-permute-done.3.refs_2_, ...), custom_call_target="tpu_custom_call" | custom-call | flops 2147483648 | bytes 9437184 | tf_op jit(solution)/shard_map/pallas_call | solution.py:71
  164.5 0.0 copy-start
  164.5 1.5 collective-permute-start.7
  166.0 0.0 copy-start.2
  166.1 1.9 copy-done.2
  167.9 0.0 copy-start.5
  167.9 0.0 copy-start.6
  167.9 5.4 %shard_map.79 = f32[4,256,256]{2,1,0:T(8,128)S(1)} custom-call(s32[128]{0:T(128)S(1)} %reshape.16.pairs_ref, s32[1]{0:T(128)} %bitcast.4.begin_ref, bf16[64,12,8,256]{3,2,1,0:T(8,128)(2,1)S(1)} %copy-done.2, bf16[64,4,8,256]{3,2,1,0:T(8,128)(2,1)} %all_to_all.10.refs_1_, bf16[64,12,8,256]{3,2,1,0:T(8,128)(2,1)} %collective-permute-done.3.refs_2_, ...), custom_call_target="tpu_custom_call" | custom-call | flops 2147483648 | bytes 9437184 | tf_op jit(solution)/shard_map/pallas_call | solution.py:71
  173.3 1.9 collective-permute-start.5
  175.2 0.0 copy-done
  175.2 0.0 copy-done.5
  175.2 0.0 copy-done.6
  175.2 0.0 copy-start.4
  175.2 1.0 copy-done.4
  176.3 0.0 copy-start.3
  176.3 6.8 %shard_map.77 = (f32[16,256,256]{2,1,0:T(8,128)S(1)}, f32[16,256,256]{2,1,0:T(8,128)S(1)}) custom-call(s32[128]{0:T(128)S(1)} %reshape.16.pairs_ref, s32[1]{0:T(128)} %bitcast.begin_ref, s32[16]{0:T(128)S(1)} %fusion.slot_ref, f32[16]{0:T(128)S(1)} %copy-done.5, s32[16]{0:T(128)S(1)} %copy-done.6, bf16[4,256,256]{2,1,0:T(8,128)(2,1)S(1)} %copy-done.4, ...), custom_call_target="tpu_custom_call" | custom-call | flops 1073741824 | bytes 12582912 | tf_op jit(solution)/shard_map/pallas_call | solution.py:185
  183.0 0.0 copy-done.3
  183.1 10.8 %shard_map.78.own_ref = f32[16,256,256]{2,1,0:T(8,128)S(1)} custom-call(s32[128]{0:T(128)S(1)} %reshape.16.pairs_ref, s32[1]{0:T(128)} %bitcast.begin_ref, bf16[64,12,8,256]{3,2,1,0:T(8,128)(2,1)S(1)} %copy-done.3, bf16[64,4,8,256]{3,2,1,0:T(8,128)(2,1)} %all_to_all.10.refs_1_, ...), custom_call_target="tpu_custom_call", output_to_operand_aliasing={{}: (6, {})} | custom-call | flops 8589934592 | bytes 16777216 | tf_op jit(solution)/shard_map/pallas_call | solution.py:114
  193.8 1.3 collective-permute-done.7.other_ref
  195.2 3.4 %shard_map.82 = (bf16[16,256,256]{2,1,0:T(8,128)(2,1)}, bf16[16,256,256]{2,1,0:T(8,128)(2,1)}) custom-call(f32[16,256,256]{2,1,0:T(8,128)S(1)} %shard_map.78.own_ref, f32[4,256,256]{2,1,0:T(8,128)} %collective-permute-done.7.other_ref, bf16[16,256,256]{2,1,0:T(8,128)(2,1)S(1)} %copy-done, f32[16,256,256]{2,1,0:T(8,128)S(1)} %get-tuple-element.19.inv_ref), custom_call_target="tpu_custom_call" | custom-call | flops 1310720 | bytes 4718592 | tf_op jit(solution)/shard_map/pallas_call | solution.py:223
  198.6 0.0 collective-permute-done.6.other_ref
  198.6 5.7 %shard_map.83 = (bf16[16,256,256]{2,1,0:T(8,128)(2,1)}, bf16[16,256,256]{2,1,0:T(8,128)(2,1)}) custom-call(f32[16,256,256]{2,1,0:T(8,128)S(1)} %shard_map.78.own_ref, f32[8,256,256]{2,1,0:T(8,128)} %collective-permute-done.6.other_ref, bf16[16,256,256]{2,1,0:T(8,128)(2,1)S(1)} %copy-done, ...), custom_call_target="tpu_custom_call", output_to_operand_aliasing={{0}: (4, {}), {1}: (5, {})} | custom-call | flops 2621440 | bytes 9437184 | tf_op jit(solution)/shard_map/pallas_call | solution.py:223
  204.3 2.1 collective-permute-done.5.other_ref
  206.4 3.4 %shard_map.84 = (bf16[16,256,256]{2,1,0:T(8,128)(2,1)}, bf16[16,256,256]{2,1,0:T(8,128)(2,1)}) custom-call(f32[16,256,256]{2,1,0:T(8,128)S(1)} %shard_map.78.own_ref, f32[4,256,256]{2,1,0:T(8,128)} %collective-permute-done.5.other_ref, bf16[16,256,256]{2,1,0:T(8,128)(2,1)S(1)} %copy-done, ...), custom_call_target="tpu_custom_call", output_to_operand_aliasing={{0}: (4, {}), {1}: (5, {})} | custom-call | flops 1310720 | bytes 4718592 | tf_op jit(solution)/shard_map/pallas_call | solution.py:223
  (1 shorter events, 0.0 us)
Async XLA Ops:
  5.2 1.9 copy-start.7
  9.0 85.8 %all-to-all-start = ((bf16[64,12,8,256]{3,2,1,0:T(8,128)(2,1)}), bf16[64,12,8,256]{3,2,1,0:T(8,128)(2,1)S(1)}, u32[]{:S(2)}, u32[]{:S(2)}) async-start(bf16[64,12,8,256]{3,2,1,0:T(8,128)(2,1)} %slice.8), calls=%async_computation | async-start | bytes 6291456 | tf_op jit(solution)/shard_map/all_to_all | solution.py:272
  21.1 111.9 %copy-start.8 = (s32[64,2]{0,1:T(2,128)S(1)}, s32[64,2]{0,1:T(2,128)}, u32[]{:S(2)}) copy-start(s32[64,2]{0,1:T(2,128)} %param.11) | copy-start | bytes 1540
  21.1 76.6 %collective-permute-start = (bf16[4,256,256]{2,1,0:T(8,128)(2,1)}, bf16[4,256,256]{2,1,0:T(8,128)(2,1)}, u32[]{:S(2)}, u32[]{:S(2)}) collective-permute-start(bf16[4,256,256]{2,1,0:T(8,128)(2,1)} %refs_0_), channel_id=1, source_target_pairs={{1,0},{2,1},{3,2},{0,3},{5,4},{6,5},{7,6},{4,7},{9,8},{10,9},{11,1... | collective-permute-start | bytes 1572872 | tf_op jit(solution)/shard_map/ppermute | solution.py:262
  24.2 73.5 %collective-permute-start.1 = (bf16[4,256,256]{2,1,0:T(8,128)(2,1)}, bf16[4,256,256]{2,1,0:T(8,128)(2,1)}, u32[]{:S(2)}, u32[]{:S(2)}) collective-permute-start(bf16[4,256,256]{2,1,0:T(8,128)(2,1)} %refs_0_), channel_id=1, source_target_pairs={{2,0},{3,1},{0,2},{1,3},{6,4},{7,5},{4,6},{5,7},{10,8},{11,9},{8,1... | collective-permute-start | bytes 1572872 | tf_op jit(solution)/shard_map/ppermute | solution.py:262
  24.8 72.9 %collective-permute-start.2 = (bf16[4,256,256]{2,1,0:T(8,128)(2,1)}, bf16[4,256,256]{2,1,0:T(8,128)(2,1)}, u32[]{:S(2)}, u32[]{:S(2)}) collective-permute-start(bf16[4,256,256]{2,1,0:T(8,128)(2,1)} %refs_0_), channel_id=1, source_target_pairs={{3,0},{0,1},{1,2},{2,3},{7,4},{4,5},{5,6},{6,7},{11,8},{8,9},{9,10... | collective-permute-start | bytes 1572872 | tf_op jit(solution)/shard_map/ppermute | solution.py:262
  94.8 63.4 %copy-start.1 = (bf16[64,12,8,256]{3,2,1,0:T(8,128)(2,1)}, bf16[64,12,8,256]{3,2,1,0:T(8,128)(2,1)S(1)}, u32[]{:S(2)}) copy-start(bf16[64,12,8,256]{3,2,1,0:T(8,128)(2,1)S(1)} %all-to-all-done.refs_0_) | copy-start | bytes 9437188
  94.8 52.9 %collective-permute-start.3 = (bf16[64,12,8,256]{3,2,1,0:T(8,128)(2,1)S(1)}, bf16[64,12,8,256]{3,2,1,0:T(8,128)(2,1)}, u32[]{:S(2)}, u32[]{:S(2)}) collective-permute-start(bf16[64,12,8,256]{3,2,1,0:T(8,128)(2,1)S(1)} %all-to-all-done.refs_0_), channel_id=1, source_target_pairs={{0,1},{1,0},{2,3},{3,2},{4,7},{5,6},{6,5},{7,4},{8,9},{9,8},{10,11... | collective-permute-start | bytes 9437192 | tf_op jit(solution)/shard_map/ppermute | solution.py:25
  132.6 15.1 %collective-permute-start.4 = (bf16[64,4,8,256]{3,2,1,0:T(8,128)(2,1)}, bf16[64,4,8,256]{3,2,1,0:T(8,128)(2,1)}, u32[]{:S(2)}, u32[]{:S(2)}) collective-permute-start(bf16[64,4,8,256]{3,2,1,0:T(8,128)(2,1)} %all_to_all.10.refs_1_), channel_id=1, source_target_pairs={{0,1},{1,0},{2,3},{3,2},{4,7},{5,6},{6,5},{7,4},{8,9},{9,8},{10,11... | collective-permute-start | bytes 3145736 | tf_op jit(solution)/shard_map/ppermute | solution.py:25
  156.3 42.3 %collective-permute-start.6 = (f32[8,256,256]{2,1,0:T(8,128)}, f32[8,256,256]{2,1,0:T(8,128)}, u32[]{:S(2)}, u32[]{:S(2)}) collective-permute-start(f32[8,256,256]{2,1,0:T(8,128)} %shard_map.80), channel_id=1, source_target_pairs={{0,3},{1,2},{2,1},{3,0},{4,5},{5,4},{6,7},{7,6},{8,11},{9,10},{10,... | collective-permute-start | bytes 6291464 | tf_op jit(solution)/shard_map/ppermute | solution.py:25
  164.5 10.7 %copy-start = (bf16[16,256,256]{2,1,0:T(8,128)(2,1)S(1)}, bf16[16,256,256]{2,1,0:T(8,128)(2,1)}, u32[]{:S(2)}) copy-start(bf16[16,256,256]{2,1,0:T(8,128)(2,1)} %amp_ref.5) | copy-start | bytes 6291460
  164.5 30.6 %collective-permute-start.7 = (f32[4,256,256]{2,1,0:T(8,128)}, f32[4,256,256]{2,1,0:T(8,128)}, u32[]{:S(2)}, u32[]{:S(2)}) collective-permute-start(f32[4,256,256]{2,1,0:T(8,128)} %shard_map.81), channel_id=1, source_target_pairs={{0,3},{1,2},{2,1},{3,0},{4,5},{5,4},{6,7},{7,6},{8,11},{9,10},{10,... | collective-permute-start | bytes 3145736 | tf_op jit(solution)/shard_map/ppermute | solution.py:25
  166.0 1.9 copy-start.2
  167.9 7.3 %copy-start.5 = (f32[16]{0:T(128)S(1)}, f32[16]{0:T(128)}, u32[]{:S(2)}) copy-start(f32[16]{0:T(128)} %occ_ref.1) | copy-start | bytes 196
  167.9 7.3 %copy-start.6 = (s32[16]{0:T(128)S(1)}, s32[16]{0:T(128)}, u32[]{:S(2)}) copy-start(s32[16]{0:T(128)} %len_ref.1) | copy-start | bytes 196
  173.3 33.0 %collective-permute-start.5 = (f32[4,256,256]{2,1,0:T(8,128)S(1)}, f32[4,256,256]{2,1,0:T(8,128)}, u32[]{:S(2)}, u32[]{:S(2)}) collective-permute-start(f32[4,256,256]{2,1,0:T(8,128)S(1)} %shard_map.79), channel_id=1, source_target_pairs={{0,3},{1,2},{2,1},{3,0},{4,5},{5,4},{6,7},{7,6},{8,11},{9,10},{10,... | collective-permute-start | bytes 3145736 | tf_op jit(solution)/shard_map/ppermute | solution.py:25
  175.2 1.0 copy-start.4
  176.3 6.8 %copy-start.3 = (bf16[64,12,8,256]{3,2,1,0:T(8,128)(2,1)S(1)}, bf16[64,12,8,256]{3,2,1,0:T(8,128)(2,1)}, u32[]{:S(2)}) copy-start(bf16[64,12,8,256]{3,2,1,0:T(8,128)(2,1)} %copy-done.1) | copy-start | bytes 9437188

commit v2 on v1

--- a/solution.py
+++ b/solution.py
@@ -10,6 +10,9 @@
 BOTH = ("orb", "pair")
 SPLITS = ((0, 12), (12, 16))
 VMEM = 24 * 2**20
+ARRANGE = 8
+STEPS = 32767.0
+TAIL = 16
 
 
 def gather_mate(orb, y):
@@ -25,22 +28,60 @@
     return lax.ppermute(x, BOTH, pairs)
 
 
+def arrange_kernel(move_ref, x_ref, *out_refs):
+    aux, rows, dom = x_ref.shape
+    group = SPLITS[-1][1]
+    for g in range(rows // group):
+        block = x_ref[:, g * group : (g + 1) * group, :].reshape(aux * group, dom)
+        moved = jnp.dot(move_ref[...], block, preferred_element_type=jnp.float32)
+        moved = moved.astype(x_ref.dtype).reshape(group, aux, dom)
+        for (lo, hi), out_ref in zip(SPLITS, out_refs):
+            out_ref[g] = moved[lo:hi]
+
+
+def arrange(integrals, orbs):
+    aux, occ, dom = integrals.shape
+    group = occ // orbs
+    size = aux * group
+    new = jnp.arange(size, dtype=jnp.int32)
+    source = (new % aux) * group + new // aux
+    move = (source[:, None] == new[None, :]).astype(integrals.dtype)
+    return pl.pallas_call(
+        arrange_kernel,
+        grid=(orbs // ARRANGE,),
+        in_specs=[
+            pl.BlockSpec((size, size), lambda g: (0, 0)),
+            pl.BlockSpec((aux, ARRANGE * group, dom), lambda g: (0, g, 0)),
+        ],
+        out_specs=[
+            pl.BlockSpec((ARRANGE, hi - lo, aux, dom), lambda g: (g, 0, 0, 0))
+            for lo, hi in SPLITS
+        ],
+        out_shape=[
+            jax.ShapeDtypeStruct((orbs, hi - lo, aux, dom), integrals.dtype)
+            for lo, hi in SPLITS
+        ],
+        compiler_params=pltpu.CompilerParams(vmem_limit_bytes=VMEM),
+        cost_estimate=pl.CostEstimate(
+            flops=2 * orbs * size * size * dom,
+            bytes_accessed=4 * aux * occ * dom,
+            transcendentals=0,
+        ),
+    )(move, integrals)
+
+
 def load_blocks(parts, held, sems):
-    copies = []
-    for half in range(2):
-        for c, (lo, hi) in enumerate(SPLITS):
-            k = half * len(SPLITS) + c
-            copies.append(
-                pltpu.make_async_copy(parts[k], held.at[half, :, lo:hi], sems.at[k])
-            )
-    return copies
-
-
-def half_sum(held, i, j):
+    return [
+        pltpu.make_async_copy(part, held.at[c // len(SPLITS), :, lo:hi], sems.at[c])
+        for c, (part, (lo, hi)) in enumerate(zip(parts, SPLITS * held.shape[0]))
+    ]
+
+
+def block_sum(held, i, j):
     total = None
-    for half in range(2):
-        left = held[half, :, i].reshape(-1, held.shape[-1])
-        right = held[half, :, j].reshape(-1, held.shape[-1])
+    for h in range(held.shape[0]):
+        left = held[h, :, i].reshape(-1, held.shape[-1])
+        right = held[h, :, j].reshape(-1, held.shape[-1])
         term = lax.dot_general(
             left, right, (((0,), (0,)), ((), ())), preferred_element_type=jnp.float32
         )
@@ -48,8 +89,33 @@
     return total
 
 
-def partial_kernel(first, pairs_ref, begin_ref, *refs):
-    parts, out_refs, held, sems = refs[:4], refs[4:-2], refs[-2], refs[-1]
+def column_tops(mantissa, power):
+    return mantissa.astype(jnp.float32) * jnp.exp2(power.astype(jnp.float32))
+
+
+def encode(total, out_ref):
+    dom = total.shape[0]
+    top = jnp.maximum(jnp.max(jnp.abs(total), axis=0, keepdims=True), 1e-30)
+    power = jnp.floor(jnp.log2(top)).astype(jnp.int32) - 13
+    mantissa = (top * jnp.exp2(-power.astype(jnp.float32))).astype(jnp.int32) + 1
+    scale = STEPS / column_tops(mantissa, power)
+    out_ref[0, :dom, :] = jnp.round(total * scale).astype(jnp.int32).astype(jnp.int16)
+    rows = lax.broadcasted_iota(jnp.int32, (TAIL, total.shape[1]), 0)
+    out_ref[0, dom:, :] = jnp.where(rows == 0, mantissa, power).astype(jnp.int16)
+
+
+def decode(code_ref):
+    dom = code_ref.shape[-1]
+    tail = code_ref[0, dom:, :].astype(jnp.int32)
+    step = column_tops(tail[0:1], tail[1:2]) * (1.0 / STEPS)
+    return code_ref[0, :dom, :].astype(jnp.float32) * step
+
+
+def sums_kernel(rows, added, coded, pairs_ref, begin_ref, *refs):
+    held, sems = refs[-2:]
+    count = held.shape[0] * len(SPLITS)
+    parts, base_refs = refs[:count], refs[count : count + sum(added)]
+    out_refs = refs[count + sum(added) : -2]
     p = pl.program_id(0)
 
     @pl.when(p == 0)
@@ -60,78 +126,54 @@
         for c in copies:
             c.wait()
 
-    row = begin_ref[0] + first + p
-    out_refs[0][0] = half_sum(held, pairs_ref[2 * row], pairs_ref[2 * row + 1])
-
-
-def partial_sums(parts, pairs, begin, first, count):
-    _, _, aux, dom = parts[0].shape
+    bases = iter(base_refs)
+    for k, (first, has) in enumerate(zip(rows, added)):
+        row = begin_ref[k] + first + p
+        total = block_sum(held, pairs_ref[2 * row], pairs_ref[2 * row + 1])
+        if has:
+            total += next(bases)[0]
+        if coded:
+            encode(total, out_refs[k])
+        else:
+            out_refs[k][0] = total
+
+
+def pair_sums(parts, bases, pairs, begins, firsts, count, coded=False):
+    src, _, aux, dom = parts[0].shape
     orbs = SPLITS[-1][1]
-    src = parts[0].shape[0]
+    added = tuple(b is not None for b in bases)
+    in_specs = [pl.BlockSpec(memory_space=pl.ANY)] * len(parts) + [
+        pl.BlockSpec((1, dom, dom), lambda p, *_, first=first: (p + first, 0, 0))
+        for first, has in zip(firsts, added)
+        if has
+    ]
+    shape = (
+        jax.ShapeDtypeStruct((count, dom + TAIL, dom), jnp.int16)
+        if coded
+        else jax.ShapeDtypeStruct((count, dom, dom), jnp.float32)
+    )
     return pl.pallas_call(
-        functools.partial(partial_kernel, first),
+        functools.partial(sums_kernel, tuple(firsts), added, coded),
         grid_spec=pltpu.PrefetchScalarGridSpec(
             num_scalar_prefetch=2,
             grid=(count,),
-            in_specs=[pl.BlockSpec(memory_space=pl.ANY)] * 4,
-            out_specs=[pl.BlockSpec((1, dom, dom), lambda p, *_: (p, 0, 0))],
+            in_specs=in_specs,
+            out_specs=[pl.BlockSpec((1,) + shape.shape[1:], lambda p, *_: (p, 0, 0))]
+            * len(begins),
             scratch_shapes=[
-                pltpu.VMEM((2, src, orbs, aux, dom), jnp.bfloat16),
-                pltpu.SemaphoreType.DMA((4,)),
+                pltpu.VMEM((len(parts) // len(SPLITS), src, orbs, aux, dom), jnp.bfloat16),
+                pltpu.SemaphoreType.DMA((len(parts),)),
             ],
         ),
-        out_shape=[jax.ShapeDtypeStruct((count, dom, dom), jnp.float32)],
+        out_shape=[shape] * len(begins),
         compiler_params=pltpu.CompilerParams(vmem_limit_bytes=VMEM),
         cost_estimate=pl.CostEstimate(
-            flops=2 * count * 2 * src * aux * dom * dom * 4,
-            bytes_accessed=4 * src * orbs * aux * dom + count * dom * dom * 4,
+            flops=2 * count * len(begins) * src * aux * dom * dom * len(parts) // len(SPLITS),
+            bytes_accessed=2 * src * orbs * aux * dom * len(parts) // len(SPLITS)
+            + count * dom * dom * 4 * (len(begins) + sum(added)),
             transcendentals=0,
         ),
-    )(pairs, begin, *parts)[0]
-
-
-def own_kernel(pairs_ref, begin_ref, *refs):
-    parts, base_ref, out_ref, held, sems = refs[:4], refs[4], refs[5], refs[6], refs[7]
-    p = pl.program_id(0)
-
-    @pl.when(p == 0)
-    def _():
-        copies = load_blocks(parts, held, sems)
-        for c in copies:
-            c.start()
-        for c in copies:
-            c.wait()
-
-    row = begin_ref[0] + p
-    out_ref[0] = base_ref[0] + half_sum(held, pairs_ref[2 * row], pairs_ref[2 * row + 1])
-
-
-def own_sums(parts, base, pairs, begin):
-    src, _, aux, dom = parts[0].shape
-    orbs = SPLITS[-1][1]
-    count = base.shape[0]
-    one = pl.BlockSpec((1, dom, dom), lambda p, *_: (p, 0, 0))
-    return pl.pallas_call(
-        own_kernel,
-        grid_spec=pltpu.PrefetchScalarGridSpec(
-            num_scalar_prefetch=2,
-            grid=(count,),
-            in_specs=[pl.BlockSpec(memory_space=pl.ANY)] * 4 + [one],
-            out_specs=[one],
-            scratch_shapes=[
-                pltpu.VMEM((2, src, orbs, aux, dom), jnp.bfloat16),
-                pltpu.SemaphoreType.DMA((4,)),
-            ],
-        ),
-        out_shape=[jax.ShapeDtypeStruct((count, dom, dom), jnp.float32)],
-        input_output_aliases={6: 0},
-        compiler_params=pltpu.CompilerParams(vmem_limit_bytes=VMEM),
-        cost_estimate=pl.CostEstimate(
-            flops=2 * count * 2 * src * aux * dom * dom * 4,
-            bytes_accessed=4 * src * orbs * aux * dom + count * dom * dom * 8,
-            transcendentals=0,
-        ),
-    )(pairs, begin, *parts, base)[0]
+    )(pairs, jnp.stack(begins), *parts, *[b for b in bases if b is not None])
 
 
 def fock_kernel(pairs_ref, begin_ref, slot_ref, occ_ref, len_ref, *refs):
@@ -208,7 +250,7 @@
     resid_ref, new_ref = refs[-2:]
     inv = inv_ref[0]
     inside = inv != 0.0
-    resid = jnp.where(inside, own_ref[0] + other_ref[0], 0.0)
+    resid = jnp.where(inside, own_ref[0] + decode(other_ref), 0.0)
     old = amp_ref[0].astype(jnp.float32)
     resid_ref[0] = resid.astype(resid_ref.dtype)
     new_ref[0] = jnp.where(inside, old - resid * inv, 0.0).astype(new_ref.dtype)
@@ -225,7 +267,7 @@
         grid=(count,),
         in_specs=[
             shifted,
-            pl.BlockSpec((1, dom, dom), lambda p: (p, 0, 0)),
+            pl.BlockSpec((1,) + other.shape[1:], lambda p: (p, 0, 0)),
             shifted,
             shifted,
         ]
@@ -242,7 +284,7 @@
     )(own, other, amplitudes, inv, *extra)
 
 
-CHUNKS = ((0, 4), (4, 12), (12, 16))
+CHUNKS = ((0, 6), (6, 11), (11, 16))
 
 
 def local(orbs, ys, integrals, fock_blocks, occ_energy, dom_len, amplitudes, pair_list):
@@ -253,8 +295,8 @@
     even = lax.rem(lax.axis_index("orb"), 2) == 0
     mate = jnp.where(even, 3 - y, y ^ 1)
     pairs = pair_list.reshape(-1)
-    mine = (y * owned).reshape(1).astype(jnp.int32)
-    theirs = (mate * owned).reshape(1).astype(jnp.int32)
+    mine = (y * owned).astype(jnp.int32)
+    theirs = (mate * owned).astype(jnp.int32)
     each = fock_blocks.shape[0]
     number = jnp.arange(group, dtype=jnp.int32)
     slot = ((number // each - y) & 3) * each + number % each
@@ -263,23 +305,25 @@
         for shift in (1, 2, 3)
     ]
 
-    blocks = integrals.reshape(aux, orbs, group, dom).transpose(1, 2, 0, 3)
+    blocks = arrange(integrals, orbs)
     near, far = [], []
-    for c, (lo, hi) in enumerate(SPLITS):
-        block = blocks[:, lo:hi]
+    for c, block in enumerate(blocks):
         if c == len(SPLITS) - 1:
             block, *focks = lax.optimization_barrier([block] + focks)
         got = lax.all_to_all(block, "orb", split_axis=0, concat_axis=0, tiled=True)
         near.append(got)
         far.append(exchange_with(got, gather_mate, orbs, ys))
-    parts = near + far
-
+
+    base, inv = fock_terms(
+        focks, amplitudes, pairs, mine.reshape(1), slot, occ_energy, dom_len
+    )
+    after, base, inv = lax.optimization_barrier((near[0], base, inv))
+    (theirs_near,) = pair_sums([after] + near[1:], [None], pairs, [theirs], [0], owned)
     others = []
     for lo, hi in CHUNKS:
-        sums = partial_sums(parts, pairs, theirs, lo, hi - lo)
+        (sums,) = pair_sums(far, [theirs_near], pairs, [theirs], [lo], hi - lo, True)
         others.append(exchange_with(sums, sum_mate, orbs, ys))
-    base, inv = fock_terms(focks, amplitudes, pairs, mine, slot, occ_energy, dom_len)
-    own = own_sums(parts, base, pairs, mine)
+    (own,) = pair_sums(near + far, [base], pairs, [mine], [0], owned)
     held = None
     for (lo, _), other in zip(CHUNKS, others):
         held = finish(own, other, amplitudes, inv, lo, held)

time: 210 us -> 185 us (0.88)
  waiting for transfers between devices: 86.9 us -> 68.4 us
  local copies, waits for them, and re-layouts: 12.9 us -> 4.99 us
    ppermute x5, waiting for transfers between devices: 17.9 us -> 0.01 us  [exchange_with(): return lax.ppermute(x, BOTH, pairs)]
    pallas_call x3, Pallas kernels: 12.6 us -> 7.1 us  [finish(): pl.pallas_call(finish_kernel, grid=(count,), in_specs=[shifted, pl.BlockS...]
    pallas_call x4 -> x6, Pallas kernels: 31.1 us -> 36 us  [the longest x5 31.4 us: pair_sums(): pl.pallas_call(functools.partial(sums_kernel, tuple(firsts), added, coded...]
    unnamed x20 -> x15, local copies, waits for them, and re-layouts: 9.54 us -> 4.85 us
    slice x2 -> x0, local copies, waits for them, and re-layouts: 3.2 us -> none  [local(): block = blocks[:, lo:hi]]
  transfers between devices with their start and end apart: 9 -> 9, of which waited for: 4 -> 1; matrix products, arithmetic and copies ran while one was open for 1% -> 0% of each run, Pallas kernels for 18% -> 21%
where the time goes in v2:
time: 185 us
  waiting for transfers between devices  68.4 us (37%)
  Pallas kernels  49.7 us (27%)
  blocking collectives  35.1 us (19%)
  starting transfers between devices  25.4 us (14%)
  local copies, waits for them, and re-layouts  4.99 us (3%)
    all_to_all x1, waiting for transfers between devices, local(): got = lax.all_to_all(block, 'orb', split_axis=0, concat_axis=0, tiled=True)  68.4 us
    all_to_all x1, blocking collectives, local(): got = lax.all_to_all(block, 'orb', split_axis=0, concat_axis=0, tiled=True)  35.1 us
    pallas_call x5, Pallas kernels, pair_sums(): pl.pallas_call(functools.partial(sums_kernel, tuple(firsts), added, coded...  31.4 us
    all_to_all x1, starting transfers between devices, local(): got = lax.all_to_all(block, 'orb', split_axis=0, concat_axis=0, tiled=True)  12.3 us
    ppermute x5, starting transfers between devices, exchange_with(): return lax.ppermute(x, BOTH, pairs)  7.82 us
    pallas_call x3, Pallas kernels, finish(): pl.pallas_call(finish_kernel, grid=(count,), in_specs=[shifted, pl.BlockS...  7.1 us
    pallas_call x1, Pallas kernels, fock_terms(): pl.pallas_call(fock_kernel, grid_spec=pltpu.PrefetchScalarGridSpec(num_sc...  6.63 us
    ppermute x3, starting transfers between devices, local(): lax.ppermute(fock_blocks, 'pair', [((s + shift) % ys, s) for s in range(y...  5.3 us
  transfers between devices with their start and end apart: 9, of which 1 were waited for; matrix products, arithmetic and copies ran while one was open for 0% of the time, Pallas kernels for 21%

profile of v2, /device:TPU:2, one launch (start us, length us, event | category | flops | bytes accessed | tf_op | source)
XLA Modules:
  0.0 184.5 jit_solution(12015803083645691736)
XLA Ops:
  0.6 0.1 fusion.move_ref
  0.7 0.0 copy-start.2
  0.7 2.2 %copy-done.2 = bf16[8,1024,256]{2,1,0:T(8,128)(2,1)S(1)} copy-done((bf16[8,1024,256]{2,1,0:T(8,128)(2,1)S(1)}, bf16[8,1024,256]{2,1,0:T(8,128)(2,1)}, u32[]{:S(2)}) %copy-start.2) | copy-done | bytes 4194328
  2.9 4.7 %shard_map.77 = (bf16[64,12,8,256]{3,2,1,0:T(8,128)(2,1)}, bf16[64,4,8,256]{3,2,1,0:T(8,128)(2,1)S(1)}) custom-call(bf16[128,128]{1,0:T(8,128)(2,1)S(1)} %fusion.move_ref, bf16[8,1024,256]{2,1,0:T(8,128)(2,1)S(1)} %copy-done.2), custom_call_target="tpu_custom_call" | custom-call | flops 536870912 | bytes 8388608 | tf_op jit(solution)/shard_map/pallas_call | solution.py:49
  7.6 0.0 copy-start.3
  7.6 1.0 copy-done.3
  8.5 0.0 copy-start.6
  8.6 0.0 copy-start.4
  8.6 0.0 copy-start.5
  8.6 12.3 %all-to-all-start = ((bf16[64,12,8,256]{3,2,1,0:T(8,128)(2,1)}), bf16[64,12,8,256]{3,2,1,0:T(8,128)(2,1)}, u32[]{:S(2)}, u32[]{:S(2)}) async-start(bf16[64,12,8,256]{3,2,1,0:T(8,128)(2,1)} %get-tuple-element.18), calls=%async_computation | async-start | bytes 6291456 | tf_op jit(solution)/shard_map/all_to_all | solution.py:313
  20.9 3.3 %collective-permute-start.1 = (bf16[4,256,256]{2,1,0:T(8,128)(2,1)}, bf16[4,256,256]{2,1,0:T(8,128)(2,1)}, u32[]{:S(2)}, u32[]{:S(2)}) collective-permute-start(bf16[4,256,256]{2,1,0:T(8,128)(2,1)} %refs_0_), channel_id=1, source_target_pairs={{2,0},{3,1},{0,2},{1,3},{6,4},{7,5},{4,6},{5,7},{10,8},{11,9},{8,1... | collective-permute-start | bytes 1572872 | tf_op jit(solution)/shard_map/ppermute | solution.py:304
  24.1 1.1 collective-permute-start
  25.2 1.0 collective-permute-start.2
  26.2 68.4 %all-to-all-done.refs_0_ = bf16[64,12,8,256]{3,2,1,0:T(8,128)(2,1)} async-done(((bf16[64,12,8,256]{3,2,1,0:T(8,128)(2,1)}), bf16[64,12,8,256]{3,2,1,0:T(8,128)(2,1)}, u32[]{:S(2)}, u32[]{:S(2)}) %all-to-all-start) | async-done | bytes 3145760 | tf_op jit(solution)/shard_map/all_to_all | solution.py:313
  94.5 1.6 collective-permute-start.3
  96.1 0.0 collective-permute-done.1.refs_2_
  96.1 0.0 collective-permute-done.refs_1_
  96.1 0.0 collective-permute-done.2.refs_3_
  96.1 35.1 %all_to_all.10.refs_1_ = bf16[64,4,8,256]{3,2,1,0:T(8,128)(2,1)} all-to-all(bf16[64,4,8,256]{3,2,1,0:T(8,128)(2,1)} %copy-done.3), channel_id=1, replica_groups=mesh['orb'=64,'pair'=4] {'orb'}, dimensions={0} | all-to-all | bytes 2097152 | tf_op jit(solution)/shard_map/all_to_all | solution.py:313
  131.2 0.1 collective-permute-start.4
  131.3 0.0 copy-done.6
  131.3 0.1 copy.13
  131.4 0.1 reshape.30.pairs_ref
  131.6 0.0 copy-done.4
  131.6 0.0 copy-done.5
  131.6 0.0 copy-start
  131.6 1.6 copy-done
  133.2 6.6 %shard_map.78 = (f32[16,256,256]{2,1,0:T(8,128)S(1)}, f32[16,256,256]{2,1,0:T(8,128)S(1)}) custom-call(s32[128]{0:T(128)S(1)} %reshape.30.pairs_ref, s32[1]{0:T(128)} %bitcast.begin_ref, s32[16]{0:T(128)S(1)} %fusion.1.slot_ref, f32[16]{0:T(128)S(1)} %copy-done.4, s32[16]{0:T(128)S(1)} %copy-done.5, bf16[4,256,256]{2,1,0:T(8,128)(2,1)} %refs_0_, ...), custom_call_target="tpu_custom_call" | custom-call | flops 1073741824 | bytes 12582912 | tf_op jit(solution)/shard_map/pallas_call | solution.py:227
  139.8 8.0 %shard_map.80.refs_2_ = f32[16,256,256]{2,1,0:T(8,128)S(1)} custom-call(s32[128]{0:T(128)S(1)} %reshape.30.pairs_ref, s32[1]{0:T(128)} %bitcast.1.begin_ref, bf16[64,12,8,256]{3,2,1,0:T(8,128)(2,1)} %all-to-all-done.refs_0_, bf16[64,4,8,256]{3,2,1,0:T(8,128)(2,1)} %all_to_all.10.refs_1_), custom_call_target="tpu_custom_call" | custom-call | flops 1073741824 | bytes 8388608 | tf_op jit(solution)/shard_map/pallas_call | solution.py:155
  147.8 0.0 collective-permute-done.4.refs_3_.refs_1_
  147.8 0.0 collective-permute-done.3.refs_2_.refs_0_
  147.9 4.6 %shard_map.83 = s16[6,272,256]{2,1,0:T(8,128)(2,1)S(1)} custom-call(s32[128]{0:T(128)S(1)} %reshape.30.pairs_ref, s32[1]{0:T(128)} %bitcast.1.begin_ref, bf16[64,12,8,256]{3,2,1,0:T(8,128)(2,1)S(1)} %collective-permute-done.3.refs_2_.refs_0_, bf16[64,4,8,256]{3,2,1,0:T(8,128)(2,1)} %collective-permute-done.4.refs_3_.refs_1_, ...), custom_call_target="tpu_custom_call" | custom-call | flops 402653184 | bytes 7340032 | tf_op jit(solution)/shard_map/pallas_call | solution.py:155
  152.5 2.7 %collective-permute-start.7 = (s16[6,272,256]{2,1,0:T(8,128)(2,1)S(1)}, s16[6,272,256]{2,1,0:T(8,128)(2,1)S(1)}, u32[]{:S(2)}, u32[]{:S(2)}) collective-permute-start(s16[6,272,256]{2,1,0:T(8,128)(2,1)S(1)} %shard_map.83), channel_id=1, source_target_pairs={{0,3},{1,2},{2,1},{3,0},{4,5},{5,4},{6,7},{7,6},{8,11},{9,10},{10,... | collective-permute-start | bytes 2506760 | tf_op jit(solution)/shard_map/ppermute | solution.py:28
  155.2 4.2 %shard_map.82 = s16[5,272,256]{2,1,0:T(8,128)(2,1)S(1)} custom-call(s32[128]{0:T(128)S(1)} %reshape.30.pairs_ref, s32[1]{0:T(128)} %bitcast.1.begin_ref, bf16[64,12,8,256]{3,2,1,0:T(8,128)(2,1)S(1)} %collective-permute-done.3.refs_2_.refs_0_, bf16[64,4,8,256]{3,2,1,0:T(8,128)(2,1)} %collective-permute-done.4.refs_3_.refs_1_, ...), custom_call_target="tpu_custom_call" | custom-call | flops 335544320 | bytes 6815744 | tf_op jit(solution)/shard_map/pallas_call | solution.py:155
  159.4 0.7 collective-permute-start.6
  160.1 4.2 %shard_map.81 = s16[5,272,256]{2,1,0:T(8,128)(2,1)S(1)} custom-call(s32[128]{0:T(128)S(1)} %reshape.30.pairs_ref, s32[1]{0:T(128)} %bitcast.1.begin_ref, bf16[64,12,8,256]{3,2,1,0:T(8,128)(2,1)S(1)} %collective-permute-done.3.refs_2_.refs_0_, bf16[64,4,8,256]{3,2,1,0:T(8,128)(2,1)} %collective-permute-done.4.refs_3_.refs_1_, ...), custom_call_target="tpu_custom_call" | custom-call | flops 335544320 | bytes 6815744 | tf_op jit(solution)/shard_map/pallas_call | solution.py:155
  164.4 0.0 copy-start.1
  164.4 2.7 %collective-permute-start.5 = (s16[5,272,256]{2,1,0:T(8,128)(2,1)S(1)}, s16[5,272,256]{2,1,0:T(8,128)(2,1)S(1)}, u32[]{:S(2)}, u32[]{:S(2)}) collective-permute-start(s16[5,272,256]{2,1,0:T(8,128)(2,1)S(1)} %shard_map.81), channel_id=1, source_target_pairs={{0,3},{1,2},{2,1},{3,0},{4,5},{5,4},{6,7},{7,6},{8,11},{9,10},{10,... | collective-permute-start | bytes 2088968 | tf_op jit(solution)/shard_map/ppermute | solution.py:28
  167.1 10.3 %shard_map.79.own_ref = f32[16,256,256]{2,1,0:T(8,128)S(1)} custom-call(s32[128]{0:T(128)S(1)} %reshape.30.pairs_ref, s32[1]{0:T(128)} %bitcast.begin_ref, bf16[64,12,8,256]{3,2,1,0:T(8,128)(2,1)} %all-to-all-done.refs_0_, bf16[64,4,8,256]{3,2,1,0:T(8,128)(2,1)} %all_to_all.10.refs_1_, bf16[64,12,8,256]{3,2,1,0:T(8,128)(2,1)S(1)} %collective-permute-done.3.refs_2_.refs_0_, ...), custom_call_target="tpu_custom_call" | custom-call | flops 2147483648 | bytes 16777216 | tf_op jit(solution)/shard_map/pallas_call | solution.py:155
  177.4 0.0 collective-permute-done.7.other_ref
  177.4 0.0 copy-done.1
  177.4 2.5 %shard_map.84 = (bf16[16,256,256]{2,1,0:T(8,128)(2,1)}, bf16[16,256,256]{2,1,0:T(8,128)(2,1)}) custom-call(f32[16,256,256]{2,1,0:T(8,128)S(1)} %shard_map.79.own_ref, s16[6,272,256]{2,1,0:T(8,128)(2,1)S(1)} %collective-permute-done.7.other_ref, bf16[16,256,256]{2,1,0:T(8,128)(2,1)S(1)} %copy-done.1, f32[16,256,256]{2,1,0:T(8,128)S(1)} %get-tuple-element.29.inv_ref), custom_call_target="tpu_custom_call" | custom-call | flops 1966080 | bytes 7077888 | tf_op jit(solution)/shard_map/pallas_call | solution.py:265
  179.9 0.0 collective-permute-done.6.other_ref
  179.9 2.3 %shard_map.85 = (bf16[16,256,256]{2,1,0:T(8,128)(2,1)}, bf16[16,256,256]{2,1,0:T(8,128)(2,1)}) custom-call(f32[16,256,256]{2,1,0:T(8,128)S(1)} %shard_map.79.own_ref, s16[5,272,256]{2,1,0:T(8,128)(2,1)S(1)} %collective-permute-done.6.other_ref, bf16[16,256,256]{2,1,0:T(8,128)(2,1)S(1)} %copy-done.1, ...), custom_call_target="tpu_custom_call", output_to_operand_aliasing={{0}: (4, {}), {1}: (5, {})} | custom-call | flops 1638400 | bytes 5898240 | tf_op jit(solution)/shard_map/pallas_call | solution.py:265
  182.2 0.0 collective-permute-done.5.other_ref
  182.2 2.3 %shard_map.86 = (bf16[16,256,256]{2,1,0:T(8,128)(2,1)}, bf16[16,256,256]{2,1,0:T(8,128)(2,1)}) custom-call(f32[16,256,256]{2,1,0:T(8,128)S(1)} %shard_map.79.own_ref, s16[5,272,256]{2,1,0:T(8,128)(2,1)S(1)} %collective-permute-done.5.other_ref, bf16[16,256,256]{2,1,0:T(8,128)(2,1)S(1)} %copy-done.1, ...), custom_call_target="tpu_custom_call", output_to_operand_aliasing={{0}: (4, {}), {1}: (5, {})} | custom-call | flops 1638400 | bytes 5898240 | tf_op jit(solution)/shard_map/pallas_call | solution.py:265
  (2 shorter events, 0.0 us)
Async XLA Ops:
  0.7 2.2 %copy-start.2 = (bf16[8,1024,256]{2,1,0:T(8,128)(2,1)S(1)}, bf16[8,1024,256]{2,1,0:T(8,128)(2,1)}, u32[]{:S(2)}) copy-start(bf16[8,1024,256]{2,1,0:T(8,128)(2,1)} %x_ref.1) | copy-start | bytes 12582916
  7.6 1.0 copy-start.3
  8.5 122.8 %copy-start.6 = (s32[64,2]{0,1:T(2,128)S(1)}, s32[64,2]{0,1:T(2,128)}, u32[]{:S(2)}) copy-start(s32[64,2]{0,1:T(2,128)} %param.11) | copy-start | bytes 1540
  8.6 123.0 %copy-start.4 = (f32[16]{0:T(128)S(1)}, f32[16]{0:T(128)}, u32[]{:S(2)}) copy-start(f32[16]{0:T(128)} %occ_ref.1) | copy-start | bytes 196
  8.6 123.0 %copy-start.5 = (s32[16]{0:T(128)S(1)}, s32[16]{0:T(128)}, u32[]{:S(2)}) copy-start(s32[16]{0:T(128)} %len_ref.1) | copy-start | bytes 196
  8.6 86.0 %all-to-all-start = ((bf16[64,12,8,256]{3,2,1,0:T(8,128)(2,1)}), bf16[64,12,8,256]{3,2,1,0:T(8,128)(2,1)}, u32[]{:S(2)}, u32[]{:S(2)}) async-start(bf16[64,12,8,256]{3,2,1,0:T(8,128)(2,1)} %get-tuple-element.18), calls=%async_computation | async-start | bytes 6291456 | tf_op jit(solution)/shard_map/all_to_all | solution.py:313
  20.9 75.3 %collective-permute-start.1 = (bf16[4,256,256]{2,1,0:T(8,128)(2,1)}, bf16[4,256,256]{2,1,0:T(8,128)(2,1)}, u32[]{:S(2)}, u32[]{:S(2)}) collective-permute-start(bf16[4,256,256]{2,1,0:T(8,128)(2,1)} %refs_0_), channel_id=1, source_target_pairs={{2,0},{3,1},{0,2},{1,3},{6,4},{7,5},{4,6},{5,7},{10,8},{11,9},{8,1... | collective-permute-start | bytes 1572872 | tf_op jit(solution)/shard_map/ppermute | solution.py:304
  24.1 72.0 %collective-permute-start = (bf16[4,256,256]{2,1,0:T(8,128)(2,1)}, bf16[4,256,256]{2,1,0:T(8,128)(2,1)}, u32[]{:S(2)}, u32[]{:S(2)}) collective-permute-start(bf16[4,256,256]{2,1,0:T(8,128)(2,1)} %refs_0_), channel_id=1, source_target_pairs={{1,0},{2,1},{3,2},{0,3},{5,4},{6,5},{7,6},{4,7},{9,8},{10,9},{11,1... | collective-permute-start | bytes 1572872 | tf_op jit(solution)/shard_map/ppermute | solution.py:304
  25.2 70.9 %collective-permute-start.2 = (bf16[4,256,256]{2,1,0:T(8,128)(2,1)}, bf16[4,256,256]{2,1,0:T(8,128)(2,1)}, u32[]{:S(2)}, u32[]{:S(2)}) collective-permute-start(bf16[4,256,256]{2,1,0:T(8,128)(2,1)} %refs_0_), channel_id=1, source_target_pairs={{3,0},{0,1},{1,2},{2,3},{7,4},{4,5},{5,6},{6,7},{11,8},{8,9},{9,10... | collective-permute-start | bytes 1572872 | tf_op jit(solution)/shard_map/ppermute | solution.py:304
  94.5 53.3 %collective-permute-start.3 = (bf16[64,12,8,256]{3,2,1,0:T(8,128)(2,1)}, bf16[64,12,8,256]{3,2,1,0:T(8,128)(2,1)S(1)}, u32[]{:S(2)}, u32[]{:S(2)}) collective-permute-start(bf16[64,12,8,256]{3,2,1,0:T(8,128)(2,1)} %all-to-all-done.refs_0_), channel_id=1, source_target_pairs={{0,1},{1,0},{2,3},{3,2},{4,7},{5,6},{6,5},{7,4},{8,9},{9,8},{10,11... | collective-permute-start | bytes 9437192 | tf_op jit(solution)/shard_map/ppermute | solution.py:28
  131.2 16.6 %collective-permute-start.4 = (bf16[64,4,8,256]{3,2,1,0:T(8,128)(2,1)}, bf16[64,4,8,256]{3,2,1,0:T(8,128)(2,1)}, u32[]{:S(2)}, u32[]{:S(2)}) collective-permute-start(bf16[64,4,8,256]{3,2,1,0:T(8,128)(2,1)} %all_to_all.10.refs_1_), channel_id=1, source_target_pairs={{0,1},{1,0},{2,3},{3,2},{4,7},{5,6},{6,5},{7,4},{8,9},{9,8},{10,11... | collective-permute-start | bytes 3145736 | tf_op jit(solution)/shard_map/ppermute | solution.py:28
  131.6 1.6 copy-start
  152.5 24.9 %collective-permute-start.7 = (s16[6,272,256]{2,1,0:T(8,128)(2,1)S(1)}, s16[6,272,256]{2,1,0:T(8,128)(2,1)S(1)}, u32[]{:S(2)}, u32[]{:S(2)}) collective-permute-start(s16[6,272,256]{2,1,0:T(8,128)(2,1)S(1)} %shard_map.83), channel_id=1, source_target_pairs={{0,3},{1,2},{2,1},{3,0},{4,5},{5,4},{6,7},{7,6},{8,11},{9,10},{10,... | collective-permute-start | bytes 2506760 | tf_op jit(solution)/shard_map/ppermute | solution.py:28
  159.4 20.4 %collective-permute-start.6 = (s16[5,272,256]{2,1,0:T(8,128)(2,1)S(1)}, s16[5,272,256]{2,1,0:T(8,128)(2,1)S(1)}, u32[]{:S(2)}, u32[]{:S(2)}) collective-permute-start(s16[5,272,256]{2,1,0:T(8,128)(2,1)S(1)} %shard_map.82), channel_id=1, source_target_pairs={{0,3},{1,2},{2,1},{3,0},{4,5},{5,4},{6,7},{7,6},{8,11},{9,10},{10,... | collective-permute-start | bytes 2088968 | tf_op jit(solution)/shard_map/ppermute | solution.py:28
  164.4 13.0 %copy-start.1 = (bf16[16,256,256]{2,1,0:T(8,128)(2,1)S(1)}, bf16[16,256,256]{2,1,0:T(8,128)(2,1)}, u32[]{:S(2)}) copy-start(bf16[16,256,256]{2,1,0:T(8,128)(2,1)} %amp_ref.5) | copy-start | bytes 6291460
  164.4 17.8 %collective-permute-start.5 = (s16[5,272,256]{2,1,0:T(8,128)(2,1)S(1)}, s16[5,272,256]{2,1,0:T(8,128)(2,1)S(1)}, u32[]{:S(2)}, u32[]{:S(2)}) collective-permute-start(s16[5,272,256]{2,1,0:T(8,128)(2,1)S(1)} %shard_map.81), channel_id=1, source_target_pairs={{0,3},{1,2},{2,1},{3,0},{4,5},{5,4},{6,7},{7,6},{8,11},{9,10},{10,... | collective-permute-start | bytes 2088968 | tf_op jit(solution)/shard_map/ppermute | solution.py:28

commit v3 on v2

--- a/solution.py
+++ b/solution.py
@@ -10,7 +10,9 @@
 BOTH = ("orb", "pair")
 SPLITS = ((0, 12), (12, 16))
 VMEM = 24 * 2**20
-ARRANGE = 8
+WIDE = 58 * 2**20
+PIECES = 8
+PER = 4
 STEPS = 32767.0
 TAIL = 16
 
@@ -28,46 +30,69 @@
     return lax.ppermute(x, BOTH, pairs)
 
 
-def arrange_kernel(move_ref, x_ref, *out_refs):
-    aux, rows, dom = x_ref.shape
+def arrange_kernel(x_ref, *refs):
+    n = len(SPLITS)
+    out_refs, x, outs, sems, out_sems = refs[:n], refs[n], refs[n + 1 : -2], refs[-2], refs[-1]
+    aux, occ, dom = x.shape
     group = SPLITS[-1][1]
-    for g in range(rows // group):
-        block = x_ref[:, g * group : (g + 1) * group, :].reshape(aux * group, dom)
-        moved = jnp.dot(move_ref[...], block, preferred_element_type=jnp.float32)
-        moved = moved.astype(x_ref.dtype).reshape(group, aux, dom)
-        for (lo, hi), out_ref in zip(SPLITS, out_refs):
-            out_ref[g] = moved[lo:hi]
+    size = aux * group
+    each = occ // group // PIECES
+    loads = [
+        pltpu.make_async_copy(
+            x_ref.at[:, k * each * group : (k + 1) * each * group],
+            x.at[:, k * each * group : (k + 1) * each * group],
+            sems.at[k],
+        )
+        for k in range(PIECES)
+    ]
+    for c in loads:
+        c.start()
+    new = lax.broadcasted_iota(jnp.int32, (size, size), 0)
+    old = lax.broadcasted_iota(jnp.int32, (size, size), 1)
+    move = jnp.where((new % aux) * group + new // aux == old, 1.0, 0.0).astype(x.dtype)
+    stores = []
+    for k in range(PIECES):
+        loads[k].wait()
+        for g in range(k * each, (k + 1) * each):
+            block = x[:, g * group : (g + 1) * group, :].reshape(size, dom)
+            moved = jnp.dot(move, block, preferred_element_type=jnp.float32)
+            moved = moved.astype(x.dtype).reshape(group, aux, dom)
+            for (lo, hi), out in zip(SPLITS, outs):
+                out[g] = moved[lo:hi]
+        for c in range(n):
+            store = pltpu.make_async_copy(
+                outs[c].at[k * each : (k + 1) * each],
+                out_refs[c].at[k * each : (k + 1) * each],
+                out_sems.at[c, k],
+            )
+            store.start()
+            stores.append(store)
+    for c in stores:
+        c.wait()
 
 
 def arrange(integrals, orbs):
     aux, occ, dom = integrals.shape
-    group = occ // orbs
-    size = aux * group
-    new = jnp.arange(size, dtype=jnp.int32)
-    source = (new % aux) * group + new // aux
-    move = (source[:, None] == new[None, :]).astype(integrals.dtype)
+    size = aux * (occ // orbs)
+    shapes = [(orbs, hi - lo, aux, dom) for lo, hi in SPLITS]
     return pl.pallas_call(
         arrange_kernel,
-        grid=(orbs // ARRANGE,),
-        in_specs=[
-            pl.BlockSpec((size, size), lambda g: (0, 0)),
-            pl.BlockSpec((aux, ARRANGE * group, dom), lambda g: (0, g, 0)),
+        in_specs=[pl.BlockSpec(memory_space=pl.ANY)],
+        out_specs=[pl.BlockSpec(memory_space=pl.ANY)] * len(shapes),
+        out_shape=[jax.ShapeDtypeStruct(v, integrals.dtype) for v in shapes],
+        scratch_shapes=[pltpu.VMEM(integrals.shape, integrals.dtype)]
+        + [pltpu.VMEM(v, integrals.dtype) for v in shapes]
+        + [
+            pltpu.SemaphoreType.DMA((PIECES,)),
+            pltpu.SemaphoreType.DMA((len(shapes), PIECES)),
         ],
-        out_specs=[
-            pl.BlockSpec((ARRANGE, hi - lo, aux, dom), lambda g: (g, 0, 0, 0))
-            for lo, hi in SPLITS
-        ],
-        out_shape=[
-            jax.ShapeDtypeStruct((orbs, hi - lo, aux, dom), integrals.dtype)
-            for lo, hi in SPLITS
-        ],
-        compiler_params=pltpu.CompilerParams(vmem_limit_bytes=VMEM),
+        compiler_params=pltpu.CompilerParams(vmem_limit_bytes=WIDE),
         cost_estimate=pl.CostEstimate(
             flops=2 * orbs * size * size * dom,
             bytes_accessed=4 * aux * occ * dom,
             transcendentals=0,
         ),
-    )(move, integrals)
+    )(integrals)
 
 
 def load_blocks(parts, held, sems):
@@ -93,22 +118,22 @@
     return mantissa.astype(jnp.float32) * jnp.exp2(power.astype(jnp.float32))
 
 
-def encode(total, out_ref):
+def encode(total, out_ref, q):
     dom = total.shape[0]
     top = jnp.maximum(jnp.max(jnp.abs(total), axis=0, keepdims=True), 1e-30)
     power = jnp.floor(jnp.log2(top)).astype(jnp.int32) - 13
     mantissa = (top * jnp.exp2(-power.astype(jnp.float32))).astype(jnp.int32) + 1
     scale = STEPS / column_tops(mantissa, power)
-    out_ref[0, :dom, :] = jnp.round(total * scale).astype(jnp.int32).astype(jnp.int16)
+    out_ref[q, :dom, :] = jnp.round(total * scale).astype(jnp.int32).astype(jnp.int16)
     rows = lax.broadcasted_iota(jnp.int32, (TAIL, total.shape[1]), 0)
-    out_ref[0, dom:, :] = jnp.where(rows == 0, mantissa, power).astype(jnp.int16)
-
-
-def decode(code_ref):
+    out_ref[q, dom:, :] = jnp.where(rows == 0, mantissa, power).astype(jnp.int16)
+
+
+def decode(code_ref, q):
     dom = code_ref.shape[-1]
-    tail = code_ref[0, dom:, :].astype(jnp.int32)
+    tail = code_ref[q, dom:, :].astype(jnp.int32)
     step = column_tops(tail[0:1], tail[1:2]) * (1.0 / STEPS)
-    return code_ref[0, :dom, :].astype(jnp.float32) * step
+    return code_ref[q, :dom, :].astype(jnp.float32) * step
 
 
 def sums_kernel(rows, added, coded, pairs_ref, begin_ref, *refs):
@@ -126,24 +151,26 @@
         for c in copies:
             c.wait()
 
-    bases = iter(base_refs)
-    for k, (first, has) in enumerate(zip(rows, added)):
-        row = begin_ref[k] + first + p
-        total = block_sum(held, pairs_ref[2 * row], pairs_ref[2 * row + 1])
-        if has:
-            total += next(bases)[0]
-        if coded:
-            encode(total, out_refs[k])
-        else:
-            out_refs[k][0] = total
-
-
-def pair_sums(parts, bases, pairs, begins, firsts, count, coded=False):
+    per = out_refs[0].shape[0]
+    for q in range(per):
+        bases = iter(base_refs)
+        for k, (first, has) in enumerate(zip(rows, added)):
+            row = begin_ref[k] + first + p * per + q
+            total = block_sum(held, pairs_ref[2 * row], pairs_ref[2 * row + 1])
+            if has:
+                total += next(bases)[q]
+            if coded:
+                encode(total, out_refs[k], q)
+            else:
+                out_refs[k][q] = total
+
+
+def pair_sums(parts, bases, pairs, begins, firsts, count, coded=False, per=PER):
     src, _, aux, dom = parts[0].shape
     orbs = SPLITS[-1][1]
     added = tuple(b is not None for b in bases)
     in_specs = [pl.BlockSpec(memory_space=pl.ANY)] * len(parts) + [
-        pl.BlockSpec((1, dom, dom), lambda p, *_, first=first: (p + first, 0, 0))
+        pl.BlockSpec((per, dom, dom), lambda p, *_, first=first: (p + first // per, 0, 0))
         for first, has in zip(firsts, added)
         if has
     ]
@@ -156,9 +183,9 @@
         functools.partial(sums_kernel, tuple(firsts), added, coded),
         grid_spec=pltpu.PrefetchScalarGridSpec(
             num_scalar_prefetch=2,
-            grid=(count,),
+            grid=(count // per,),
             in_specs=in_specs,
-            out_specs=[pl.BlockSpec((1,) + shape.shape[1:], lambda p, *_: (p, 0, 0))]
+            out_specs=[pl.BlockSpec((per,) + shape.shape[1:], lambda p, *_: (p, 0, 0))]
             * len(begins),
             scratch_shapes=[
                 pltpu.VMEM((len(parts) // len(SPLITS), src, orbs, aux, dom), jnp.bfloat16),
@@ -195,40 +222,42 @@
         for c in copies:
             c.wait()
 
-    row = begin_ref[0] + p
-    i = pairs_ref[2 * row]
-    j = pairs_ref[2 * row + 1]
-    energies = occ_ref[i] + occ_ref[j]
-    old = amp_ref[0]
-    fock_i = fock[slot_ref[i]]
-    fock_j = fock[slot_ref[j]]
-    total = jnp.dot(fock_i, old, preferred_element_type=jnp.float32)
-    total += lax.dot_general(
-        old, fock_j, (((1,), (1,)), ((), ())), preferred_element_type=jnp.float32
-    )
-    base_ref[0] = total - energies * old.astype(jnp.float32)
-    rows = lax.broadcasted_iota(jnp.int32, (dom, dom), 0)
-    columns = lax.broadcasted_iota(jnp.int32, (dom, dom), 1)
-    eye = rows == columns
-    diag_i = jnp.sum(
-        jnp.where(eye, fock_i.astype(jnp.float32), 0.0), axis=1, keepdims=True
-    )
-    diag_j = jnp.sum(
-        jnp.where(eye, fock_j.astype(jnp.float32), 0.0), axis=0, keepdims=True
-    )
-    inside = (rows < len_ref[i]) & (columns < len_ref[j])
-    inv_ref[0] = jnp.where(inside, 1.0 / (diag_i + diag_j - energies), 0.0)
+    per = amp_ref.shape[0]
+    for q in range(per):
+        row = begin_ref[0] + p * per + q
+        i = pairs_ref[2 * row]
+        j = pairs_ref[2 * row + 1]
+        energies = occ_ref[i] + occ_ref[j]
+        old = amp_ref[q]
+        fock_i = fock[slot_ref[i]]
+        fock_j = fock[slot_ref[j]]
+        total = jnp.dot(fock_i, old, preferred_element_type=jnp.float32)
+        total += lax.dot_general(
+            old, fock_j, (((1,), (1,)), ((), ())), preferred_element_type=jnp.float32
+        )
+        base_ref[q] = total - energies * old.astype(jnp.float32)
+        rows = lax.broadcasted_iota(jnp.int32, (dom, dom), 0)
+        columns = lax.broadcasted_iota(jnp.int32, (dom, dom), 1)
+        eye = rows == columns
+        diag_i = jnp.sum(
+            jnp.where(eye, fock_i.astype(jnp.float32), 0.0), axis=1, keepdims=True
+        )
+        diag_j = jnp.sum(
+            jnp.where(eye, fock_j.astype(jnp.float32), 0.0), axis=0, keepdims=True
+        )
+        inside = (rows < len_ref[i]) & (columns < len_ref[j])
+        inv_ref[q] = jnp.where(inside, 1.0 / (diag_i + diag_j - energies), 0.0)
 
 
 def fock_terms(focks, amplitudes, pairs, begin, slot, occ, lengths):
     count, dom, _ = amplitudes.shape
-    one = pl.BlockSpec((1, dom, dom), lambda p, *_: (p, 0, 0))
+    one = pl.BlockSpec((PER, dom, dom), lambda p, *_: (p, 0, 0))
     shape = jax.ShapeDtypeStruct((count, dom, dom), jnp.float32)
     return pl.pallas_call(
         fock_kernel,
         grid_spec=pltpu.PrefetchScalarGridSpec(
             num_scalar_prefetch=5,
-            grid=(count,),
+            grid=(count // PER,),
             in_specs=[pl.BlockSpec(memory_space=pl.ANY)] * 4 + [one],
             out_specs=[one, one],
             scratch_shapes=[
@@ -248,26 +277,27 @@
 
 def finish_kernel(own_ref, other_ref, amp_ref, inv_ref, *refs):
     resid_ref, new_ref = refs[-2:]
-    inv = inv_ref[0]
-    inside = inv != 0.0
-    resid = jnp.where(inside, own_ref[0] + decode(other_ref), 0.0)
-    old = amp_ref[0].astype(jnp.float32)
-    resid_ref[0] = resid.astype(resid_ref.dtype)
-    new_ref[0] = jnp.where(inside, old - resid * inv, 0.0).astype(new_ref.dtype)
+    for q in range(own_ref.shape[0]):
+        inv = inv_ref[q]
+        inside = inv != 0.0
+        resid = jnp.where(inside, own_ref[q] + decode(other_ref, q), 0.0)
+        old = amp_ref[q].astype(jnp.float32)
+        resid_ref[q] = resid.astype(resid_ref.dtype)
+        new_ref[q] = jnp.where(inside, old - resid * inv, 0.0).astype(new_ref.dtype)
 
 
 def finish(own, other, amplitudes, inv, first, held):
     total, dom, _ = amplitudes.shape
     count = other.shape[0]
-    shifted = pl.BlockSpec((1, dom, dom), lambda p: (p + first, 0, 0))
+    shifted = pl.BlockSpec((PER, dom, dom), lambda p: (p + first // PER, 0, 0))
     shape = jax.ShapeDtypeStruct((total, dom, dom), jnp.bfloat16)
     extra = [] if held is None else list(held)
     return pl.pallas_call(
         finish_kernel,
-        grid=(count,),
+        grid=(count // PER,),
         in_specs=[
             shifted,
-            pl.BlockSpec((1,) + other.shape[1:], lambda p: (p, 0, 0)),
+            pl.BlockSpec((PER,) + other.shape[1:], lambda p: (p, 0, 0)),
             shifted,
             shifted,
         ]
@@ -284,7 +314,7 @@
     )(own, other, amplitudes, inv, *extra)
 
 
-CHUNKS = ((0, 6), (6, 11), (11, 16))
+CHUNKS = ((0, 4), (4, 8), (8, 12), (12, 16))
 
 
 def local(orbs, ys, integrals, fock_blocks, occ_energy, dom_len, amplitudes, pair_list):
@@ -310,20 +340,21 @@
     for c, block in enumerate(blocks):
         if c == len(SPLITS) - 1:
             block, *focks = lax.optimization_barrier([block] + focks)
+            base, inv = fock_terms(
+                focks, amplitudes, pairs, mine.reshape(1), slot, occ_energy, dom_len
+            )
         got = lax.all_to_all(block, "orb", split_axis=0, concat_axis=0, tiled=True)
+        if c == len(SPLITS) - 1:
+            got, base, inv = lax.optimization_barrier((got, base, inv))
         near.append(got)
         far.append(exchange_with(got, gather_mate, orbs, ys))
 
-    base, inv = fock_terms(
-        focks, amplitudes, pairs, mine.reshape(1), slot, occ_energy, dom_len
-    )
-    after, base, inv = lax.optimization_barrier((near[0], base, inv))
-    (theirs_near,) = pair_sums([after] + near[1:], [None], pairs, [theirs], [0], owned)
+    theirs_near, own = pair_sums(near, [None, base], pairs, [theirs, mine], [0, 0], owned)
     others = []
     for lo, hi in CHUNKS:
         (sums,) = pair_sums(far, [theirs_near], pairs, [theirs], [lo], hi - lo, True)
         others.append(exchange_with(sums, sum_mate, orbs, ys))
-    (own,) = pair_sums(near + far, [base], pairs, [mine], [0], owned)
+    (own,) = pair_sums(far, [own], pairs, [mine], [0], owned)
     held = None
     for (lo, _), other in zip(CHUNKS, others):
         held = finish(own, other, amplitudes, inv, lo, held)

time: 185 us -> 177 us (0.957)
  blocking collectives: 35.1 us -> 0 us
  waiting for transfers between devices: 68.4 us -> 95.1 us
  Pallas kernels: 49.7 us -> 39.4 us
  starting transfers between devices: 25.4 us -> 32.7 us
  local copies, waits for them, and re-layouts: 4.99 us -> 7.99 us
    all_to_all x1 -> x0, blocking collectives: 35.1 us -> none  [local(): got = lax.all_to_all(block, 'orb', split_axis=0, concat_axis=0, tiled=True)]
    all_to_all x1 -> x2, waiting for transfers between devices: 68.4 us -> 86.5 us  [local(): got = lax.all_to_all(block, 'orb', split_axis=0, concat_axis=0, tiled=True)]
    ppermute x5 -> x6, waiting for transfers between devices: 0.01 us -> 8.56 us  [exchange_with(): return lax.ppermute(x, BOTH, pairs)]
    pallas_call x5 -> x6, Pallas kernels: 31.4 us -> 24.9 us  [pair_sums(): pl.pallas_call(functools.partial(sums_kernel, tuple(firsts), added, coded...]
    all_to_all x1 -> x2, starting transfers between devices: 12.3 us -> 18.7 us  [local(): got = lax.all_to_all(block, 'orb', split_axis=0, concat_axis=0, tiled=True)]
    unnamed x15 -> x19, local copies, waits for them, and re-layouts: 4.85 us -> 7.86 us
    pallas_call x4 -> x5, Pallas kernels: 11.8 us -> 9.71 us  [the longest x4 5.39 us: finish(): pl.pallas_call(finish_kernel, grid=(count // PER,), in_specs=[shifted, pl...]
    pallas_call x1, Pallas kernels: 6.63 us -> 4.71 us  [fock_terms(): pl.pallas_call(fock_kernel, grid_spec=pltpu.PrefetchScalarGridSpec(num_sc...]
  transfers between devices with their start and end apart: 9 -> 11, of which waited for: 1 -> 5; matrix products, arithmetic and copies ran while one was open for 0% -> 0% of each run, Pallas kernels for 21% -> 17%
where the time goes in v3:
time: 177 us; the launch traced here: 176 us
  waiting for transfers between devices  95.1 us (54%)
  Pallas kernels  39.4 us (22%)
  starting transfers between devices  32.7 us (18%)
  local copies, waits for them, and re-layouts  7.99 us (5%)
    all_to_all x2, waiting for transfers between devices, local(): got = lax.all_to_all(block, 'orb', split_axis=0, concat_axis=0, tiled=True)  86.5 us
    pallas_call x6, Pallas kernels, pair_sums(): pl.pallas_call(functools.partial(sums_kernel, tuple(firsts), added, coded...  24.9 us
    all_to_all x2, starting transfers between devices, local(): got = lax.all_to_all(block, 'orb', split_axis=0, concat_axis=0, tiled=True)  18.7 us
    ppermute x6, starting transfers between devices, exchange_with(): return lax.ppermute(x, BOTH, pairs)  8.7 us
    ppermute x6, waiting for transfers between devices, exchange_with(): return lax.ppermute(x, BOTH, pairs)  8.56 us
    unnamed x19, local copies, waits for them, and re-layouts  7.86 us
    pallas_call x4, Pallas kernels, finish(): pl.pallas_call(finish_kernel, grid=(count // PER,), in_specs=[shifted, pl...  5.39 us
    ppermute x3, starting transfers between devices, local(): lax.ppermute(fock_blocks, 'pair', [((s + shift) % ys, s) for s in range(y...  5.3 us
  transfers between devices with their start and end apart: 11, of which 5 were waited for; matrix products, arithmetic and copies ran while one was open for 0% of the time, Pallas kernels for 17%

profile of v3, /device:TPU:2, one launch (start us, length us, event | category | flops | bytes accessed | tf_op | source)
XLA Modules:
  0.0 176.0 jit_solution(3762940718511410369)
XLA Ops:
  0.6 4.3 %shard_map.77 = (bf16[64,12,8,256]{3,2,1,0:T(8,128)(2,1)}, bf16[64,4,8,256]{3,2,1,0:T(8,128)(2,1)}) custom-call(bf16[8,1024,256]{2,1,0:T(8,128)(2,1)} %x_ref.1), custom_call_target="tpu_custom_call" | custom-call | flops 536870912 | bytes 8388608 | tf_op jit(solution)/shard_map/pallas_call | solution.py:78
  5.0 0.0 copy-start.8
  5.0 0.0 copy-start.6
  5.0 0.0 copy-start.7
  5.0 12.3 %all-to-all-start = ((bf16[64,12,8,256]{3,2,1,0:T(8,128)(2,1)}), bf16[64,12,8,256]{3,2,1,0:T(8,128)(2,1)}, u32[]{:S(2)}, u32[]{:S(2)}) async-start(bf16[64,12,8,256]{3,2,1,0:T(8,128)(2,1)} %get-tuple-element.22), calls=%async_computation | async-start | bytes 6291456 | tf_op jit(solution)/shard_map/all_to_all | solution.py:346
  17.3 3.3 %collective-permute-start.2 = (bf16[4,256,256]{2,1,0:T(8,128)(2,1)}, bf16[4,256,256]{2,1,0:T(8,128)(2,1)}, u32[]{:S(2)}, u32[]{:S(2)}) collective-permute-start(bf16[4,256,256]{2,1,0:T(8,128)(2,1)} %refs_0_), channel_id=1, source_target_pairs={{2,0},{3,1},{0,2},{1,3},{6,4},{7,5},{4,6},{5,7},{10,8},{11,9},{8,1... | collective-permute-start | bytes 1572872 | tf_op jit(solution)/shard_map/ppermute | solution.py:334
  20.6 1.1 collective-permute-start.1
  21.7 1.0 collective-permute-start.3
  22.6 68.4 %all-to-all-done.refs_0_ = bf16[64,12,8,256]{3,2,1,0:T(8,128)(2,1)} async-done(((bf16[64,12,8,256]{3,2,1,0:T(8,128)(2,1)}), bf16[64,12,8,256]{3,2,1,0:T(8,128)(2,1)}, u32[]{:S(2)}, u32[]{:S(2)}) %all-to-all-start) | async-done | bytes 3145760 | tf_op jit(solution)/shard_map/all_to_all | solution.py:346
  91.0 1.6 collective-permute-start
  92.6 0.0 collective-permute-done.2.refs_2_
  92.6 0.0 collective-permute-done.1.refs_1_
  92.6 0.0 collective-permute-done.3.refs_3_
  92.6 6.4 %all-to-all-start.1 = ((bf16[64,4,8,256]{3,2,1,0:T(8,128)(2,1)}), bf16[64,4,8,256]{3,2,1,0:T(8,128)(2,1)}, u32[]{:S(2)}, u32[]{:S(2)}) async-start(bf16[64,4,8,256]{3,2,1,0:T(8,128)(2,1)} %get-tuple-element.24), calls=%async_computation.1 | async-start | bytes 2097152 | tf_op jit(solution)/shard_map/all_to_all | solution.py:346
  99.0 0.0 copy-done.8
  99.0 0.1 copy.15
  99.1 0.1 reshape.8.pairs_ref
  99.2 0.0 copy-done.6
  99.2 0.0 copy-done.7
  99.2 0.0 copy-start.2
  99.3 1.6 copy-done.2
  100.8 4.7 %shard_map.78 = (f32[16,256,256]{2,1,0:T(8,128)S(1)}, f32[16,256,256]{2,1,0:T(8,128)S(1)}) custom-call(s32[128]{0:T(128)S(1)} %reshape.8.pairs_ref, s32[1]{0:T(128)} %bitcast.begin_ref, s32[16]{0:T(128)S(1)} %fusion.slot_ref, f32[16]{0:T(128)S(1)} %copy-done.6, s32[16]{0:T(128)S(1)} %copy-done.7, bf16[4,256,256]{2,1,0:T(8,128)(2,1)} %refs_0_, ...), custom_call_target="tpu_custom_call" | custom-call | flops 1073741824 | bytes 12582912 | tf_op jit(solution)/shard_map/pallas_call | solution.py:256
  105.5 0.0 copy-start
  105.6 1.9 %copy-done = f32[16,256,256]{2,1,0:T(8,128)} copy-done((f32[16,256,256]{2,1,0:T(8,128)}, f32[16,256,256]{2,1,0:T(8,128)S(1)}, u32[]{:S(2)}) %copy-start) | copy-done | bytes 4194328
  107.5 0.0 copy-start.4
  107.5 2.0 %copy-done.4 = f32[16,256,256]{2,1,0:T(8,128)} copy-done((f32[16,256,256]{2,1,0:T(8,128)}, f32[16,256,256]{2,1,0:T(8,128)S(1)}, u32[]{:S(2)}) %copy-start.4) | copy-done | bytes 4194328
  109.5 18.1 %all-to-all-done.1.refs_1_ = bf16[64,4,8,256]{3,2,1,0:T(8,128)(2,1)} async-done(((bf16[64,4,8,256]{3,2,1,0:T(8,128)(2,1)}), bf16[64,4,8,256]{3,2,1,0:T(8,128)(2,1)}, u32[]{:S(2)}, u32[]{:S(2)}) %all-to-all-start.1) | async-done | bytes 1048608 | tf_op jit(solution)/shard_map/all_to_all | solution.py:346
  127.7 0.1 collective-permute-start.4
  127.8 0.1 pad_add_fusion.begin_ref
  127.9 0.0 copy-start.5
  127.9 2.2 %copy-done.5 = f32[16,256,256]{2,1,0:T(8,128)S(1)} copy-done((f32[16,256,256]{2,1,0:T(8,128)S(1)}, f32[16,256,256]{2,1,0:T(8,128)}, u32[]{:S(2)}) %copy-start.5) | copy-done | bytes 4194328
  130.1 6.7 %shard_map.79 = (f32[16,256,256]{2,1,0:T(8,128)S(1)}, f32[16,256,256]{2,1,0:T(8,128)S(1)}) custom-call(s32[128]{0:T(128)S(1)} %reshape.8.pairs_ref, s32[2]{0:T(128)S(1)} %pad_add_fusion.begin_ref, bf16[64,12,8,256]{3,2,1,0:T(8,128)(2,1)} %all-to-all-done.refs_0_, bf16[64,4,8,256]{3,2,1,0:T(8,128)(2,1)} %all-to-all-done.1.refs_1_, f32[16,256,256]{2,1,0:T(8,128)S(1)} %copy-done.5), custom_call_target="tpu_custom_call" | custom-call | flops 2147483648 | bytes 16777216 | tf_op jit(solution)/shard_map/pallas_call | solution.py:182
  136.7 6.1 %collective-permute-done.4.refs_1_ = bf16[64,4,8,256]{3,2,1,0:T(8,128)(2,1)} collective-permute-done((bf16[64,4,8,256]{3,2,1,0:T(8,128)(2,1)}, bf16[64,4,8,256]{3,2,1,0:T(8,128)(2,1)}, u32[]{:S(2)}, u32[]{:S(2)}) %collective-permute-start.4) | collective-permute-done | bytes 1048608 | tf_op jit(solution)/shard_map/ppermute | solution.py:30
  142.8 0.0 collective-permute-done.refs_0_
  142.8 3.1 %shard_map.82 = s16[4,272,256]{2,1,0:T(8,128)(2,1)S(1)} custom-call(s32[128]{0:T(128)S(1)} %reshape.8.pairs_ref, s32[1]{0:T(128)} %bitcast.1.begin_ref, bf16[64,12,8,256]{3,2,1,0:T(8,128)(2,1)S(1)} %collective-permute-done.refs_0_, bf16[64,4,8,256]{3,2,1,0:T(8,128)(2,1)} %collective-permute-done.4.refs_1_, f32[16,256,256]{2,1,0:T(8,128)S(1)} %get-tuple-element.34.refs_2_), custom_call_target="tpu_custom_call" | custom-call | flops 268435456 | bytes 6291456 | tf_op jit(solution)/shard_map/pallas_call | solution.py:182
  145.9 1.6 collective-permute-start.6
  147.5 3.1 %shard_map.83 = s16[4,272,256]{2,1,0:T(8,128)(2,1)S(1)} custom-call(s32[128]{0:T(128)S(1)} %reshape.8.pairs_ref, s32[1]{0:T(128)} %bitcast.1.begin_ref, bf16[64,12,8,256]{3,2,1,0:T(8,128)(2,1)S(1)} %collective-permute-done.refs_0_, bf16[64,4,8,256]{3,2,1,0:T(8,128)(2,1)} %collective-permute-done.4.refs_1_, f32[16,256,256]{2,1,0:T(8,128)S(1)} %get-tuple-element.34.refs_2_), custom_call_target="tpu_custom_call" | custom-call | flops 268435456 | bytes 6291456 | tf_op jit(solution)/shard_map/pallas_call | solution.py:182
  150.6 1.8 %collective-permute-start.7 = (s16[4,272,256]{2,1,0:T(8,128)(2,1)S(1)}, s16[4,272,256]{2,1,0:T(8,128)(2,1)S(1)}, u32[]{:S(2)}, u32[]{:S(2)}) collective-permute-start(s16[4,272,256]{2,1,0:T(8,128)(2,1)S(1)} %shard_map.83), channel_id=1, source_target_pairs={{0,3},{1,2},{2,1},{3,0},{4,5},{5,4},{6,7},{7,6},{8,11},{9,10},{10,... | collective-permute-start | bytes 1671176 | tf_op jit(solution)/shard_map/ppermute | solution.py:30
  152.5 3.1 %shard_map.84 = s16[4,272,256]{2,1,0:T(8,128)(2,1)S(1)} custom-call(s32[128]{0:T(128)S(1)} %reshape.8.pairs_ref, s32[1]{0:T(128)} %bitcast.1.begin_ref, bf16[64,12,8,256]{3,2,1,0:T(8,128)(2,1)S(1)} %collective-permute-done.refs_0_, bf16[64,4,8,256]{3,2,1,0:T(8,128)(2,1)} %collective-permute-done.4.refs_1_, f32[16,256,256]{2,1,0:T(8,128)S(1)} %get-tuple-element.34.refs_2_), custom_call_target="tpu_custom_call" | custom-call | flops 268435456 | bytes 6291456 | tf_op jit(solution)/shard_map/pallas_call | solution.py:182
  155.6 1.7 collective-permute-start.8
  157.4 3.1 %shard_map.81 = s16[4,272,256]{2,1,0:T(8,128)(2,1)S(1)} custom-call(s32[128]{0:T(128)S(1)} %reshape.8.pairs_ref, s32[1]{0:T(128)} %bitcast.1.begin_ref, bf16[64,12,8,256]{3,2,1,0:T(8,128)(2,1)S(1)} %collective-permute-done.refs_0_, bf16[64,4,8,256]{3,2,1,0:T(8,128)(2,1)} %collective-permute-done.4.refs_1_, f32[16,256,256]{2,1,0:T(8,128)S(1)} %get-tuple-element.34.refs_2_), custom_call_target="tpu_custom_call" | custom-call | flops 268435456 | bytes 6291456 | tf_op jit(solution)/shard_map/pallas_call | solution.py:182
  160.5 1.8 %collective-permute-start.5 = (s16[4,272,256]{2,1,0:T(8,128)(2,1)S(1)}, s16[4,272,256]{2,1,0:T(8,128)(2,1)S(1)}, u32[]{:S(2)}, u32[]{:S(2)}) collective-permute-start(s16[4,272,256]{2,1,0:T(8,128)(2,1)S(1)} %shard_map.81), channel_id=1, source_target_pairs={{0,3},{1,2},{2,1},{3,0},{4,5},{5,4},{6,7},{7,6},{8,11},{9,10},{10,... | collective-permute-start | bytes 1671176 | tf_op jit(solution)/shard_map/ppermute | solution.py:30
  162.4 0.0 copy-start.1
  162.4 0.0 copy-start.3
  162.4 5.7 %shard_map.80.own_ref = f32[16,256,256]{2,1,0:T(8,128)S(1)} custom-call(s32[128]{0:T(128)S(1)} %reshape.8.pairs_ref, s32[1]{0:T(128)} %bitcast.begin_ref, bf16[64,12,8,256]{3,2,1,0:T(8,128)(2,1)S(1)} %collective-permute-done.refs_0_, bf16[64,4,8,256]{3,2,1,0:T(8,128)(2,1)} %collective-permute-done.4.refs_1_, f32[16,256,256]{2,1,0:T(8,128)S(1)} %get-tuple-element.33.refs_2_), custom_call_target="tpu_custom_call" | custom-call | flops 1073741824 | bytes 12582912 | tf_op jit(solution)/shard_map/pallas_call | solution.py:182
  168.1 0.6 collective-permute-done.8.other_ref
  168.7 0.0 copy-done.1
  168.7 0.0 copy-done.3
  168.7 1.3 shard_map.85
  170.0 0.0 collective-permute-done.7.other_ref
  170.0 1.3 shard_map.86
  171.4 0.0 collective-permute-done.6.other_ref
  171.4 1.3 shard_map.87
  172.7 1.9 %collective-permute-done.5.other_ref = s16[4,272,256]{2,1,0:T(8,128)(2,1)S(1)} collective-permute-done((s16[4,272,256]{2,1,0:T(8,128)(2,1)S(1)}, s16[4,272,256]{2,1,0:T(8,128)(2,1)S(1)}, u32[]{:S(2)}, u32[]{:S(2)}) %collective-permute-start.5) | collective-permute-done | bytes 557088 | tf_op jit(solution)/shard_map/ppermute | solution.py:30
  174.6 1.3 shard_map.88
  (1 shorter events, 0.0 us)
Async XLA Ops:
  5.0 94.0 %copy-start.8 = (s32[64,2]{0,1:T(2,128)S(1)}, s32[64,2]{0,1:T(2,128)}, u32[]{:S(2)}) copy-start(s32[64,2]{0,1:T(2,128)} %param.11) | copy-start | bytes 1540
  5.0 94.3 %copy-start.6 = (f32[16]{0:T(128)S(1)}, f32[16]{0:T(128)}, u32[]{:S(2)}) copy-start(f32[16]{0:T(128)} %occ_ref.1) | copy-start | bytes 196
  5.0 94.3 %copy-start.7 = (s32[16]{0:T(128)S(1)}, s32[16]{0:T(128)}, u32[]{:S(2)}) copy-start(s32[16]{0:T(128)} %len_ref.1) | copy-start | bytes 196
  5.0 86.0 %all-to-all-start = ((bf16[64,12,8,256]{3,2,1,0:T(8,128)(2,1)}), bf16[64,12,8,256]{3,2,1,0:T(8,128)(2,1)}, u32[]{:S(2)}, u32[]{:S(2)}) async-start(bf16[64,12,8,256]{3,2,1,0:T(8,128)(2,1)} %get-tuple-element.22), calls=%async_computation | async-start | bytes 6291456 | tf_op jit(solution)/shard_map/all_to_all | solution.py:346
  17.3 75.3 %collective-permute-start.2 = (bf16[4,256,256]{2,1,0:T(8,128)(2,1)}, bf16[4,256,256]{2,1,0:T(8,128)(2,1)}, u32[]{:S(2)}, u32[]{:S(2)}) collective-permute-start(bf16[4,256,256]{2,1,0:T(8,128)(2,1)} %refs_0_), channel_id=1, source_target_pairs={{2,0},{3,1},{0,2},{1,3},{6,4},{7,5},{4,6},{5,7},{10,8},{11,9},{8,1... | collective-permute-start | bytes 1572872 | tf_op jit(solution)/shard_map/ppermute | solution.py:334
  20.6 72.0 %collective-permute-start.1 = (bf16[4,256,256]{2,1,0:T(8,128)(2,1)}, bf16[4,256,256]{2,1,0:T(8,128)(2,1)}, u32[]{:S(2)}, u32[]{:S(2)}) collective-permute-start(bf16[4,256,256]{2,1,0:T(8,128)(2,1)} %refs_0_), channel_id=1, source_target_pairs={{1,0},{2,1},{3,2},{0,3},{5,4},{6,5},{7,6},{4,7},{9,8},{10,9},{11,1... | collective-permute-start | bytes 1572872 | tf_op jit(solution)/shard_map/ppermute | solution.py:334
  21.7 70.9 %collective-permute-start.3 = (bf16[4,256,256]{2,1,0:T(8,128)(2,1)}, bf16[4,256,256]{2,1,0:T(8,128)(2,1)}, u32[]{:S(2)}, u32[]{:S(2)}) collective-permute-start(bf16[4,256,256]{2,1,0:T(8,128)(2,1)} %refs_0_), channel_id=1, source_target_pairs={{3,0},{0,1},{1,2},{2,3},{7,4},{4,5},{5,6},{6,7},{11,8},{8,9},{9,10... | collective-permute-start | bytes 1572872 | tf_op jit(solution)/shard_map/ppermute | solution.py:334
  91.0 51.8 %collective-permute-start = (bf16[64,12,8,256]{3,2,1,0:T(8,128)(2,1)}, bf16[64,12,8,256]{3,2,1,0:T(8,128)(2,1)S(1)}, u32[]{:S(2)}, u32[]{:S(2)}) collective-permute-start(bf16[64,12,8,256]{3,2,1,0:T(8,128)(2,1)} %all-to-all-done.refs_0_), channel_id=1, source_target_pairs={{0,1},{1,0},{2,3},{3,2},{4,7},{5,6},{6,5},{7,4},{8,9},{9,8},{10,11... | collective-permute-start | bytes 9437192 | tf_op jit(solution)/shard_map/ppermute | solution.py:30
  92.6 35.1 %all-to-all-start.1 = ((bf16[64,4,8,256]{3,2,1,0:T(8,128)(2,1)}), bf16[64,4,8,256]{3,2,1,0:T(8,128)(2,1)}, u32[]{:S(2)}, u32[]{:S(2)}) async-start(bf16[64,4,8,256]{3,2,1,0:T(8,128)(2,1)} %get-tuple-element.24), calls=%async_computation.1 | async-start | bytes 2097152 | tf_op jit(solution)/shard_map/all_to_all | solution.py:346
  99.2 1.6 copy-start.2
  105.5 2.0 %copy-start = (f32[16,256,256]{2,1,0:T(8,128)}, f32[16,256,256]{2,1,0:T(8,128)S(1)}, u32[]{:S(2)}) copy-start(f32[16,256,256]{2,1,0:T(8,128)S(1)} %get-tuple-element.35.inv_ref) | copy-start | bytes 12582916
  107.5 2.0 %copy-start.4 = (f32[16,256,256]{2,1,0:T(8,128)}, f32[16,256,256]{2,1,0:T(8,128)S(1)}, u32[]{:S(2)}) copy-start(f32[16,256,256]{2,1,0:T(8,128)S(1)} %get-tuple-element.32.refs_2_) | copy-start | bytes 12582916
  127.7 15.1 %collective-permute-start.4 = (bf16[64,4,8,256]{3,2,1,0:T(8,128)(2,1)}, bf16[64,4,8,256]{3,2,1,0:T(8,128)(2,1)}, u32[]{:S(2)}, u32[]{:S(2)}) collective-permute-start(bf16[64,4,8,256]{3,2,1,0:T(8,128)(2,1)} %all-to-all-done.1.refs_1_), channel_id=1, source_target_pairs={{0,1},{1,0},{2,3},{3,2},{4,7},{5,6},{6,5},{7,4},{8,9},{9,8},{10,11... | collective-permute-start | bytes 3145736 | tf_op jit(solution)/shard_map/ppermute | solution.py:30
  127.9 2.2 %copy-start.5 = (f32[16,256,256]{2,1,0:T(8,128)S(1)}, f32[16,256,256]{2,1,0:T(8,128)}, u32[]{:S(2)}) copy-start(f32[16,256,256]{2,1,0:T(8,128)} %copy-done.4) | copy-start | bytes 12582916
  145.9 25.5 %collective-permute-start.6 = (s16[4,272,256]{2,1,0:T(8,128)(2,1)S(1)}, s16[4,272,256]{2,1,0:T(8,128)(2,1)S(1)}, u32[]{:S(2)}, u32[]{:S(2)}) collective-permute-start(s16[4,272,256]{2,1,0:T(8,128)(2,1)S(1)} %shard_map.82), channel_id=1, source_target_pairs={{0,3},{1,2},{2,1},{3,0},{4,5},{5,4},{6,7},{7,6},{8,11},{9,10},{10,... | collective-permute-start | bytes 1671176 | tf_op jit(solution)/shard_map/ppermute | solution.py:30
  150.6 19.4 %collective-permute-start.7 = (s16[4,272,256]{2,1,0:T(8,128)(2,1)S(1)}, s16[4,272,256]{2,1,0:T(8,128)(2,1)S(1)}, u32[]{:S(2)}, u32[]{:S(2)}) collective-permute-start(s16[4,272,256]{2,1,0:T(8,128)(2,1)S(1)} %shard_map.83), channel_id=1, source_target_pairs={{0,3},{1,2},{2,1},{3,0},{4,5},{5,4},{6,7},{7,6},{8,11},{9,10},{10,... | collective-permute-start | bytes 1671176 | tf_op jit(solution)/shard_map/ppermute | solution.py:30
  155.6 13.1 %collective-permute-start.8 = (s16[4,272,256]{2,1,0:T(8,128)(2,1)S(1)}, s16[4,272,256]{2,1,0:T(8,128)(2,1)S(1)}, u32[]{:S(2)}, u32[]{:S(2)}) collective-permute-start(s16[4,272,256]{2,1,0:T(8,128)(2,1)S(1)} %shard_map.84), channel_id=1, source_target_pairs={{0,3},{1,2},{2,1},{3,0},{4,5},{5,4},{6,7},{7,6},{8,11},{9,10},{10,... | collective-permute-start | bytes 1671176 | tf_op jit(solution)/shard_map/ppermute | solution.py:30
  160.5 14.1 %collective-permute-start.5 = (s16[4,272,256]{2,1,0:T(8,128)(2,1)S(1)}, s16[4,272,256]{2,1,0:T(8,128)(2,1)S(1)}, u32[]{:S(2)}, u32[]{:S(2)}) collective-permute-start(s16[4,272,256]{2,1,0:T(8,128)(2,1)S(1)} %shard_map.81), channel_id=1, source_target_pairs={{0,3},{1,2},{2,1},{3,0},{4,5},{5,4},{6,7},{7,6},{8,11},{9,10},{10,... | collective-permute-start | bytes 1671176 | tf_op jit(solution)/shard_map/ppermute | solution.py:30
  162.4 6.3 %copy-start.1 = (f32[16,256,256]{2,1,0:T(8,128)S(1)}, f32[16,256,256]{2,1,0:T(8,128)}, u32[]{:S(2)}) copy-start(f32[16,256,256]{2,1,0:T(8,128)} %copy-done) | copy-start | bytes 12582916
  162.4 6.3 %copy-start.3 = (bf16[16,256,256]{2,1,0:T(8,128)(2,1)S(1)}, bf16[16,256,256]{2,1,0:T(8,128)(2,1)}, u32[]{:S(2)}) copy-start(bf16[16,256,256]{2,1,0:T(8,128)(2,1)} %amp_ref.7) | copy-start | bytes 6291460

commit v4 on v3

--- a/solution.py
+++ b/solution.py
@@ -1,4 +1,5 @@
 import functools
+import math
 
 import jax
 import jax.numpy as jnp
@@ -11,7 +12,7 @@
 SPLITS = ((0, 12), (12, 16))
 VMEM = 24 * 2**20
 WIDE = 58 * 2**20
-PIECES = 8
+PIECES = 4
 PER = 4
 STEPS = 32767.0
 TAIL = 16
@@ -30,12 +31,9 @@
     return lax.ppermute(x, BOTH, pairs)
 
 
-def arrange_kernel(x_ref, *refs):
-    n = len(SPLITS)
-    out_refs, x, outs, sems, out_sems = refs[:n], refs[n], refs[n + 1 : -2], refs[-2], refs[-1]
+def arrange_kernel(lo, hi, x_ref, out_ref, x, out, sems, out_sems):
     aux, occ, dom = x.shape
     group = SPLITS[-1][1]
-    size = aux * group
     each = occ // group // PIECES
     loads = [
         pltpu.make_async_copy(
@@ -47,49 +45,46 @@
     ]
     for c in loads:
         c.start()
-    new = lax.broadcasted_iota(jnp.int32, (size, size), 0)
-    old = lax.broadcasted_iota(jnp.int32, (size, size), 1)
-    move = jnp.where((new % aux) * group + new // aux == old, 1.0, 0.0).astype(x.dtype)
+    size = ((hi - lo) * aux, aux * group)
+    new = lax.broadcasted_iota(jnp.int32, size, 0)
+    old = lax.broadcasted_iota(jnp.int32, size, 1)
+    move = jnp.where((new % aux) * group + new // aux + lo == old, 1.0, 0.0).astype(x.dtype)
     stores = []
     for k in range(PIECES):
         loads[k].wait()
         for g in range(k * each, (k + 1) * each):
-            block = x[:, g * group : (g + 1) * group, :].reshape(size, dom)
+            block = x[:, g * group : (g + 1) * group, :].reshape(aux * group, dom)
             moved = jnp.dot(move, block, preferred_element_type=jnp.float32)
-            moved = moved.astype(x.dtype).reshape(group, aux, dom)
-            for (lo, hi), out in zip(SPLITS, outs):
-                out[g] = moved[lo:hi]
-        for c in range(n):
-            store = pltpu.make_async_copy(
-                outs[c].at[k * each : (k + 1) * each],
-                out_refs[c].at[k * each : (k + 1) * each],
-                out_sems.at[c, k],
-            )
-            store.start()
-            stores.append(store)
+            out[g] = moved.astype(x.dtype).reshape(hi - lo, aux, dom)
+        store = pltpu.make_async_copy(
+            out.at[k * each : (k + 1) * each],
+            out_ref.at[k * each : (k + 1) * each],
+            out_sems.at[k],
+        )
+        store.start()
+        stores.append(store)
     for c in stores:
         c.wait()
 
 
-def arrange(integrals, orbs):
+def arrange(integrals, orbs, lo, hi):
     aux, occ, dom = integrals.shape
-    size = aux * (occ // orbs)
-    shapes = [(orbs, hi - lo, aux, dom) for lo, hi in SPLITS]
+    shape = (orbs, hi - lo, aux, dom)
     return pl.pallas_call(
-        arrange_kernel,
+        functools.partial(arrange_kernel, lo, hi),
         in_specs=[pl.BlockSpec(memory_space=pl.ANY)],
-        out_specs=[pl.BlockSpec(memory_space=pl.ANY)] * len(shapes),
-        out_shape=[jax.ShapeDtypeStruct(v, integrals.dtype) for v in shapes],
-        scratch_shapes=[pltpu.VMEM(integrals.shape, integrals.dtype)]
-        + [pltpu.VMEM(v, integrals.dtype) for v in shapes]
-        + [
+        out_specs=pl.BlockSpec(memory_space=pl.ANY),
+        out_shape=jax.ShapeDtypeStruct(shape, integrals.dtype),
+        scratch_shapes=[
+            pltpu.VMEM(integrals.shape, integrals.dtype),
+            pltpu.VMEM(shape, integrals.dtype),
             pltpu.SemaphoreType.DMA((PIECES,)),
-            pltpu.SemaphoreType.DMA((len(shapes), PIECES)),
+            pltpu.SemaphoreType.DMA((PIECES,)),
         ],
         compiler_params=pltpu.CompilerParams(vmem_limit_bytes=WIDE),
         cost_estimate=pl.CostEstimate(
-            flops=2 * orbs * size * size * dom,
-            bytes_accessed=4 * aux * occ * dom,
+            flops=2 * orbs * (hi - lo) * aux * aux * (occ // orbs) * dom,
+            bytes_accessed=2 * aux * occ * dom,
             transcendentals=0,
         ),
     )(integrals)
@@ -118,25 +113,97 @@
     return mantissa.astype(jnp.float32) * jnp.exp2(power.astype(jnp.float32))
 
 
-def encode(total, out_ref, q):
-    dom = total.shape[0]
-    top = jnp.maximum(jnp.max(jnp.abs(total), axis=0, keepdims=True), 1e-30)
-    power = jnp.floor(jnp.log2(top)).astype(jnp.int32) - 13
-    mantissa = (top * jnp.exp2(-power.astype(jnp.float32))).astype(jnp.int32) + 1
-    scale = STEPS / column_tops(mantissa, power)
-    out_ref[q, :dom, :] = jnp.round(total * scale).astype(jnp.int32).astype(jnp.int16)
-    rows = lax.broadcasted_iota(jnp.int32, (TAIL, total.shape[1]), 0)
-    out_ref[q, dom:, :] = jnp.where(rows == 0, mantissa, power).astype(jnp.int16)
+def encode(totals, out_ref):
+    dom = out_ref.shape[1]
+    rows = lax.broadcasted_iota(jnp.int32, (TAIL, dom), 0)
+    sizes = jnp.zeros((TAIL, dom), jnp.int32)
+    for q, total in enumerate(totals):
+        top = jnp.maximum(jnp.max(jnp.abs(total), axis=0, keepdims=True), 1e-30)
+        power = jnp.floor(jnp.log2(top)).astype(jnp.int32) - 13
+        mantissa = (top * jnp.exp2(-power.astype(jnp.float32))).astype(jnp.int32) + 1
+        steps = jnp.round(total * (STEPS / column_tops(mantissa, power)))
+        out_ref[q * dom : (q + 1) * dom, :] = steps.astype(jnp.int32).astype(jnp.int16)
+        sizes = jnp.where(rows == 2 * q, mantissa, sizes)
+        sizes = jnp.where(rows == 2 * q + 1, power, sizes)
+    out_ref[len(totals) * dom :, :] = sizes.astype(jnp.int16)
 
 
 def decode(code_ref, q):
-    dom = code_ref.shape[-1]
-    tail = code_ref[q, dom:, :].astype(jnp.int32)
-    step = column_tops(tail[0:1], tail[1:2]) * (1.0 / STEPS)
-    return code_ref[q, :dom, :].astype(jnp.float32) * step
-
-
-def sums_kernel(rows, added, coded, pairs_ref, begin_ref, *refs):
+    dom = code_ref.shape[1]
+    rows = lax.broadcasted_iota(jnp.int32, (TAIL, dom), 0)
+    sizes = code_ref[code_ref.shape[0] - TAIL :, :].astype(jnp.int32)
+    mantissa = jnp.sum(jnp.where(rows == 2 * q, sizes, 0), axis=0, keepdims=True)
+    power = jnp.sum(jnp.where(rows == 2 * q + 1, sizes, 0), axis=0, keepdims=True)
+    start = pl.multiple_of(q * dom, dom)
+    steps = code_ref[pl.ds(start, dom), :].astype(jnp.int32).astype(jnp.float32)
+    return steps * (column_tops(mantissa, power) * (1.0 / STEPS))
+
+
+def send_kernel(first, pairs_ref, begin_ref, *refs):
+    parts, base_ref, out_ref, held, base, sems, base_sem = refs[:2], *refs[2:]
+    count = base.shape[0]
+    cut = SPLITS[0][1]
+    whole = pltpu.make_async_copy(base_ref.at[first : first + count], base, base_sem)
+    for q in range(count):
+        row = begin_ref[0] + first + q
+        for side in range(2):
+            k = pairs_ref[2 * row + side]
+
+            @pl.when(k < cut)
+            def _():
+                pltpu.make_async_copy(
+                    parts[0].at[:, k], held.at[q, side], sems.at[q, side]
+                ).start()
+
+            @pl.when(k >= cut)
+            def _():
+                pltpu.make_async_copy(
+                    parts[1].at[:, k - cut], held.at[q, side], sems.at[q, side]
+                ).start()
+
+        if q == 0:
+            whole.start()
+    totals = []
+    for q in range(count):
+        for side in range(2):
+            pltpu.make_async_copy(
+                parts[0].at[:, 0], held.at[q, side], sems.at[q, side]
+            ).wait()
+        if q == 0:
+            whole.wait()
+        left = held[q, 0].reshape(-1, held.shape[-1])
+        right = held[q, 1].reshape(-1, held.shape[-1])
+        term = lax.dot_general(
+            left, right, (((0,), (0,)), ((), ())), preferred_element_type=jnp.float32
+        )
+        totals.append(base[q] + term)
+    encode(totals, out_ref)
+
+
+def send_sums(parts, base, pairs, begin, first, count):
+    src, _, aux, dom = parts[0].shape
+    return pl.pallas_call(
+        functools.partial(send_kernel, first),
+        in_specs=[pl.BlockSpec(memory_space=pltpu.SMEM)] * 2
+        + [pl.BlockSpec(memory_space=pl.ANY)] * 3,
+        out_specs=pl.BlockSpec(memory_space=pltpu.VMEM),
+        out_shape=jax.ShapeDtypeStruct((count * dom + TAIL, dom), jnp.int16),
+        scratch_shapes=[
+            pltpu.VMEM((count, 2, src, aux, dom), jnp.bfloat16),
+            pltpu.VMEM((count, dom, dom), jnp.float32),
+            pltpu.SemaphoreType.DMA((count, 2)),
+            pltpu.SemaphoreType.DMA,
+        ],
+        compiler_params=pltpu.CompilerParams(vmem_limit_bytes=VMEM),
+        cost_estimate=pl.CostEstimate(
+            flops=2 * count * src * aux * dom * dom,
+            bytes_accessed=count * (4 * src * aux * dom + dom * dom * 6),
+            transcendentals=0,
+        ),
+    )(pairs, begin.reshape(1), *parts, base)
+
+
+def sums_kernel(rows, added, pairs_ref, begin_ref, *refs):
     held, sems = refs[-2:]
     count = held.shape[0] * len(SPLITS)
     parts, base_refs = refs[:count], refs[count : count + sum(added)]
@@ -159,13 +226,10 @@
             total = block_sum(held, pairs_ref[2 * row], pairs_ref[2 * row + 1])
             if has:
                 total += next(bases)[q]
-            if coded:
-                encode(total, out_refs[k], q)
-            else:
-                out_refs[k][q] = total
-
-
-def pair_sums(parts, bases, pairs, begins, firsts, count, coded=False, per=PER):
+            out_refs[k][q] = total
+
+
+def pair_sums(parts, bases, pairs, begins, firsts, count, per=PER):
     src, _, aux, dom = parts[0].shape
     orbs = SPLITS[-1][1]
     added = tuple(b is not None for b in bases)
@@ -174,13 +238,9 @@
         for first, has in zip(firsts, added)
         if has
     ]
-    shape = (
-        jax.ShapeDtypeStruct((count, dom + TAIL, dom), jnp.int16)
-        if coded
-        else jax.ShapeDtypeStruct((count, dom, dom), jnp.float32)
-    )
+    shape = jax.ShapeDtypeStruct((count, dom, dom), jnp.float32)
     return pl.pallas_call(
-        functools.partial(sums_kernel, tuple(firsts), added, coded),
+        functools.partial(sums_kernel, tuple(firsts), added),
         grid_spec=pltpu.PrefetchScalarGridSpec(
             num_scalar_prefetch=2,
             grid=(count // per,),
@@ -277,10 +337,12 @@
 
 def finish_kernel(own_ref, other_ref, amp_ref, inv_ref, *refs):
     resid_ref, new_ref = refs[-2:]
-    for q in range(own_ref.shape[0]):
+    per = own_ref.shape[0]
+    p = pl.program_id(0)
+    for q in range(per):
         inv = inv_ref[q]
         inside = inv != 0.0
-        resid = jnp.where(inside, own_ref[q] + decode(other_ref, q), 0.0)
+        resid = jnp.where(inside, own_ref[q] + decode(other_ref, p * per + q), 0.0)
         old = amp_ref[q].astype(jnp.float32)
         resid_ref[q] = resid.astype(resid_ref.dtype)
         new_ref[q] = jnp.where(inside, old - resid * inv, 0.0).astype(new_ref.dtype)
@@ -288,16 +350,17 @@
 
 def finish(own, other, amplitudes, inv, first, held):
     total, dom, _ = amplitudes.shape
-    count = other.shape[0]
-    shifted = pl.BlockSpec((PER, dom, dom), lambda p: (p + first // PER, 0, 0))
+    count = (other.shape[0] - TAIL) // dom
+    per = math.gcd(first, count)
+    shifted = pl.BlockSpec((per, dom, dom), lambda p: (p + first // per, 0, 0))
     shape = jax.ShapeDtypeStruct((total, dom, dom), jnp.bfloat16)
     extra = [] if held is None else list(held)
     return pl.pallas_call(
         finish_kernel,
-        grid=(count // PER,),
+        grid=(count // per,),
         in_specs=[
             shifted,
-            pl.BlockSpec((PER,) + other.shape[1:], lambda p: (p, 0, 0)),
+            pl.BlockSpec(other.shape, lambda p: (0, 0)),
             shifted,
             shifted,
         ]
@@ -335,15 +398,18 @@
         for shift in (1, 2, 3)
     ]
 
-    blocks = arrange(integrals, orbs)
+    blocks = [arrange(integrals, orbs, lo, hi) for lo, hi in SPLITS]
     near, far = [], []
-    for c, block in enumerate(blocks):
+    for c in range(len(SPLITS)):
+        block = blocks[c]
         if c == len(SPLITS) - 1:
             block, *focks = lax.optimization_barrier([block] + focks)
             base, inv = fock_terms(
                 focks, amplitudes, pairs, mine.reshape(1), slot, occ_energy, dom_len
             )
         got = lax.all_to_all(block, "orb", split_axis=0, concat_axis=0, tiled=True)
+        if c == 0:
+            got, blocks[1] = lax.optimization_barrier((got, blocks[1]))
         if c == len(SPLITS) - 1:
             got, base, inv = lax.optimization_barrier((got, base, inv))
         near.append(got)
@@ -352,7 +418,7 @@
     theirs_near, own = pair_sums(near, [None, base], pairs, [theirs, mine], [0, 0], owned)
     others = []
     for lo, hi in CHUNKS:
-        (sums,) = pair_sums(far, [theirs_near], pairs, [theirs], [lo], hi - lo, True)
+        sums = send_sums(far, theirs_near, pairs, theirs, lo, hi - lo)
         others.append(exchange_with(sums, sum_mate, orbs, ys))
     (own,) = pair_sums(far, [own], pairs, [mine], [0], owned)
     held = None

time: 177 us -> 174 us (0.983)
  waiting for transfers between devices: 95.1 us -> 92 us
    all_to_all x2, waiting for transfers between devices: 86.5 us -> 83.3 us  [local(): got = lax.all_to_all(block, 'orb', split_axis=0, concat_axis=0, tiled=True)]
    pallas_call x11 -> x12, Pallas kernels: 34.6 us -> 35.9 us  [the longest x2 12.4 us: pair_sums(): pl.pallas_call(functools.partial(sums_kernel, tuple(firsts), added), grid...]
  transfers between devices with their start and end apart: 11 -> 11, of which waited for: 5 -> 5; matrix products, arithmetic and copies ran while one was open for 0% -> 0% of each run, Pallas kernels for 17% -> 19%
where the time goes in v4:
time: 174 us
  waiting for transfers between devices  92 us (53%)
  Pallas kernels  40.6 us (23%)
  starting transfers between devices  32.6 us (19%)
  local copies, waits for them, and re-layouts  7.99 us (5%)
    all_to_all x2, waiting for transfers between devices, local(): got = lax.all_to_all(block, 'orb', split_axis=0, concat_axis=0, tiled=True)  83.3 us
    all_to_all x2, starting transfers between devices, local(): got = lax.all_to_all(block, 'orb', split_axis=0, concat_axis=0, tiled=True)  18.6 us
    pallas_call x2, Pallas kernels, pair_sums(): pl.pallas_call(functools.partial(sums_kernel, tuple(firsts), added), grid...  12.4 us
    pallas_call x4, Pallas kernels, send_sums(): pl.pallas_call(functools.partial(send_kernel, first), in_specs=[pl.BlockS...  11 us
    ppermute x6, starting transfers between devices, exchange_with(): return lax.ppermute(x, BOTH, pairs)  8.72 us
    ppermute x6, waiting for transfers between devices, exchange_with(): return lax.ppermute(x, BOTH, pairs)  8.72 us
    unnamed x19, local copies, waits for them, and re-layouts  7.85 us
    pallas_call x2, Pallas kernels, arrange(): pl.pallas_call(functools.partial(arrange_kernel, lo, hi), in_specs=[pl.Bl...  6.85 us
  transfers between devices with their start and end apart: 11, of which 5 were waited for; matrix products, arithmetic and copies ran while one was open for 0% of the time, Pallas kernels for 19%

profile of v4, /device:TPU:2, one launch (start us, length us, event | category | flops | bytes accessed | tf_op | source)
XLA Modules:
  0.0 174.0 jit_solution(1207756873108647164)
XLA Ops:
  0.6 3.6 %shard_map.77 = bf16[64,12,8,256]{3,2,1,0:T(8,128)(2,1)} custom-call(bf16[8,1024,256]{2,1,0:T(8,128)(2,1)} %x_ref.3), custom_call_target="tpu_custom_call" | custom-call | flops 402653184 | bytes 4194304 | tf_op jit(solution)/shard_map/pallas_call | solution.py:73
  4.3 12.2 %all-to-all-start = ((bf16[64,12,8,256]{3,2,1,0:T(8,128)(2,1)}), bf16[64,12,8,256]{3,2,1,0:T(8,128)(2,1)}, u32[]{:S(2)}, u32[]{:S(2)}) async-start(bf16[64,12,8,256]{3,2,1,0:T(8,128)(2,1)} %shard_map.77), calls=%async_computation | async-start | bytes 6291456 | tf_op jit(solution)/shard_map/all_to_all | solution.py:410
  16.5 0.0 copy-start.8
  16.5 0.0 copy-start.6
  16.5 0.0 copy-start.7
  16.5 3.3 %collective-permute-start.2 = (bf16[4,256,256]{2,1,0:T(8,128)(2,1)}, bf16[4,256,256]{2,1,0:T(8,128)(2,1)}, u32[]{:S(2)}, u32[]{:S(2)}) collective-permute-start(bf16[4,256,256]{2,1,0:T(8,128)(2,1)} %refs_0_), channel_id=1, source_target_pairs={{2,0},{3,1},{0,2},{1,3},{6,4},{7,5},{4,6},{5,7},{10,8},{11,9},{8,1... | collective-permute-start | bytes 1572872 | tf_op jit(solution)/shard_map/ppermute | solution.py:397
  19.8 1.1 collective-permute-start.1
  20.8 1.0 collective-permute-start.3
  21.8 3.2 %shard_map.78 = bf16[64,4,8,256]{3,2,1,0:T(8,128)(2,1)} custom-call(bf16[8,1024,256]{2,1,0:T(8,128)(2,1)} %x_ref.3), custom_call_target="tpu_custom_call" | custom-call | flops 134217728 | bytes 4194304 | tf_op jit(solution)/shard_map/pallas_call | solution.py:73
  25.0 65.1 %all-to-all-done.refs_0_ = bf16[64,12,8,256]{3,2,1,0:T(8,128)(2,1)} async-done(((bf16[64,12,8,256]{3,2,1,0:T(8,128)(2,1)}), bf16[64,12,8,256]{3,2,1,0:T(8,128)(2,1)}, u32[]{:S(2)}, u32[]{:S(2)}) %all-to-all-start) | async-done | bytes 3145760 | tf_op jit(solution)/shard_map/all_to_all | solution.py:410
  90.1 1.6 collective-permute-start
  91.7 0.0 collective-permute-done.2.refs_2_
  91.7 0.0 collective-permute-done.1.refs_1_
  91.7 0.0 collective-permute-done.3.refs_3_
  91.7 6.4 %all-to-all-start.1 = ((bf16[64,4,8,256]{3,2,1,0:T(8,128)(2,1)}), bf16[64,4,8,256]{3,2,1,0:T(8,128)(2,1)}, u32[]{:S(2)}, u32[]{:S(2)}) async-start(bf16[64,4,8,256]{3,2,1,0:T(8,128)(2,1)} %shard_map.78), calls=%async_computation.1 | async-start | bytes 2097152 | tf_op jit(solution)/shard_map/all_to_all | solution.py:410
  98.1 0.0 copy-done.8
  98.1 0.1 copy.15
  98.2 0.1 reshape.2.pairs_ref
  98.4 0.0 copy-done.6
  98.4 0.0 copy-done.7
  98.4 0.0 copy-start.2
  98.4 1.6 copy-done.2
  100.0 4.7 %shard_map.79 = (f32[16,256,256]{2,1,0:T(8,128)S(1)}, f32[16,256,256]{2,1,0:T(8,128)S(1)}) custom-call(s32[128]{0:T(128)S(1)} %reshape.2.pairs_ref, s32[1]{0:T(128)} %bitcast.begin_ref, s32[16]{0:T(128)S(1)} %fusion.slot_ref, f32[16]{0:T(128)S(1)} %copy-done.6, s32[16]{0:T(128)S(1)} %copy-done.7, bf16[4,256,256]{2,1,0:T(8,128)(2,1)} %refs_0_, ...), custom_call_target="tpu_custom_call" | custom-call | flops 1073741824 | bytes 12582912 | tf_op jit(solution)/shard_map/pallas_call | solution.py:316
  104.7 0.0 copy-start
  104.7 1.9 %copy-done = f32[16,256,256]{2,1,0:T(8,128)} copy-done((f32[16,256,256]{2,1,0:T(8,128)}, f32[16,256,256]{2,1,0:T(8,128)S(1)}, u32[]{:S(2)}) %copy-start) | copy-done | bytes 4194328
  106.6 0.0 copy-start.4
  106.6 2.0 %copy-done.4 = f32[16,256,256]{2,1,0:T(8,128)} copy-done((f32[16,256,256]{2,1,0:T(8,128)}, f32[16,256,256]{2,1,0:T(8,128)S(1)}, u32[]{:S(2)}) %copy-start.4) | copy-done | bytes 4194328
  108.7 18.1 %all-to-all-done.1.refs_1_ = bf16[64,4,8,256]{3,2,1,0:T(8,128)(2,1)} async-done(((bf16[64,4,8,256]{3,2,1,0:T(8,128)(2,1)}), bf16[64,4,8,256]{3,2,1,0:T(8,128)(2,1)}, u32[]{:S(2)}, u32[]{:S(2)}) %all-to-all-start.1) | async-done | bytes 1048608 | tf_op jit(solution)/shard_map/all_to_all | solution.py:410
  126.8 0.1 collective-permute-start.4
  126.9 0.1 pad_add_fusion.begin_ref
  127.0 0.0 copy-start.5
  127.0 2.2 %copy-done.5 = f32[16,256,256]{2,1,0:T(8,128)S(1)} copy-done((f32[16,256,256]{2,1,0:T(8,128)S(1)}, f32[16,256,256]{2,1,0:T(8,128)}, u32[]{:S(2)}) %copy-start.5) | copy-done | bytes 4194328
  129.2 6.6 %shard_map.80 = (f32[16,256,256]{2,1,0:T(8,128)S(1)}, f32[16,256,256]{2,1,0:T(8,128)S(1)}) custom-call(s32[128]{0:T(128)S(1)} %reshape.2.pairs_ref, s32[2]{0:T(128)S(1)} %pad_add_fusion.begin_ref, bf16[64,12,8,256]{3,2,1,0:T(8,128)(2,1)} %all-to-all-done.refs_0_, bf16[64,4,8,256]{3,2,1,0:T(8,128)(2,1)} %all-to-all-done.1.refs_1_, f32[16,256,256]{2,1,0:T(8,128)S(1)} %copy-done.5), custom_call_target="tpu_custom_call" | custom-call | flops 2147483648 | bytes 16777216 | tf_op jit(solution)/shard_map/pallas_call | solution.py:242
  135.9 6.1 %collective-permute-done.4.refs_1_ = bf16[64,4,8,256]{3,2,1,0:T(8,128)(2,1)} collective-permute-done((bf16[64,4,8,256]{3,2,1,0:T(8,128)(2,1)}, bf16[64,4,8,256]{3,2,1,0:T(8,128)(2,1)}, u32[]{:S(2)}, u32[]{:S(2)}) %collective-permute-start.4) | collective-permute-done | bytes 1048608 | tf_op jit(solution)/shard_map/ppermute | solution.py:31
  141.9 0.0 collective-permute-done.refs_0_
  141.9 3.0 %shard_map.83 = s16[1040,256]{1,0:T(8,128)(2,1)S(1)} custom-call(s32[128]{0:T(128)S(1)} %reshape.2.pairs_ref, s32[1]{0:T(128)} %bitcast.1.begin_ref, bf16[64,12,8,256]{3,2,1,0:T(8,128)(2,1)S(1)} %collective-permute-done.refs_0_, bf16[64,4,8,256]{3,2,1,0:T(8,128)(2,1)} %collective-permute-done.4.refs_1_, f32[16,256,256]{2,1,0:T(8,128)S(1)} %get-tuple-element.34.refs_2_), custom_call_target="tpu_custom_call" | custom-call | flops 268435456 | bytes 3670016 | tf_op jit(solution)/shard_map/pallas_call | solution.py:185
  144.9 1.6 collective-permute-start.6
  146.5 3.0 %shard_map.84 = s16[1040,256]{1,0:T(8,128)(2,1)S(1)} custom-call(s32[128]{0:T(128)S(1)} %reshape.2.pairs_ref, s32[1]{0:T(128)} %bitcast.1.begin_ref, bf16[64,12,8,256]{3,2,1,0:T(8,128)(2,1)S(1)} %collective-permute-done.refs_0_, bf16[64,4,8,256]{3,2,1,0:T(8,128)(2,1)} %collective-permute-done.4.refs_1_, f32[16,256,256]{2,1,0:T(8,128)S(1)} %get-tuple-element.34.refs_2_), custom_call_target="tpu_custom_call" | custom-call | flops 268435456 | bytes 3670016 | tf_op jit(solution)/shard_map/pallas_call | solution.py:185
  149.5 1.5 collective-permute-start.7
  150.9 2.6 %shard_map.85 = s16[1040,256]{1,0:T(8,128)(2,1)S(1)} custom-call(s32[128]{0:T(128)S(1)} %reshape.2.pairs_ref, s32[1]{0:T(128)} %bitcast.1.begin_ref, bf16[64,12,8,256]{3,2,1,0:T(8,128)(2,1)S(1)} %collective-permute-done.refs_0_, bf16[64,4,8,256]{3,2,1,0:T(8,128)(2,1)} %collective-permute-done.4.refs_1_, f32[16,256,256]{2,1,0:T(8,128)S(1)} %get-tuple-element.34.refs_2_), custom_call_target="tpu_custom_call" | custom-call | flops 268435456 | bytes 3670016 | tf_op jit(solution)/shard_map/pallas_call | solution.py:185
  153.5 1.9 %collective-permute-start.8 = (s16[1040,256]{1,0:T(8,128)(2,1)S(1)}, s16[1040,256]{1,0:T(8,128)(2,1)S(1)}, u32[]{:S(2)}, u32[]{:S(2)}) collective-permute-start(s16[1040,256]{1,0:T(8,128)(2,1)S(1)} %shard_map.85), channel_id=1, source_target_pairs={{0,3},{1,2},{2,1},{3,0},{4,5},{5,4},{6,7},{7,6},{8,11},{9,10},{10,... | collective-permute-start | bytes 1597448 | tf_op jit(solution)/shard_map/ppermute | solution.py:31
  155.5 2.4 %shard_map.82 = s16[1040,256]{1,0:T(8,128)(2,1)S(1)} custom-call(s32[128]{0:T(128)S(1)} %reshape.2.pairs_ref, s32[1]{0:T(128)} %bitcast.1.begin_ref, bf16[64,12,8,256]{3,2,1,0:T(8,128)(2,1)S(1)} %collective-permute-done.refs_0_, bf16[64,4,8,256]{3,2,1,0:T(8,128)(2,1)} %collective-permute-done.4.refs_1_, f32[16,256,256]{2,1,0:T(8,128)S(1)} %get-tuple-element.34.refs_2_), custom_call_target="tpu_custom_call" | custom-call | flops 268435456 | bytes 3670016 | tf_op jit(solution)/shard_map/pallas_call | solution.py:185
  157.9 2.0 %collective-permute-start.5 = (s16[1040,256]{1,0:T(8,128)(2,1)S(1)}, s16[1040,256]{1,0:T(8,128)(2,1)S(1)}, u32[]{:S(2)}, u32[]{:S(2)}) collective-permute-start(s16[1040,256]{1,0:T(8,128)(2,1)S(1)} %shard_map.82), channel_id=1, source_target_pairs={{0,3},{1,2},{2,1},{3,0},{4,5},{5,4},{6,7},{7,6},{8,11},{9,10},{10,... | collective-permute-start | bytes 1597448 | tf_op jit(solution)/shard_map/ppermute | solution.py:31
  159.9 0.0 copy-start.1
  159.9 0.0 copy-start.3
  159.9 5.7 %shard_map.81.own_ref = f32[16,256,256]{2,1,0:T(8,128)S(1)} custom-call(s32[128]{0:T(128)S(1)} %reshape.2.pairs_ref, s32[1]{0:T(128)} %bitcast.begin_ref, bf16[64,12,8,256]{3,2,1,0:T(8,128)(2,1)S(1)} %collective-permute-done.refs_0_, bf16[64,4,8,256]{3,2,1,0:T(8,128)(2,1)} %collective-permute-done.4.refs_1_, f32[16,256,256]{2,1,0:T(8,128)S(1)} %get-tuple-element.33.refs_2_), custom_call_target="tpu_custom_call" | custom-call | flops 1073741824 | bytes 12582912 | tf_op jit(solution)/shard_map/pallas_call | solution.py:242
  165.7 1.2 collective-permute-done.8.other_ref
  166.9 0.0 copy-done.1
  166.9 0.0 copy-done.3
  166.9 1.4 shard_map.86
  168.3 0.0 collective-permute-done.7.other_ref
  168.3 1.4 shard_map.87
  169.7 0.0 collective-permute-done.6.other_ref
  169.7 1.4 shard_map.88
  171.2 1.4 collective-permute-done.5.other_ref
  172.6 1.4 shard_map.89
  (1 shorter events, 0.0 us)
Async XLA Ops:
  4.3 85.9 %all-to-all-start = ((bf16[64,12,8,256]{3,2,1,0:T(8,128)(2,1)}), bf16[64,12,8,256]{3,2,1,0:T(8,128)(2,1)}, u32[]{:S(2)}, u32[]{:S(2)}) async-start(bf16[64,12,8,256]{3,2,1,0:T(8,128)(2,1)} %shard_map.77), calls=%async_computation | async-start | bytes 6291456 | tf_op jit(solution)/shard_map/all_to_all | solution.py:410
  16.5 81.6 %copy-start.8 = (s32[64,2]{0,1:T(2,128)S(1)}, s32[64,2]{0,1:T(2,128)}, u32[]{:S(2)}) copy-start(s32[64,2]{0,1:T(2,128)} %param.11) | copy-start | bytes 1540
  16.5 81.9 %copy-start.6 = (f32[16]{0:T(128)S(1)}, f32[16]{0:T(128)}, u32[]{:S(2)}) copy-start(f32[16]{0:T(128)} %occ_ref.1) | copy-start | bytes 196
  16.5 81.9 %copy-start.7 = (s32[16]{0:T(128)S(1)}, s32[16]{0:T(128)}, u32[]{:S(2)}) copy-start(s32[16]{0:T(128)} %len_ref.1) | copy-start | bytes 196
  16.5 75.2 %collective-permute-start.2 = (bf16[4,256,256]{2,1,0:T(8,128)(2,1)}, bf16[4,256,256]{2,1,0:T(8,128)(2,1)}, u32[]{:S(2)}, u32[]{:S(2)}) collective-permute-start(bf16[4,256,256]{2,1,0:T(8,128)(2,1)} %refs_0_), channel_id=1, source_target_pairs={{2,0},{3,1},{0,2},{1,3},{6,4},{7,5},{4,6},{5,7},{10,8},{11,9},{8,1... | collective-permute-start | bytes 1572872 | tf_op jit(solution)/shard_map/ppermute | solution.py:397
  19.8 71.9 %collective-permute-start.1 = (bf16[4,256,256]{2,1,0:T(8,128)(2,1)}, bf16[4,256,256]{2,1,0:T(8,128)(2,1)}, u32[]{:S(2)}, u32[]{:S(2)}) collective-permute-start(bf16[4,256,256]{2,1,0:T(8,128)(2,1)} %refs_0_), channel_id=1, source_target_pairs={{1,0},{2,1},{3,2},{0,3},{5,4},{6,5},{7,6},{4,7},{9,8},{10,9},{11,1... | collective-permute-start | bytes 1572872 | tf_op jit(solution)/shard_map/ppermute | solution.py:397
  20.8 70.9 %collective-permute-start.3 = (bf16[4,256,256]{2,1,0:T(8,128)(2,1)}, bf16[4,256,256]{2,1,0:T(8,128)(2,1)}, u32[]{:S(2)}, u32[]{:S(2)}) collective-permute-start(bf16[4,256,256]{2,1,0:T(8,128)(2,1)} %refs_0_), channel_id=1, source_target_pairs={{3,0},{0,1},{1,2},{2,3},{7,4},{4,5},{5,6},{6,7},{11,8},{8,9},{9,10... | collective-permute-start | bytes 1572872 | tf_op jit(solution)/shard_map/ppermute | solution.py:397
  90.1 51.8 %collective-permute-start = (bf16[64,12,8,256]{3,2,1,0:T(8,128)(2,1)}, bf16[64,12,8,256]{3,2,1,0:T(8,128)(2,1)S(1)}, u32[]{:S(2)}, u32[]{:S(2)}) collective-permute-start(bf16[64,12,8,256]{3,2,1,0:T(8,128)(2,1)} %all-to-all-done.refs_0_), channel_id=1, source_target_pairs={{0,1},{1,0},{2,3},{3,2},{4,7},{5,6},{6,5},{7,4},{8,9},{9,8},{10,11... | collective-permute-start | bytes 9437192 | tf_op jit(solution)/shard_map/ppermute | solution.py:31
  91.7 35.1 %all-to-all-start.1 = ((bf16[64,4,8,256]{3,2,1,0:T(8,128)(2,1)}), bf16[64,4,8,256]{3,2,1,0:T(8,128)(2,1)}, u32[]{:S(2)}, u32[]{:S(2)}) async-start(bf16[64,4,8,256]{3,2,1,0:T(8,128)(2,1)} %shard_map.78), calls=%async_computation.1 | async-start | bytes 2097152 | tf_op jit(solution)/shard_map/all_to_all | solution.py:410
  98.4 1.6 copy-start.2
  104.7 1.9 %copy-start = (f32[16,256,256]{2,1,0:T(8,128)}, f32[16,256,256]{2,1,0:T(8,128)S(1)}, u32[]{:S(2)}) copy-start(f32[16,256,256]{2,1,0:T(8,128)S(1)} %get-tuple-element.35.inv_ref) | copy-start | bytes 12582916
  106.6 2.0 %copy-start.4 = (f32[16,256,256]{2,1,0:T(8,128)}, f32[16,256,256]{2,1,0:T(8,128)S(1)}, u32[]{:S(2)}) copy-start(f32[16,256,256]{2,1,0:T(8,128)S(1)} %get-tuple-element.32.refs_2_) | copy-start | bytes 12582916
  126.8 15.1 %collective-permute-start.4 = (bf16[64,4,8,256]{3,2,1,0:T(8,128)(2,1)}, bf16[64,4,8,256]{3,2,1,0:T(8,128)(2,1)}, u32[]{:S(2)}, u32[]{:S(2)}) collective-permute-start(bf16[64,4,8,256]{3,2,1,0:T(8,128)(2,1)} %all-to-all-done.1.refs_1_), channel_id=1, source_target_pairs={{0,1},{1,0},{2,3},{3,2},{4,7},{5,6},{6,5},{7,4},{8,9},{9,8},{10,11... | collective-permute-start | bytes 3145736 | tf_op jit(solution)/shard_map/ppermute | solution.py:31
  127.0 2.2 %copy-start.5 = (f32[16,256,256]{2,1,0:T(8,128)S(1)}, f32[16,256,256]{2,1,0:T(8,128)}, u32[]{:S(2)}) copy-start(f32[16,256,256]{2,1,0:T(8,128)} %copy-done.4) | copy-start | bytes 12582916
  144.9 24.8 %collective-permute-start.6 = (s16[1040,256]{1,0:T(8,128)(2,1)S(1)}, s16[1040,256]{1,0:T(8,128)(2,1)S(1)}, u32[]{:S(2)}, u32[]{:S(2)}) collective-permute-start(s16[1040,256]{1,0:T(8,128)(2,1)S(1)} %shard_map.83), channel_id=1, source_target_pairs={{0,3},{1,2},{2,1},{3,0},{4,5},{5,4},{6,7},{7,6},{8,11},{9,10},{10,... | collective-permute-start | bytes 1597448 | tf_op jit(solution)/shard_map/ppermute | solution.py:31
  149.5 18.8 %collective-permute-start.7 = (s16[1040,256]{1,0:T(8,128)(2,1)S(1)}, s16[1040,256]{1,0:T(8,128)(2,1)S(1)}, u32[]{:S(2)}, u32[]{:S(2)}) collective-permute-start(s16[1040,256]{1,0:T(8,128)(2,1)S(1)} %shard_map.84), channel_id=1, source_target_pairs={{0,3},{1,2},{2,1},{3,0},{4,5},{5,4},{6,7},{7,6},{8,11},{9,10},{10,... | collective-permute-start | bytes 1597448 | tf_op jit(solution)/shard_map/ppermute | solution.py:31
  153.5 13.3 %collective-permute-start.8 = (s16[1040,256]{1,0:T(8,128)(2,1)S(1)}, s16[1040,256]{1,0:T(8,128)(2,1)S(1)}, u32[]{:S(2)}, u32[]{:S(2)}) collective-permute-start(s16[1040,256]{1,0:T(8,128)(2,1)S(1)} %shard_map.85), channel_id=1, source_target_pairs={{0,3},{1,2},{2,1},{3,0},{4,5},{5,4},{6,7},{7,6},{8,11},{9,10},{10,... | collective-permute-start | bytes 1597448 | tf_op jit(solution)/shard_map/ppermute | solution.py:31
  157.9 14.7 %collective-permute-start.5 = (s16[1040,256]{1,0:T(8,128)(2,1)S(1)}, s16[1040,256]{1,0:T(8,128)(2,1)S(1)}, u32[]{:S(2)}, u32[]{:S(2)}) collective-permute-start(s16[1040,256]{1,0:T(8,128)(2,1)S(1)} %shard_map.82), channel_id=1, source_target_pairs={{0,3},{1,2},{2,1},{3,0},{4,5},{5,4},{6,7},{7,6},{8,11},{9,10},{10,... | collective-permute-start | bytes 1597448 | tf_op jit(solution)/shard_map/ppermute | solution.py:31
  159.9 7.0 %copy-start.1 = (f32[16,256,256]{2,1,0:T(8,128)S(1)}, f32[16,256,256]{2,1,0:T(8,128)}, u32[]{:S(2)}) copy-start(f32[16,256,256]{2,1,0:T(8,128)} %copy-done) | copy-start | bytes 12582916
  159.9 7.0 %copy-start.3 = (bf16[16,256,256]{2,1,0:T(8,128)(2,1)S(1)}, bf16[16,256,256]{2,1,0:T(8,128)(2,1)}, u32[]{:S(2)}) copy-start(bf16[16,256,256]{2,1,0:T(8,128)(2,1)} %amp_ref.7) | copy-start | bytes 6291460

commit v5 on v4

--- a/solution.py
+++ b/solution.py
@@ -351,7 +351,7 @@
 def finish(own, other, amplitudes, inv, first, held):
     total, dom, _ = amplitudes.shape
     count = (other.shape[0] - TAIL) // dom
-    per = math.gcd(first, count)
+    per = min(math.gcd(first, count), 2)
     shifted = pl.BlockSpec((per, dom, dom), lambda p: (p + first // per, 0, 0))
     shape = jax.ShapeDtypeStruct((total, dom, dom), jnp.bfloat16)
     extra = [] if held is None else list(held)

time: 174 us -> 174 us (level)
  no operation moved by 1% of the time
where the time goes in v5:
time: 174 us
  waiting for transfers between devices  92.6 us (53%)
  Pallas kernels  40.5 us (23%)
  starting transfers between devices  31.9 us (18%)
  local copies, waits for them, and re-layouts  7.99 us (5%)
    all_to_all x2, waiting for transfers between devices, local(): got = lax.all_to_all(block, 'orb', split_axis=0, concat_axis=0, tiled=True)  83.3 us
    all_to_all x2, starting transfers between devices, local(): got = lax.all_to_all(block, 'orb', split_axis=0, concat_axis=0, tiled=True)  18.6 us
    pallas_call x2, Pallas kernels, pair_sums(): pl.pallas_call(functools.partial(sums_kernel, tuple(firsts), added), grid...  12.4 us
    pallas_call x4, Pallas kernels, send_sums(): pl.pallas_call(functools.partial(send_kernel, first), in_specs=[pl.BlockS...  11.4 us
    ppermute x6, waiting for transfers between devices, exchange_with(): return lax.ppermute(x, BOTH, pairs)  9.29 us
    ppermute x6, starting transfers between devices, exchange_with(): return lax.ppermute(x, BOTH, pairs)  8.07 us
    unnamed x19, local copies, waits for them, and re-layouts  7.85 us
    pallas_call x2, Pallas kernels, arrange(): pl.pallas_call(functools.partial(arrange_kernel, lo, hi), in_specs=[pl.Bl...  6.85 us
  transfers between devices with their start and end apart: 11, of which 5 were waited for; matrix products, arithmetic and copies ran while one was open for 0% of the time, Pallas kernels for 19%

profile of v5, /device:TPU:2, one launch (start us, length us, event | category | flops | bytes accessed | tf_op | source)
XLA Modules:
  0.0 173.9 jit_solution(5746284499086378949)
XLA Ops:
  0.6 3.6 %shard_map.77 = bf16[64,12,8,256]{3,2,1,0:T(8,128)(2,1)} custom-call(bf16[8,1024,256]{2,1,0:T(8,128)(2,1)} %x_ref.3), custom_call_target="tpu_custom_call" | custom-call | flops 402653184 | bytes 4194304 | tf_op jit(solution)/shard_map/pallas_call | solution.py:73
  4.3 12.2 %all-to-all-start = ((bf16[64,12,8,256]{3,2,1,0:T(8,128)(2,1)}), bf16[64,12,8,256]{3,2,1,0:T(8,128)(2,1)}, u32[]{:S(2)}, u32[]{:S(2)}) async-start(bf16[64,12,8,256]{3,2,1,0:T(8,128)(2,1)} %shard_map.77), calls=%async_computation | async-start | bytes 6291456 | tf_op jit(solution)/shard_map/all_to_all | solution.py:410
  16.5 0.0 copy-start.8
  16.5 0.0 copy-start.6
  16.5 0.0 copy-start.7
  16.5 3.3 %collective-permute-start.2 = (bf16[4,256,256]{2,1,0:T(8,128)(2,1)}, bf16[4,256,256]{2,1,0:T(8,128)(2,1)}, u32[]{:S(2)}, u32[]{:S(2)}) collective-permute-start(bf16[4,256,256]{2,1,0:T(8,128)(2,1)} %refs_0_), channel_id=1, source_target_pairs={{2,0},{3,1},{0,2},{1,3},{6,4},{7,5},{4,6},{5,7},{10,8},{11,9},{8,1... | collective-permute-start | bytes 1572872 | tf_op jit(solution)/shard_map/ppermute | solution.py:397
  19.8 1.1 collective-permute-start.1
  20.8 1.0 collective-permute-start.3
  21.8 3.2 %shard_map.78 = bf16[64,4,8,256]{3,2,1,0:T(8,128)(2,1)} custom-call(bf16[8,1024,256]{2,1,0:T(8,128)(2,1)} %x_ref.3), custom_call_target="tpu_custom_call" | custom-call | flops 134217728 | bytes 4194304 | tf_op jit(solution)/shard_map/pallas_call | solution.py:73
  25.0 65.1 %all-to-all-done.refs_0_ = bf16[64,12,8,256]{3,2,1,0:T(8,128)(2,1)} async-done(((bf16[64,12,8,256]{3,2,1,0:T(8,128)(2,1)}), bf16[64,12,8,256]{3,2,1,0:T(8,128)(2,1)}, u32[]{:S(2)}, u32[]{:S(2)}) %all-to-all-start) | async-done | bytes 3145760 | tf_op jit(solution)/shard_map/all_to_all | solution.py:410
  90.1 1.6 collective-permute-start
  91.7 0.0 collective-permute-done.2.refs_2_
  91.7 0.0 collective-permute-done.1.refs_1_
  91.7 0.0 collective-permute-done.3.refs_3_
  91.7 6.4 %all-to-all-start.1 = ((bf16[64,4,8,256]{3,2,1,0:T(8,128)(2,1)}), bf16[64,4,8,256]{3,2,1,0:T(8,128)(2,1)}, u32[]{:S(2)}, u32[]{:S(2)}) async-start(bf16[64,4,8,256]{3,2,1,0:T(8,128)(2,1)} %shard_map.78), calls=%async_computation.1 | async-start | bytes 2097152 | tf_op jit(solution)/shard_map/all_to_all | solution.py:410
  98.1 0.0 copy-done.8
  98.1 0.1 copy.15
  98.2 0.1 reshape.2.pairs_ref
  98.4 0.0 copy-done.6
  98.4 0.0 copy-done.7
  98.4 0.0 copy-start.2
  98.4 1.6 copy-done.2
  100.0 4.7 %shard_map.79 = (f32[16,256,256]{2,1,0:T(8,128)S(1)}, f32[16,256,256]{2,1,0:T(8,128)S(1)}) custom-call(s32[128]{0:T(128)S(1)} %reshape.2.pairs_ref, s32[1]{0:T(128)} %bitcast.begin_ref, s32[16]{0:T(128)S(1)} %fusion.slot_ref, f32[16]{0:T(128)S(1)} %copy-done.6, s32[16]{0:T(128)S(1)} %copy-done.7, bf16[4,256,256]{2,1,0:T(8,128)(2,1)} %refs_0_, ...), custom_call_target="tpu_custom_call" | custom-call | flops 1073741824 | bytes 12582912 | tf_op jit(solution)/shard_map/pallas_call | solution.py:316
  104.7 0.0 copy-start
  104.7 1.9 %copy-done = f32[16,256,256]{2,1,0:T(8,128)} copy-done((f32[16,256,256]{2,1,0:T(8,128)}, f32[16,256,256]{2,1,0:T(8,128)S(1)}, u32[]{:S(2)}) %copy-start) | copy-done | bytes 4194328
  106.6 0.0 copy-start.4
  106.6 2.0 %copy-done.4 = f32[16,256,256]{2,1,0:T(8,128)} copy-done((f32[16,256,256]{2,1,0:T(8,128)}, f32[16,256,256]{2,1,0:T(8,128)S(1)}, u32[]{:S(2)}) %copy-start.4) | copy-done | bytes 4194328
  108.7 18.1 %all-to-all-done.1.refs_1_ = bf16[64,4,8,256]{3,2,1,0:T(8,128)(2,1)} async-done(((bf16[64,4,8,256]{3,2,1,0:T(8,128)(2,1)}), bf16[64,4,8,256]{3,2,1,0:T(8,128)(2,1)}, u32[]{:S(2)}, u32[]{:S(2)}) %all-to-all-start.1) | async-done | bytes 1048608 | tf_op jit(solution)/shard_map/all_to_all | solution.py:410
  126.8 0.1 collective-permute-start.4
  126.9 0.1 pad_add_fusion.begin_ref
  127.0 0.0 copy-start.5
  127.0 2.2 %copy-done.5 = f32[16,256,256]{2,1,0:T(8,128)S(1)} copy-done((f32[16,256,256]{2,1,0:T(8,128)S(1)}, f32[16,256,256]{2,1,0:T(8,128)}, u32[]{:S(2)}) %copy-start.5) | copy-done | bytes 4194328
  129.2 6.6 %shard_map.80 = (f32[16,256,256]{2,1,0:T(8,128)S(1)}, f32[16,256,256]{2,1,0:T(8,128)S(1)}) custom-call(s32[128]{0:T(128)S(1)} %reshape.2.pairs_ref, s32[2]{0:T(128)S(1)} %pad_add_fusion.begin_ref, bf16[64,12,8,256]{3,2,1,0:T(8,128)(2,1)} %all-to-all-done.refs_0_, bf16[64,4,8,256]{3,2,1,0:T(8,128)(2,1)} %all-to-all-done.1.refs_1_, f32[16,256,256]{2,1,0:T(8,128)S(1)} %copy-done.5), custom_call_target="tpu_custom_call" | custom-call | flops 2147483648 | bytes 16777216 | tf_op jit(solution)/shard_map/pallas_call | solution.py:242
  135.9 6.1 %collective-permute-done.4.refs_1_ = bf16[64,4,8,256]{3,2,1,0:T(8,128)(2,1)} collective-permute-done((bf16[64,4,8,256]{3,2,1,0:T(8,128)(2,1)}, bf16[64,4,8,256]{3,2,1,0:T(8,128)(2,1)}, u32[]{:S(2)}, u32[]{:S(2)}) %collective-permute-start.4) | collective-permute-done | bytes 1048608 | tf_op jit(solution)/shard_map/ppermute | solution.py:31
  141.9 0.0 collective-permute-done.refs_0_
  141.9 3.0 %shard_map.83 = s16[1040,256]{1,0:T(8,128)(2,1)S(1)} custom-call(s32[128]{0:T(128)S(1)} %reshape.2.pairs_ref, s32[1]{0:T(128)} %bitcast.1.begin_ref, bf16[64,12,8,256]{3,2,1,0:T(8,128)(2,1)S(1)} %collective-permute-done.refs_0_, bf16[64,4,8,256]{3,2,1,0:T(8,128)(2,1)} %collective-permute-done.4.refs_1_, f32[16,256,256]{2,1,0:T(8,128)S(1)} %get-tuple-element.34.refs_2_), custom_call_target="tpu_custom_call" | custom-call | flops 268435456 | bytes 3670016 | tf_op jit(solution)/shard_map/pallas_call | solution.py:185
  144.9 1.0 collective-permute-start.6
  145.9 3.0 %shard_map.84 = s16[1040,256]{1,0:T(8,128)(2,1)S(1)} custom-call(s32[128]{0:T(128)S(1)} %reshape.2.pairs_ref, s32[1]{0:T(128)} %bitcast.1.begin_ref, bf16[64,12,8,256]{3,2,1,0:T(8,128)(2,1)S(1)} %collective-permute-done.refs_0_, bf16[64,4,8,256]{3,2,1,0:T(8,128)(2,1)} %collective-permute-done.4.refs_1_, f32[16,256,256]{2,1,0:T(8,128)S(1)} %get-tuple-element.34.refs_2_), custom_call_target="tpu_custom_call" | custom-call | flops 268435456 | bytes 3670016 | tf_op jit(solution)/shard_map/pallas_call | solution.py:185
  148.9 2.4 %collective-permute-start.7 = (s16[1040,256]{1,0:T(8,128)(2,1)S(1)}, s16[1040,256]{1,0:T(8,128)(2,1)S(1)}, u32[]{:S(2)}, u32[]{:S(2)}) collective-permute-start(s16[1040,256]{1,0:T(8,128)(2,1)S(1)} %shard_map.84), channel_id=1, source_target_pairs={{0,3},{1,2},{2,1},{3,0},{4,5},{5,4},{6,7},{7,6},{8,11},{9,10},{10,... | collective-permute-start | bytes 1597448 | tf_op jit(solution)/shard_map/ppermute | solution.py:31
  151.3 2.6 %shard_map.85 = s16[1040,256]{1,0:T(8,128)(2,1)S(1)} custom-call(s32[128]{0:T(128)S(1)} %reshape.2.pairs_ref, s32[1]{0:T(128)} %bitcast.1.begin_ref, bf16[64,12,8,256]{3,2,1,0:T(8,128)(2,1)S(1)} %collective-permute-done.refs_0_, bf16[64,4,8,256]{3,2,1,0:T(8,128)(2,1)} %collective-permute-done.4.refs_1_, f32[16,256,256]{2,1,0:T(8,128)S(1)} %get-tuple-element.34.refs_2_), custom_call_target="tpu_custom_call" | custom-call | flops 268435456 | bytes 3670016 | tf_op jit(solution)/shard_map/pallas_call | solution.py:185
  153.9 1.5 collective-permute-start.8
  155.5 2.9 %shard_map.82 = s16[1040,256]{1,0:T(8,128)(2,1)S(1)} custom-call(s32[128]{0:T(128)S(1)} %reshape.2.pairs_ref, s32[1]{0:T(128)} %bitcast.1.begin_ref, bf16[64,12,8,256]{3,2,1,0:T(8,128)(2,1)S(1)} %collective-permute-done.refs_0_, bf16[64,4,8,256]{3,2,1,0:T(8,128)(2,1)} %collective-permute-done.4.refs_1_, f32[16,256,256]{2,1,0:T(8,128)S(1)} %get-tuple-element.34.refs_2_), custom_call_target="tpu_custom_call" | custom-call | flops 268435456 | bytes 3670016 | tf_op jit(solution)/shard_map/pallas_call | solution.py:185
  158.3 1.4 collective-permute-start.5
  159.8 0.0 copy-start.1
  159.8 0.0 copy-start.3
  159.8 5.8 %shard_map.81.own_ref = f32[16,256,256]{2,1,0:T(8,128)S(1)} custom-call(s32[128]{0:T(128)S(1)} %reshape.2.pairs_ref, s32[1]{0:T(128)} %bitcast.begin_ref, bf16[64,12,8,256]{3,2,1,0:T(8,128)(2,1)S(1)} %collective-permute-done.refs_0_, bf16[64,4,8,256]{3,2,1,0:T(8,128)(2,1)} %collective-permute-done.4.refs_1_, f32[16,256,256]{2,1,0:T(8,128)S(1)} %get-tuple-element.33.refs_2_), custom_call_target="tpu_custom_call" | custom-call | flops 1073741824 | bytes 12582912 | tf_op jit(solution)/shard_map/pallas_call | solution.py:242
  165.5 1.4 collective-permute-done.8.other_ref
  166.9 0.0 copy-done.1
  166.9 0.0 copy-done.3
  166.9 1.3 shard_map.86
  168.2 0.0 collective-permute-done.7.other_ref
  168.2 1.3 shard_map.87
  169.5 0.0 collective-permute-done.6.other_ref
  169.5 1.3 shard_map.88
  170.7 1.9 %collective-permute-done.5.other_ref = s16[1040,256]{1,0:T(8,128)(2,1)S(1)} collective-permute-done((s16[1040,256]{1,0:T(8,128)(2,1)S(1)}, s16[1040,256]{1,0:T(8,128)(2,1)S(1)}, u32[]{:S(2)}, u32[]{:S(2)}) %collective-permute-start.5) | collective-permute-done | bytes 532512 | tf_op jit(solution)/shard_map/ppermute | solution.py:31
  172.6 1.3 shard_map.89
  (1 shorter events, 0.0 us)
Async XLA Ops:
  4.3 85.9 %all-to-all-start = ((bf16[64,12,8,256]{3,2,1,0:T(8,128)(2,1)}), bf16[64,12,8,256]{3,2,1,0:T(8,128)(2,1)}, u32[]{:S(2)}, u32[]{:S(2)}) async-start(bf16[64,12,8,256]{3,2,1,0:T(8,128)(2,1)} %shard_map.77), calls=%async_computation | async-start | bytes 6291456 | tf_op jit(solution)/shard_map/all_to_all | solution.py:410
  16.5 81.6 %copy-start.8 = (s32[64,2]{0,1:T(2,128)S(1)}, s32[64,2]{0,1:T(2,128)}, u32[]{:S(2)}) copy-start(s32[64,2]{0,1:T(2,128)} %param.11) | copy-start | bytes 1540
  16.5 81.9 %copy-start.6 = (f32[16]{0:T(128)S(1)}, f32[16]{0:T(128)}, u32[]{:S(2)}) copy-start(f32[16]{0:T(128)} %occ_ref.1) | copy-start | bytes 196
  16.5 81.9 %copy-start.7 = (s32[16]{0:T(128)S(1)}, s32[16]{0:T(128)}, u32[]{:S(2)}) copy-start(s32[16]{0:T(128)} %len_ref.1) | copy-start | bytes 196
  16.5 75.2 %collective-permute-start.2 = (bf16[4,256,256]{2,1,0:T(8,128)(2,1)}, bf16[4,256,256]{2,1,0:T(8,128)(2,1)}, u32[]{:S(2)}, u32[]{:S(2)}) collective-permute-start(bf16[4,256,256]{2,1,0:T(8,128)(2,1)} %refs_0_), channel_id=1, source_target_pairs={{2,0},{3,1},{0,2},{1,3},{6,4},{7,5},{4,6},{5,7},{10,8},{11,9},{8,1... | collective-permute-start | bytes 1572872 | tf_op jit(solution)/shard_map/ppermute | solution.py:397
  19.8 71.9 %collective-permute-start.1 = (bf16[4,256,256]{2,1,0:T(8,128)(2,1)}, bf16[4,256,256]{2,1,0:T(8,128)(2,1)}, u32[]{:S(2)}, u32[]{:S(2)}) collective-permute-start(bf16[4,256,256]{2,1,0:T(8,128)(2,1)} %refs_0_), channel_id=1, source_target_pairs={{1,0},{2,1},{3,2},{0,3},{5,4},{6,5},{7,6},{4,7},{9,8},{10,9},{11,1... | collective-permute-start | bytes 1572872 | tf_op jit(solution)/shard_map/ppermute | solution.py:397
  20.8 70.9 %collective-permute-start.3 = (bf16[4,256,256]{2,1,0:T(8,128)(2,1)}, bf16[4,256,256]{2,1,0:T(8,128)(2,1)}, u32[]{:S(2)}, u32[]{:S(2)}) collective-permute-start(bf16[4,256,256]{2,1,0:T(8,128)(2,1)} %refs_0_), channel_id=1, source_target_pairs={{3,0},{0,1},{1,2},{2,3},{7,4},{4,5},{5,6},{6,7},{11,8},{8,9},{9,10... | collective-permute-start | bytes 1572872 | tf_op jit(solution)/shard_map/ppermute | solution.py:397
  90.1 51.8 %collective-permute-start = (bf16[64,12,8,256]{3,2,1,0:T(8,128)(2,1)}, bf16[64,12,8,256]{3,2,1,0:T(8,128)(2,1)S(1)}, u32[]{:S(2)}, u32[]{:S(2)}) collective-permute-start(bf16[64,12,8,256]{3,2,1,0:T(8,128)(2,1)} %all-to-all-done.refs_0_), channel_id=1, source_target_pairs={{0,1},{1,0},{2,3},{3,2},{4,7},{5,6},{6,5},{7,4},{8,9},{9,8},{10,11... | collective-permute-start | bytes 9437192 | tf_op jit(solution)/shard_map/ppermute | solution.py:31
  91.7 35.1 %all-to-all-start.1 = ((bf16[64,4,8,256]{3,2,1,0:T(8,128)(2,1)}), bf16[64,4,8,256]{3,2,1,0:T(8,128)(2,1)}, u32[]{:S(2)}, u32[]{:S(2)}) async-start(bf16[64,4,8,256]{3,2,1,0:T(8,128)(2,1)} %shard_map.78), calls=%async_computation.1 | async-start | bytes 2097152 | tf_op jit(solution)/shard_map/all_to_all | solution.py:410
  98.4 1.6 copy-start.2
  104.7 1.9 %copy-start = (f32[16,256,256]{2,1,0:T(8,128)}, f32[16,256,256]{2,1,0:T(8,128)S(1)}, u32[]{:S(2)}) copy-start(f32[16,256,256]{2,1,0:T(8,128)S(1)} %get-tuple-element.35.inv_ref) | copy-start | bytes 12582916
  106.6 2.0 %copy-start.4 = (f32[16,256,256]{2,1,0:T(8,128)}, f32[16,256,256]{2,1,0:T(8,128)S(1)}, u32[]{:S(2)}) copy-start(f32[16,256,256]{2,1,0:T(8,128)S(1)} %get-tuple-element.32.refs_2_) | copy-start | bytes 12582916
  126.8 15.1 %collective-permute-start.4 = (bf16[64,4,8,256]{3,2,1,0:T(8,128)(2,1)}, bf16[64,4,8,256]{3,2,1,0:T(8,128)(2,1)}, u32[]{:S(2)}, u32[]{:S(2)}) collective-permute-start(bf16[64,4,8,256]{3,2,1,0:T(8,128)(2,1)} %all-to-all-done.1.refs_1_), channel_id=1, source_target_pairs={{0,1},{1,0},{2,3},{3,2},{4,7},{5,6},{6,5},{7,4},{8,9},{9,8},{10,11... | collective-permute-start | bytes 3145736 | tf_op jit(solution)/shard_map/ppermute | solution.py:31
  127.0 2.2 %copy-start.5 = (f32[16,256,256]{2,1,0:T(8,128)S(1)}, f32[16,256,256]{2,1,0:T(8,128)}, u32[]{:S(2)}) copy-start(f32[16,256,256]{2,1,0:T(8,128)} %copy-done.4) | copy-start | bytes 12582916
  144.9 24.6 %collective-permute-start.6 = (s16[1040,256]{1,0:T(8,128)(2,1)S(1)}, s16[1040,256]{1,0:T(8,128)(2,1)S(1)}, u32[]{:S(2)}, u32[]{:S(2)}) collective-permute-start(s16[1040,256]{1,0:T(8,128)(2,1)S(1)} %shard_map.83), channel_id=1, source_target_pairs={{0,3},{1,2},{2,1},{3,0},{4,5},{5,4},{6,7},{7,6},{8,11},{9,10},{10,... | collective-permute-start | bytes 1597448 | tf_op jit(solution)/shard_map/ppermute | solution.py:31
  148.9 19.3 %collective-permute-start.7 = (s16[1040,256]{1,0:T(8,128)(2,1)S(1)}, s16[1040,256]{1,0:T(8,128)(2,1)S(1)}, u32[]{:S(2)}, u32[]{:S(2)}) collective-permute-start(s16[1040,256]{1,0:T(8,128)(2,1)S(1)} %shard_map.84), channel_id=1, source_target_pairs={{0,3},{1,2},{2,1},{3,0},{4,5},{5,4},{6,7},{7,6},{8,11},{9,10},{10,... | collective-permute-start | bytes 1597448 | tf_op jit(solution)/shard_map/ppermute | solution.py:31
  153.9 12.9 %collective-permute-start.8 = (s16[1040,256]{1,0:T(8,128)(2,1)S(1)}, s16[1040,256]{1,0:T(8,128)(2,1)S(1)}, u32[]{:S(2)}, u32[]{:S(2)}) collective-permute-start(s16[1040,256]{1,0:T(8,128)(2,1)S(1)} %shard_map.85), channel_id=1, source_target_pairs={{0,3},{1,2},{2,1},{3,0},{4,5},{5,4},{6,7},{7,6},{8,11},{9,10},{10,... | collective-permute-start | bytes 1597448 | tf_op jit(solution)/shard_map/ppermute | solution.py:31
  158.3 14.3 %collective-permute-start.5 = (s16[1040,256]{1,0:T(8,128)(2,1)S(1)}, s16[1040,256]{1,0:T(8,128)(2,1)S(1)}, u32[]{:S(2)}, u32[]{:S(2)}) collective-permute-start(s16[1040,256]{1,0:T(8,128)(2,1)S(1)} %shard_map.82), channel_id=1, source_target_pairs={{0,3},{1,2},{2,1},{3,0},{4,5},{5,4},{6,7},{7,6},{8,11},{9,10},{10,... | collective-permute-start | bytes 1597448 | tf_op jit(solution)/shard_map/ppermute | solution.py:31
  159.8 7.1 %copy-start.1 = (f32[16,256,256]{2,1,0:T(8,128)S(1)}, f32[16,256,256]{2,1,0:T(8,128)}, u32[]{:S(2)}) copy-start(f32[16,256,256]{2,1,0:T(8,128)} %copy-done) | copy-start | bytes 12582916
  159.8 7.1 %copy-start.3 = (bf16[16,256,256]{2,1,0:T(8,128)(2,1)S(1)}, bf16[16,256,256]{2,1,0:T(8,128)(2,1)}, u32[]{:S(2)}) copy-start(bf16[16,256,256]{2,1,0:T(8,128)(2,1)} %amp_ref.7) | copy-start | bytes 6291460

commit v6 on v5

--- a/solution.py
+++ b/solution.py
@@ -143,7 +143,10 @@
     parts, base_ref, out_ref, held, base, sems, base_sem = refs[:2], *refs[2:]
     count = base.shape[0]
     cut = SPLITS[0][1]
-    whole = pltpu.make_async_copy(base_ref.at[first : first + count], base, base_sem)
+    bases = [
+        pltpu.make_async_copy(base_ref.at[first + q], base.at[q], base_sem.at[q])
+        for q in range(count)
+    ]
     for q in range(count):
         row = begin_ref[0] + first + q
         for side in range(2):
@@ -161,16 +164,14 @@
                     parts[1].at[:, k - cut], held.at[q, side], sems.at[q, side]
                 ).start()
 
-        if q == 0:
-            whole.start()
+        bases[q].start()
     totals = []
     for q in range(count):
         for side in range(2):
             pltpu.make_async_copy(
                 parts[0].at[:, 0], held.at[q, side], sems.at[q, side]
             ).wait()
-        if q == 0:
-            whole.wait()
+        bases[q].wait()
         left = held[q, 0].reshape(-1, held.shape[-1])
         right = held[q, 1].reshape(-1, held.shape[-1])
         term = lax.dot_general(
@@ -192,7 +193,7 @@
             pltpu.VMEM((count, 2, src, aux, dom), jnp.bfloat16),
             pltpu.VMEM((count, dom, dom), jnp.float32),
             pltpu.SemaphoreType.DMA((count, 2)),
-            pltpu.SemaphoreType.DMA,
+            pltpu.SemaphoreType.DMA((count,)),
         ],
         compiler_params=pltpu.CompilerParams(vmem_limit_bytes=VMEM),
         cost_estimate=pl.CostEstimate(

time: 174 us -> 174 us (level)
  no operation moved by 1% of the time
where the time goes in v6:
time: 174 us
  waiting for transfers between devices  91.8 us (53%)
  Pallas kernels  40.3 us (23%)
  starting transfers between devices  32.9 us (19%)
  local copies, waits for them, and re-layouts  7.99 us (5%)
    all_to_all x2, waiting for transfers between devices, local(): got = lax.all_to_all(block, 'orb', split_axis=0, concat_axis=0, tiled=True)  83.3 us
    all_to_all x2, starting transfers between devices, local(): got = lax.all_to_all(block, 'orb', split_axis=0, concat_axis=0, tiled=True)  18.6 us
    pallas_call x2, Pallas kernels, pair_sums(): pl.pallas_call(functools.partial(sums_kernel, tuple(firsts), added), grid...  12.4 us
    pallas_call x4, Pallas kernels, send_sums(): pl.pallas_call(functools.partial(send_kernel, first), in_specs=[pl.BlockS...  11.2 us
    ppermute x6, starting transfers between devices, exchange_with(): return lax.ppermute(x, BOTH, pairs)  9.08 us
    ppermute x6, waiting for transfers between devices, exchange_with(): return lax.ppermute(x, BOTH, pairs)  8.52 us
    unnamed x19, local copies, waits for them, and re-layouts  7.85 us
    pallas_call x2, Pallas kernels, arrange(): pl.pallas_call(functools.partial(arrange_kernel, lo, hi), in_specs=[pl.Bl...  6.85 us
  transfers between devices with their start and end apart: 11, of which 5 were waited for; matrix products, arithmetic and copies ran while one was open for 0% of the time, Pallas kernels for 19%

profile of v6, /device:TPU:2, one launch (start us, length us, event | category | flops | bytes accessed | tf_op | source)
XLA Modules:
  0.0 173.9 jit_solution(13008277029779074581)
XLA Ops:
  0.6 3.6 %shard_map.77 = bf16[64,12,8,256]{3,2,1,0:T(8,128)(2,1)} custom-call(bf16[8,1024,256]{2,1,0:T(8,128)(2,1)} %x_ref.3), custom_call_target="tpu_custom_call" | custom-call | flops 402653184 | bytes 4194304 | tf_op jit(solution)/shard_map/pallas_call | solution.py:73
  4.3 12.2 %all-to-all-start = ((bf16[64,12,8,256]{3,2,1,0:T(8,128)(2,1)}), bf16[64,12,8,256]{3,2,1,0:T(8,128)(2,1)}, u32[]{:S(2)}, u32[]{:S(2)}) async-start(bf16[64,12,8,256]{3,2,1,0:T(8,128)(2,1)} %shard_map.77), calls=%async_computation | async-start | bytes 6291456 | tf_op jit(solution)/shard_map/all_to_all | solution.py:411
  16.5 0.0 copy-start.8
  16.5 0.0 copy-start.6
  16.5 0.0 copy-start.7
  16.5 3.3 %collective-permute-start.2 = (bf16[4,256,256]{2,1,0:T(8,128)(2,1)}, bf16[4,256,256]{2,1,0:T(8,128)(2,1)}, u32[]{:S(2)}, u32[]{:S(2)}) collective-permute-start(bf16[4,256,256]{2,1,0:T(8,128)(2,1)} %refs_0_), channel_id=1, source_target_pairs={{2,0},{3,1},{0,2},{1,3},{6,4},{7,5},{4,6},{5,7},{10,8},{11,9},{8,1... | collective-permute-start | bytes 1572872 | tf_op jit(solution)/shard_map/ppermute | solution.py:398
  19.8 1.1 collective-permute-start.1
  20.8 1.0 collective-permute-start.3
  21.8 3.2 %shard_map.78 = bf16[64,4,8,256]{3,2,1,0:T(8,128)(2,1)} custom-call(bf16[8,1024,256]{2,1,0:T(8,128)(2,1)} %x_ref.3), custom_call_target="tpu_custom_call" | custom-call | flops 134217728 | bytes 4194304 | tf_op jit(solution)/shard_map/pallas_call | solution.py:73
  25.0 65.1 %all-to-all-done.refs_0_ = bf16[64,12,8,256]{3,2,1,0:T(8,128)(2,1)} async-done(((bf16[64,12,8,256]{3,2,1,0:T(8,128)(2,1)}), bf16[64,12,8,256]{3,2,1,0:T(8,128)(2,1)}, u32[]{:S(2)}, u32[]{:S(2)}) %all-to-all-start) | async-done | bytes 3145760 | tf_op jit(solution)/shard_map/all_to_all | solution.py:411
  90.1 1.6 collective-permute-start
  91.7 0.0 collective-permute-done.2.refs_2_
  91.7 0.0 collective-permute-done.1.refs_1_
  91.7 0.0 collective-permute-done.3.refs_3_
  91.7 6.4 %all-to-all-start.1 = ((bf16[64,4,8,256]{3,2,1,0:T(8,128)(2,1)}), bf16[64,4,8,256]{3,2,1,0:T(8,128)(2,1)}, u32[]{:S(2)}, u32[]{:S(2)}) async-start(bf16[64,4,8,256]{3,2,1,0:T(8,128)(2,1)} %shard_map.78), calls=%async_computation.1 | async-start | bytes 2097152 | tf_op jit(solution)/shard_map/all_to_all | solution.py:411
  98.1 0.0 copy-done.8
  98.1 0.1 copy.15
  98.2 0.1 reshape.2.pairs_ref
  98.4 0.0 copy-done.6
  98.4 0.0 copy-done.7
  98.4 0.0 copy-start.2
  98.4 1.6 copy-done.2
  100.0 4.7 %shard_map.79 = (f32[16,256,256]{2,1,0:T(8,128)S(1)}, f32[16,256,256]{2,1,0:T(8,128)S(1)}) custom-call(s32[128]{0:T(128)S(1)} %reshape.2.pairs_ref, s32[1]{0:T(128)} %bitcast.begin_ref, s32[16]{0:T(128)S(1)} %fusion.slot_ref, f32[16]{0:T(128)S(1)} %copy-done.6, s32[16]{0:T(128)S(1)} %copy-done.7, bf16[4,256,256]{2,1,0:T(8,128)(2,1)} %refs_0_, ...), custom_call_target="tpu_custom_call" | custom-call | flops 1073741824 | bytes 12582912 | tf_op jit(solution)/shard_map/pallas_call | solution.py:317
  104.7 0.0 copy-start
  104.7 1.9 %copy-done = f32[16,256,256]{2,1,0:T(8,128)} copy-done((f32[16,256,256]{2,1,0:T(8,128)}, f32[16,256,256]{2,1,0:T(8,128)S(1)}, u32[]{:S(2)}) %copy-start) | copy-done | bytes 4194328
  106.6 0.0 copy-start.4
  106.6 2.0 %copy-done.4 = f32[16,256,256]{2,1,0:T(8,128)} copy-done((f32[16,256,256]{2,1,0:T(8,128)}, f32[16,256,256]{2,1,0:T(8,128)S(1)}, u32[]{:S(2)}) %copy-start.4) | copy-done | bytes 4194328
  108.7 18.1 %all-to-all-done.1.refs_1_ = bf16[64,4,8,256]{3,2,1,0:T(8,128)(2,1)} async-done(((bf16[64,4,8,256]{3,2,1,0:T(8,128)(2,1)}), bf16[64,4,8,256]{3,2,1,0:T(8,128)(2,1)}, u32[]{:S(2)}, u32[]{:S(2)}) %all-to-all-start.1) | async-done | bytes 1048608 | tf_op jit(solution)/shard_map/all_to_all | solution.py:411
  126.8 0.1 collective-permute-start.4
  126.9 0.1 pad_add_fusion.begin_ref
  127.0 0.0 copy-start.5
  127.0 2.2 %copy-done.5 = f32[16,256,256]{2,1,0:T(8,128)S(1)} copy-done((f32[16,256,256]{2,1,0:T(8,128)S(1)}, f32[16,256,256]{2,1,0:T(8,128)}, u32[]{:S(2)}) %copy-start.5) | copy-done | bytes 4194328
  129.2 6.6 %shard_map.80 = (f32[16,256,256]{2,1,0:T(8,128)S(1)}, f32[16,256,256]{2,1,0:T(8,128)S(1)}) custom-call(s32[128]{0:T(128)S(1)} %reshape.2.pairs_ref, s32[2]{0:T(128)S(1)} %pad_add_fusion.begin_ref, bf16[64,12,8,256]{3,2,1,0:T(8,128)(2,1)} %all-to-all-done.refs_0_, bf16[64,4,8,256]{3,2,1,0:T(8,128)(2,1)} %all-to-all-done.1.refs_1_, f32[16,256,256]{2,1,0:T(8,128)S(1)} %copy-done.5), custom_call_target="tpu_custom_call" | custom-call | flops 2147483648 | bytes 16777216 | tf_op jit(solution)/shard_map/pallas_call | solution.py:243
  135.9 6.1 %collective-permute-done.4.refs_1_ = bf16[64,4,8,256]{3,2,1,0:T(8,128)(2,1)} collective-permute-done((bf16[64,4,8,256]{3,2,1,0:T(8,128)(2,1)}, bf16[64,4,8,256]{3,2,1,0:T(8,128)(2,1)}, u32[]{:S(2)}, u32[]{:S(2)}) %collective-permute-start.4) | collective-permute-done | bytes 1048608 | tf_op jit(solution)/shard_map/ppermute | solution.py:31
  141.9 0.0 collective-permute-done.refs_0_
  141.9 3.0 %shard_map.83 = s16[1040,256]{1,0:T(8,128)(2,1)S(1)} custom-call(s32[128]{0:T(128)S(1)} %reshape.2.pairs_ref, s32[1]{0:T(128)} %bitcast.1.begin_ref, bf16[64,12,8,256]{3,2,1,0:T(8,128)(2,1)S(1)} %collective-permute-done.refs_0_, bf16[64,4,8,256]{3,2,1,0:T(8,128)(2,1)} %collective-permute-done.4.refs_1_, f32[16,256,256]{2,1,0:T(8,128)S(1)} %get-tuple-element.34.refs_2_), custom_call_target="tpu_custom_call" | custom-call | flops 268435456 | bytes 3670016 | tf_op jit(solution)/shard_map/pallas_call | solution.py:186
  144.9 1.1 collective-permute-start.6
  146.1 2.8 %shard_map.84 = s16[1040,256]{1,0:T(8,128)(2,1)S(1)} custom-call(s32[128]{0:T(128)S(1)} %reshape.2.pairs_ref, s32[1]{0:T(128)} %bitcast.1.begin_ref, bf16[64,12,8,256]{3,2,1,0:T(8,128)(2,1)S(1)} %collective-permute-done.refs_0_, bf16[64,4,8,256]{3,2,1,0:T(8,128)(2,1)} %collective-permute-done.4.refs_1_, f32[16,256,256]{2,1,0:T(8,128)S(1)} %get-tuple-element.34.refs_2_), custom_call_target="tpu_custom_call" | custom-call | flops 268435456 | bytes 3670016 | tf_op jit(solution)/shard_map/pallas_call | solution.py:186
  148.9 2.2 %collective-permute-start.7 = (s16[1040,256]{1,0:T(8,128)(2,1)S(1)}, s16[1040,256]{1,0:T(8,128)(2,1)S(1)}, u32[]{:S(2)}, u32[]{:S(2)}) collective-permute-start(s16[1040,256]{1,0:T(8,128)(2,1)S(1)} %shard_map.84), channel_id=1, source_target_pairs={{0,3},{1,2},{2,1},{3,0},{4,5},{5,4},{6,7},{7,6},{8,11},{9,10},{10,... | collective-permute-start | bytes 1597448 | tf_op jit(solution)/shard_map/ppermute | solution.py:31
  151.1 3.0 %shard_map.85 = s16[1040,256]{1,0:T(8,128)(2,1)S(1)} custom-call(s32[128]{0:T(128)S(1)} %reshape.2.pairs_ref, s32[1]{0:T(128)} %bitcast.1.begin_ref, bf16[64,12,8,256]{3,2,1,0:T(8,128)(2,1)S(1)} %collective-permute-done.refs_0_, bf16[64,4,8,256]{3,2,1,0:T(8,128)(2,1)} %collective-permute-done.4.refs_1_, f32[16,256,256]{2,1,0:T(8,128)S(1)} %get-tuple-element.34.refs_2_), custom_call_target="tpu_custom_call" | custom-call | flops 268435456 | bytes 3670016 | tf_op jit(solution)/shard_map/pallas_call | solution.py:186
  154.1 0.8 collective-permute-start.8
  154.9 2.4 %shard_map.82 = s16[1040,256]{1,0:T(8,128)(2,1)S(1)} custom-call(s32[128]{0:T(128)S(1)} %reshape.2.pairs_ref, s32[1]{0:T(128)} %bitcast.1.begin_ref, bf16[64,12,8,256]{3,2,1,0:T(8,128)(2,1)S(1)} %collective-permute-done.refs_0_, bf16[64,4,8,256]{3,2,1,0:T(8,128)(2,1)} %collective-permute-done.4.refs_1_, f32[16,256,256]{2,1,0:T(8,128)S(1)} %get-tuple-element.34.refs_2_), custom_call_target="tpu_custom_call" | custom-call | flops 268435456 | bytes 3670016 | tf_op jit(solution)/shard_map/pallas_call | solution.py:186
  157.4 3.2 %collective-permute-start.5 = (s16[1040,256]{1,0:T(8,128)(2,1)S(1)}, s16[1040,256]{1,0:T(8,128)(2,1)S(1)}, u32[]{:S(2)}, u32[]{:S(2)}) collective-permute-start(s16[1040,256]{1,0:T(8,128)(2,1)S(1)} %shard_map.82), channel_id=1, source_target_pairs={{0,3},{1,2},{2,1},{3,0},{4,5},{5,4},{6,7},{7,6},{8,11},{9,10},{10,... | collective-permute-start | bytes 1597448 | tf_op jit(solution)/shard_map/ppermute | solution.py:31
  160.6 0.0 copy-start.1
  160.6 0.0 copy-start.3
  160.6 5.7 %shard_map.81.own_ref = f32[16,256,256]{2,1,0:T(8,128)S(1)} custom-call(s32[128]{0:T(128)S(1)} %reshape.2.pairs_ref, s32[1]{0:T(128)} %bitcast.begin_ref, bf16[64,12,8,256]{3,2,1,0:T(8,128)(2,1)S(1)} %collective-permute-done.refs_0_, bf16[64,4,8,256]{3,2,1,0:T(8,128)(2,1)} %collective-permute-done.4.refs_1_, f32[16,256,256]{2,1,0:T(8,128)S(1)} %get-tuple-element.33.refs_2_), custom_call_target="tpu_custom_call" | custom-call | flops 1073741824 | bytes 12582912 | tf_op jit(solution)/shard_map/pallas_call | solution.py:243
  166.3 0.6 collective-permute-done.8.other_ref
  166.9 0.0 copy-done.1
  166.9 0.0 copy-done.3
  166.9 1.3 shard_map.86
  168.2 0.0 collective-permute-done.7.other_ref
  168.2 1.3 shard_map.87
  169.5 0.0 collective-permute-done.6.other_ref
  169.5 1.3 shard_map.88
  170.8 1.9 %collective-permute-done.5.other_ref = s16[1040,256]{1,0:T(8,128)(2,1)S(1)} collective-permute-done((s16[1040,256]{1,0:T(8,128)(2,1)S(1)}, s16[1040,256]{1,0:T(8,128)(2,1)S(1)}, u32[]{:S(2)}, u32[]{:S(2)}) %collective-permute-start.5) | collective-permute-done | bytes 532512 | tf_op jit(solution)/shard_map/ppermute | solution.py:31
  172.6 1.3 shard_map.89
  (1 shorter events, 0.0 us)
Async XLA Ops:
  4.3 85.9 %all-to-all-start = ((bf16[64,12,8,256]{3,2,1,0:T(8,128)(2,1)}), bf16[64,12,8,256]{3,2,1,0:T(8,128)(2,1)}, u32[]{:S(2)}, u32[]{:S(2)}) async-start(bf16[64,12,8,256]{3,2,1,0:T(8,128)(2,1)} %shard_map.77), calls=%async_computation | async-start | bytes 6291456 | tf_op jit(solution)/shard_map/all_to_all | solution.py:411
  16.5 81.6 %copy-start.8 = (s32[64,2]{0,1:T(2,128)S(1)}, s32[64,2]{0,1:T(2,128)}, u32[]{:S(2)}) copy-start(s32[64,2]{0,1:T(2,128)} %param.11) | copy-start | bytes 1540
  16.5 81.9 %copy-start.6 = (f32[16]{0:T(128)S(1)}, f32[16]{0:T(128)}, u32[]{:S(2)}) copy-start(f32[16]{0:T(128)} %occ_ref.1) | copy-start | bytes 196
  16.5 81.9 %copy-start.7 = (s32[16]{0:T(128)S(1)}, s32[16]{0:T(128)}, u32[]{:S(2)}) copy-start(s32[16]{0:T(128)} %len_ref.1) | copy-start | bytes 196
  16.5 75.2 %collective-permute-start.2 = (bf16[4,256,256]{2,1,0:T(8,128)(2,1)}, bf16[4,256,256]{2,1,0:T(8,128)(2,1)}, u32[]{:S(2)}, u32[]{:S(2)}) collective-permute-start(bf16[4,256,256]{2,1,0:T(8,128)(2,1)} %refs_0_), channel_id=1, source_target_pairs={{2,0},{3,1},{0,2},{1,3},{6,4},{7,5},{4,6},{5,7},{10,8},{11,9},{8,1... | collective-permute-start | bytes 1572872 | tf_op jit(solution)/shard_map/ppermute | solution.py:398
  19.8 71.9 %collective-permute-start.1 = (bf16[4,256,256]{2,1,0:T(8,128)(2,1)}, bf16[4,256,256]{2,1,0:T(8,128)(2,1)}, u32[]{:S(2)}, u32[]{:S(2)}) collective-permute-start(bf16[4,256,256]{2,1,0:T(8,128)(2,1)} %refs_0_), channel_id=1, source_target_pairs={{1,0},{2,1},{3,2},{0,3},{5,4},{6,5},{7,6},{4,7},{9,8},{10,9},{11,1... | collective-permute-start | bytes 1572872 | tf_op jit(solution)/shard_map/ppermute | solution.py:398
  20.8 70.9 %collective-permute-start.3 = (bf16[4,256,256]{2,1,0:T(8,128)(2,1)}, bf16[4,256,256]{2,1,0:T(8,128)(2,1)}, u32[]{:S(2)}, u32[]{:S(2)}) collective-permute-start(bf16[4,256,256]{2,1,0:T(8,128)(2,1)} %refs_0_), channel_id=1, source_target_pairs={{3,0},{0,1},{1,2},{2,3},{7,4},{4,5},{5,6},{6,7},{11,8},{8,9},{9,10... | collective-permute-start | bytes 1572872 | tf_op jit(solution)/shard_map/ppermute | solution.py:398
  90.1 51.8 %collective-permute-start = (bf16[64,12,8,256]{3,2,1,0:T(8,128)(2,1)}, bf16[64,12,8,256]{3,2,1,0:T(8,128)(2,1)S(1)}, u32[]{:S(2)}, u32[]{:S(2)}) collective-permute-start(bf16[64,12,8,256]{3,2,1,0:T(8,128)(2,1)} %all-to-all-done.refs_0_), channel_id=1, source_target_pairs={{0,1},{1,0},{2,3},{3,2},{4,7},{5,6},{6,5},{7,4},{8,9},{9,8},{10,11... | collective-permute-start | bytes 9437192 | tf_op jit(solution)/shard_map/ppermute | solution.py:31
  91.7 35.1 %all-to-all-start.1 = ((bf16[64,4,8,256]{3,2,1,0:T(8,128)(2,1)}), bf16[64,4,8,256]{3,2,1,0:T(8,128)(2,1)}, u32[]{:S(2)}, u32[]{:S(2)}) async-start(bf16[64,4,8,256]{3,2,1,0:T(8,128)(2,1)} %shard_map.78), calls=%async_computation.1 | async-start | bytes 2097152 | tf_op jit(solution)/shard_map/all_to_all | solution.py:411
  98.4 1.6 copy-start.2
  104.7 1.9 %copy-start = (f32[16,256,256]{2,1,0:T(8,128)}, f32[16,256,256]{2,1,0:T(8,128)S(1)}, u32[]{:S(2)}) copy-start(f32[16,256,256]{2,1,0:T(8,128)S(1)} %get-tuple-element.35.inv_ref) | copy-start | bytes 12582916
  106.6 2.0 %copy-start.4 = (f32[16,256,256]{2,1,0:T(8,128)}, f32[16,256,256]{2,1,0:T(8,128)S(1)}, u32[]{:S(2)}) copy-start(f32[16,256,256]{2,1,0:T(8,128)S(1)} %get-tuple-element.32.refs_2_) | copy-start | bytes 12582916
  126.8 15.1 %collective-permute-start.4 = (bf16[64,4,8,256]{3,2,1,0:T(8,128)(2,1)}, bf16[64,4,8,256]{3,2,1,0:T(8,128)(2,1)}, u32[]{:S(2)}, u32[]{:S(2)}) collective-permute-start(bf16[64,4,8,256]{3,2,1,0:T(8,128)(2,1)} %all-to-all-done.1.refs_1_), channel_id=1, source_target_pairs={{0,1},{1,0},{2,3},{3,2},{4,7},{5,6},{6,5},{7,4},{8,9},{9,8},{10,11... | collective-permute-start | bytes 3145736 | tf_op jit(solution)/shard_map/ppermute | solution.py:31
  127.0 2.2 %copy-start.5 = (f32[16,256,256]{2,1,0:T(8,128)S(1)}, f32[16,256,256]{2,1,0:T(8,128)}, u32[]{:S(2)}) copy-start(f32[16,256,256]{2,1,0:T(8,128)} %copy-done.4) | copy-start | bytes 12582916
  144.9 24.6 %collective-permute-start.6 = (s16[1040,256]{1,0:T(8,128)(2,1)S(1)}, s16[1040,256]{1,0:T(8,128)(2,1)S(1)}, u32[]{:S(2)}, u32[]{:S(2)}) collective-permute-start(s16[1040,256]{1,0:T(8,128)(2,1)S(1)} %shard_map.83), channel_id=1, source_target_pairs={{0,3},{1,2},{2,1},{3,0},{4,5},{5,4},{6,7},{7,6},{8,11},{9,10},{10,... | collective-permute-start | bytes 1597448 | tf_op jit(solution)/shard_map/ppermute | solution.py:31
  148.9 19.3 %collective-permute-start.7 = (s16[1040,256]{1,0:T(8,128)(2,1)S(1)}, s16[1040,256]{1,0:T(8,128)(2,1)S(1)}, u32[]{:S(2)}, u32[]{:S(2)}) collective-permute-start(s16[1040,256]{1,0:T(8,128)(2,1)S(1)} %shard_map.84), channel_id=1, source_target_pairs={{0,3},{1,2},{2,1},{3,0},{4,5},{5,4},{6,7},{7,6},{8,11},{9,10},{10,... | collective-permute-start | bytes 1597448 | tf_op jit(solution)/shard_map/ppermute | solution.py:31
  154.1 12.8 %collective-permute-start.8 = (s16[1040,256]{1,0:T(8,128)(2,1)S(1)}, s16[1040,256]{1,0:T(8,128)(2,1)S(1)}, u32[]{:S(2)}, u32[]{:S(2)}) collective-permute-start(s16[1040,256]{1,0:T(8,128)(2,1)S(1)} %shard_map.85), channel_id=1, source_target_pairs={{0,3},{1,2},{2,1},{3,0},{4,5},{5,4},{6,7},{7,6},{8,11},{9,10},{10,... | collective-permute-start | bytes 1597448 | tf_op jit(solution)/shard_map/ppermute | solution.py:31
  157.4 15.3 %collective-permute-start.5 = (s16[1040,256]{1,0:T(8,128)(2,1)S(1)}, s16[1040,256]{1,0:T(8,128)(2,1)S(1)}, u32[]{:S(2)}, u32[]{:S(2)}) collective-permute-start(s16[1040,256]{1,0:T(8,128)(2,1)S(1)} %shard_map.82), channel_id=1, source_target_pairs={{0,3},{1,2},{2,1},{3,0},{4,5},{5,4},{6,7},{7,6},{8,11},{9,10},{10,... | collective-permute-start | bytes 1597448 | tf_op jit(solution)/shard_map/ppermute | solution.py:31
  160.6 6.4 %copy-start.1 = (f32[16,256,256]{2,1,0:T(8,128)S(1)}, f32[16,256,256]{2,1,0:T(8,128)}, u32[]{:S(2)}) copy-start(f32[16,256,256]{2,1,0:T(8,128)} %copy-done) | copy-start | bytes 12582916
  160.6 6.4 %copy-start.3 = (bf16[16,256,256]{2,1,0:T(8,128)(2,1)S(1)}, bf16[16,256,256]{2,1,0:T(8,128)(2,1)}, u32[]{:S(2)}) copy-start(bf16[16,256,256]{2,1,0:T(8,128)(2,1)} %amp_ref.7) | copy-start | bytes 6291460
